TPU v7x, 128 devices: a whole 4x4x4 slice. The times are simulated.
128 devices in a mesh: rep: 8 (over z, core), tp: 16 (over y, x).
Axes of the slice: x: 4, y: 4, z: 4, core: 2. Of those that a mesh axis runs over, the one named last changes fastest.
Arguments:
- queries: bfloat16 [2048, 64, 128], P(('rep', 'tp')), may hold values from -32 to 32
- cached_key_rows: bfloat16 [2048, 8, 256, 128], P(('rep', 'tp')), may hold values from -32 to 32
- cached_value_rows: bfloat16 [2048, 8, 256, 128], P(('rep', 'tp')), may hold values from -6 to 6
- fresh_key: bfloat16 [2048, 8, 128], P(('rep', 'tp')), may hold values from -6 to 6
- fresh_value: bfloat16 [2048, 8, 128], P(('rep', 'tp')), may hold values from -6 to 6
- lengths: int32 [2048], P(('rep', 'tp')), may hold values from 2 to 256
- adapter_index: int32 [2048, 1], P('rep'), may hold values from 0 to 127; in each aligned block of 256 rows (0 to 255, 256 to 511, ...) at most 4 rows name the same one
- skip_stream: bfloat16 [2048, 8192], P(('rep', 'tp')), may hold values from -2 to 2
- output_weight: bfloat16 [8192, 8192], P('tp'), may hold values from -0.0625 to 0.0625
- adapter_down_weight: bfloat16 [128, 8192, 64], P('rep', 'tp'), may hold values from -0.0625 to 0.0625
- adapter_up_weight: bfloat16 [128, 64, 8192], P('rep', None, 'tp'), may hold values from -0.75 to 0.75
Outputs:
- stream_updated: bfloat16 [2048, 8192], P(('rep', 'tp'))
Inputs may be any that keep to these rules, and one draw needn't show every extreme that they name: `adapter_index`: among the 256 requests of each rep index, at most 4 name one adapter; every adapter is named by some request.
All inputs are finite; a program needn't handle non-finite values.
Results may differ from a plain program's by a relative error of at most 0.01.
Values may be sent and summed in bfloat16 or wider, within the bound.
No kernel may reach another device: no remote copies, remote signals or barrier semaphores. Data moves between devices by JAX's collectives and lax.ppermute only.
A program may use at most 128 MiB of HBM per device.

v0:
```python
import math

import jax
import jax.numpy as jnp
from jax import lax
from jax.sharding import PartitionSpec as P


def attend_local(queries, cached_key_rows, cached_value_rows, fresh_key, fresh_value, lengths):
    count, heads, width = queries.shape
    groups = cached_key_rows.shape[1]
    span = cached_key_rows.shape[2]
    grouped = queries.reshape(count, groups, heads // groups, width)
    factor = 1.0 / math.sqrt(width)
    scores = (
        jnp.einsum("rgqd,rgld->rgql", grouped, cached_key_rows, preferred_element_type=jnp.float32)
        * factor
    )
    own = (
        jnp.einsum("rgqd,rgd->rgq", grouped, fresh_key, preferred_element_type=jnp.float32) * factor
    )
    position = jnp.arange(span, dtype=jnp.int32)
    valid = position[None, None, None, :] < lengths[:, None, None, None]
    masked = jnp.where(valid, scores, -jnp.inf)
    top = jnp.maximum(jnp.max(masked, axis=-1), own)
    expo = jnp.where(valid, jnp.exp(scores - top[..., None]), 0.0)
    expo_own = jnp.exp(own - top)
    total = jnp.sum(expo, axis=-1) + expo_own
    probs = (expo / total[..., None]).astype(jnp.bfloat16)
    probs_own = (expo_own / total).astype(jnp.bfloat16)
    mixed = jnp.einsum(
        "rgql,rgld->rgqd", probs, cached_value_rows, preferred_element_type=jnp.float32
    )
    mixed = (
        mixed
        + probs_own.astype(jnp.float32)[..., None] * fresh_value.astype(jnp.float32)[:, :, None, :]
    )
    return mixed.reshape(count, heads * width).astype(jnp.bfloat16)


def slot_layout(feature_rows, group_index, adapter_count, slot_capacity):
    rows_rep = feature_rows.shape[0]
    slots_all = adapter_count * slot_capacity
    order = jnp.arange(rows_rep, dtype=jnp.int32)
    same = group_index[:, None] == group_index[None, :]
    earlier = order[:, None] > order[None, :]
    rank_in = jnp.sum((same & earlier).astype(jnp.int32), axis=1)
    slot = group_index * slot_capacity + rank_in
    placing = (jnp.arange(slots_all, dtype=jnp.int32)[:, None] == slot[None, :]).astype(
        jnp.bfloat16
    )
    placed = jnp.dot(placing, feature_rows, preferred_element_type=jnp.float32).astype(jnp.bfloat16)
    return (placing, placed)


def via_owners(
    feature_rows, group_index, adapter_down_weight, adapter_up_weight, slot_capacity, repeat_factor
):
    cols = feature_rows.shape[1]
    device_adapters = adapter_down_weight.shape[0]
    placing, placed = slot_layout(
        feature_rows, group_index, device_adapters * repeat_factor, slot_capacity
    )
    outgoing = placed.reshape(repeat_factor, device_adapters, slot_capacity, cols)
    partial_down = jnp.einsum(
        "sacf,afk->sack",
        lax.all_to_all(outgoing, "rep", split_axis=0, concat_axis=0, tiled=True),
        adapter_down_weight,
        preferred_element_type=jnp.float32,
    )
    reduced_rows = lax.psum(partial_down, "tp").astype(jnp.bfloat16)
    returned = jnp.einsum(
        "vmou,muz->vmoz", reduced_rows, adapter_up_weight, preferred_element_type=jnp.float32
    ).astype(jnp.bfloat16)
    back = lax.all_to_all(returned, "rep", split_axis=0, concat_axis=0, tiled=True).reshape(
        placing.shape[0], cols
    )
    lowrank_delta = lax.dot_general(
        placing, back, (((0,), (0,)), ((), ())), preferred_element_type=jnp.float32
    )
    return lowrank_delta.astype(jnp.bfloat16)


def body(
    queries,
    cached_key_rows,
    cached_value_rows,
    fresh_key,
    fresh_value,
    lengths,
    adapter_index,
    skip_stream,
    output_weight,
    adapter_down_weight,
    adapter_up_weight,
):
    mixed_heads = attend_local(
        queries, cached_key_rows, cached_value_rows, fresh_key, fresh_value, lengths
    )
    feature_rows = lax.all_to_all(mixed_heads, "tp", split_axis=1, concat_axis=0, tiled=True)
    rows_rep, cols = feature_rows.shape
    repeat_factor = lax.axis_size("rep")
    group_index = adapter_index[:, 0]
    adapter_count = adapter_down_weight.shape[0] * repeat_factor
    slot_capacity = max(2, 2 * rows_rep // adapter_count)
    lowrank_delta = via_owners(
        feature_rows,
        group_index,
        adapter_down_weight,
        adapter_up_weight,
        slot_capacity,
        repeat_factor,
    )
    summed = lax.psum_scatter(
        jnp.dot(feature_rows, output_weight, preferred_element_type=jnp.float32),
        "tp",
        scatter_dimension=0,
        tiled=True,
    )
    shifted_operand = lax.all_to_all(lowrank_delta, "tp", split_axis=0, concat_axis=1, tiled=True)
    summed = summed + 2.0 * shifted_operand.astype(jnp.float32)
    return (skip_stream.astype(jnp.float32) + summed).astype(jnp.bfloat16)


def solution(mesh):
    return jax.shard_map(
        body,
        mesh=mesh,
        in_specs=(
            P(("rep", "tp"), None, None),
            P(("rep", "tp"), None, None, None),
            P(("rep", "tp"), None, None, None),
            P(("rep", "tp"), None, None),
            P(("rep", "tp"), None, None),
            P(("rep", "tp")),
            P("rep", None),
            P(("rep", "tp"), None),
            P("tp", None),
            P("rep", "tp", None),
            P("rep", None, "tp"),
        ),
        out_specs=P(("rep", "tp"), None),
        check_vma=False,
    )
```

profile of v0, /device:TPU:0, one launch (start us, length us, event | category | flops | bytes accessed | tf_op | source)
XLA Modules:
  0.0 167.8 jit_solution(9463241630156310291)
XLA Ops:
  6.5 0.0 copy-start
  6.5 0.0 reduce-scatter.2.cloned.1.call-start
  6.5 0.9 iota_compare_fusion.4
  7.4 1.7 %fusion.10 = f32[16,8,1,8]{3,2,1,0:T(1,128)S(1)} fusion(bf16[16,64,128]{2,1,0:T(8,128)(2,1)} %param.11, bf16[16,8,128,1]{2,1,0,3:T(8,128)(2,1)} %bitcast.50), kind=kOutput, calls=%fused_computation.22 | convolution fusion | flops 262144 | bytes 299008 | tf_op jit(solution)/shard_map/rgqd,rgd->rgq/dot_general | solution.py:20
  9.1 5.9 %select_reduce_fusion = (f32[16,8,8]{2,1,0:T(8,128)S(1)}, f32[16,8,8,256]{3,2,1,0:T(8,128)S(1)}) fusion(pred[16,256]{1,0:T(8,128)(4,1)S(1)} %iota_compare_fusion.4, bf16[16,8,256,128]{3,2,1,0:T(8,128)(2,1)} %param.12, bf16[16,64,128]{2,1,0:T(8,128)(2,1)} %param.11), kind=kOutput, calls=%fused_computation.12 | convolution fusion | flops 67894272 | bytes 9707520 | tf_op jit(solution)/shard_map/rgqd,rgld->rgql/dot_general | solution.py:16
  15.1 0.4 fusion.4
  15.5 0.0 copy-done.2
  15.6 0.0 copy-done.4
  15.6 1.4 fusion.1
  17.0 0.2 convert_element_type.55
  17.2 0.2 copy.24
  17.3 15.6 %all_to_all.39 = bf16[16,16,512]{2,0,1:T(8,128)(2,1)S(1)} all-to-all(bf16[16,16,512]{2,0,1:T(8,128)(2,1)S(1)} %copy.24), channel_id=1, replica_groups=mesh['rep'=8,'tp'=16] {'tp'}, dimensions={1} | all-to-all | bytes 524288 | tf_op jit(solution)/shard_map/all_to_all | solution.py:100
  32.9 9.0 %fusion.21 = f32[256,8192]{1,0:T(8,128)} fusion(bf16[256,512]{1,0:T(8,128)(2,1)S(1)} %bitcast.42, bf16[512,8192]{1,0:T(8,128)(2,1)} %param.19), kind=kOutput, calls=%fused_computation.40 | convolution fusion | flops 2147483648 | bytes 17039360 | tf_op jit(solution)/shard_map/dot_general | solution.py:115
  41.9 0.0 reduce-scatter.2.cloned.1.call-update
  41.9 0.7 copy-done.3
  42.6 0.2 convert_reduce_fusion
  42.8 0.3 convolution_convert_fusion.1
  43.1 0.1 reshape.56
  43.2 15.5 %all_to_all.40 = bf16[8,16,4,512]{3,2,1,0:T(4,128)(2,1)S(1)} all-to-all(bf16[8,16,4,512]{3,2,1,0:T(4,128)(2,1)S(1)} %reshape.56), channel_id=1, replica_groups=mesh['rep'=8,'tp'=16] {'rep'}, dimensions={0} | all-to-all | bytes 1048576 | tf_op jit(solution)/shard_map/all_to_all | solution.py:67
  58.7 0.0 copy-done.1
  58.7 0.4 convolution_bitcast_fusion
  59.2 74.6 %all-reduce.1 = bf16[8,16,4,64]{3,0,2,1:T(8,128)(2,1)S(1)} all-reduce(f32[8,16,4,64]{3,0,2,1:T(8,128)S(1)} %convolution_bitcast_fusion), channel_id=1, replica_groups=mesh['rep'=8,'tp'=16] {'tp'}, use_global_device_ids=true, to_apply=%region_4.5 | all-reduce | flops 32768 | bytes 196608 | tf_op jit(solution)/shard_map/psum | solution.py:71
  133.7 0.0 copy-done
  133.7 0.3 fusion
  134.0 0.3 copy.26
  134.3 12.8 %all_to_all.41 = bf16[8,16,4,512]{3,2,1,0:T(4,128)(2,1)S(1)} all-to-all(bf16[8,16,4,512]{3,2,1,0:T(4,128)(2,1)S(1)} %copy.26), channel_id=1, replica_groups=mesh['rep'=8,'tp'=16] {'rep'}, dimensions={0} | all-to-all | bytes 1048576 | tf_op jit(solution)/shard_map/all_to_all | solution.py:75
  147.1 0.1 reshape.57
  147.3 0.3 convolution_convert_fusion.2
  147.6 11.3 %all_to_all.42 = bf16[16,16,512]{2,1,0:T(8,128)(2,1)S(1)} all-to-all(bf16[16,16,512]{2,1,0:T(8,128)(2,1)S(1)} %bitcast.47), channel_id=1, replica_groups=mesh['rep'=8,'tp'=16] {'tp'}, dimensions={0} | all-to-all | bytes 524288 | tf_op jit(solution)/shard_map/all_to_all | solution.py:120
  158.9 0.1 multiply_bitcast_fusion
  159.0 0.0 reduce-scatter.2.cloned.1.call-done
  159.1 1.9 %add_convert_fusion = bf16[16,8192]{1,0:T(8,128)(2,1)} fusion(f32[16,8192]{1,0:T(8,128)} %reduce-scatter.2.cloned.1.call-done, f32[16,8192]{1,0:T(8,128)S(1)} %bitcast.44, bf16[16,8192]{1,0:T(8,128)(2,1)} %param.18), kind=kLoop, calls=%fused_computation.15 | loop fusion | flops 524288 | bytes 1572864 | tf_op jit(solution)/shard_map/convert_element_type | solution.py:122
  (9 shorter events, 0.1 us)
Async XLA Ops:
  6.5 127.2 %copy-start = (bf16[16,64,512]{2,1,0:T(8,128)(2,1)S(1)}, bf16[16,64,512]{2,1,0:T(8,128)(2,1)}, u32[]{:S(2)}) copy-start(bf16[16,64,512]{2,1,0:T(8,128)(2,1)} %param.21) | copy-start | bytes 3145732
  6.5 9.0 %copy-start.2 = (bf16[16,8,128]{2,1,0:T(8,128)(2,1)S(1)}, bf16[16,8,128]{2,1,0:T(8,128)(2,1)}, u32[]{:S(2)}) copy-start(bf16[16,8,128]{2,1,0:T(8,128)(2,1)} %param.15) | copy-start | bytes 98308
  6.5 152.5 %reduce-scatter.2.cloned.1.call-start = ((), (), s32[]{:S(2)}) async-start(), calls=%async_computation.5 | async-start | bytes 8912896 | tf_op jit(solution)/shard_map/reduce_scatter | solution.py:114
  6.5 9.0 %copy-start.4 = (bf16[16,8,256,128]{3,2,1,0:T(8,128)(2,1)S(1)}, bf16[16,8,256,128]{3,2,1,0:T(8,128)(2,1)}, u32[]{:S(2)}) copy-start(bf16[16,8,256,128]{3,2,1,0:T(8,128)(2,1)} %param.13) | copy-start | bytes 25165828
  41.9 0.7 copy-start.3
  41.9 16.8 %copy-start.1 = (bf16[16,512,64]{1,2,0:T(8,128)(2,1)S(1)}, bf16[16,512,64]{1,2,0:T(8,128)(2,1)}, u32[]{:S(2)}) copy-start(bf16[16,512,64]{1,2,0:T(8,128)(2,1)} %param.20) | copy-start | bytes 3145732
Sparse Core Ops, SparseCore 0:
  42.0 84.8 reduce-scatter.1
where the time goes:
time: 168 us
  blocking collectives  130 us (77%)
  matrix products  19.4 us (12%)
  between operations  13.6 us (8%)
  other arithmetic  3.47 us (2%)
    psum x1, blocking collectives, via_owners(): reduced_rows = lax.psum(partial_down, 'tp').astype(jnp.bfloat16)  74.6 us
    all_to_all x1, blocking collectives, body(): lax.all_to_all(mixed_heads, 'tp', split_axis=1, concat_axis=0, tiled=True)  15.6 us
    all_to_all x1, blocking collectives, via_owners(): lax.all_to_all(outgoing, 'rep', split_axis=0, concat_axis=0, tiled=True)  15.5 us
    all_to_all x1, blocking collectives, via_owners(): lax.all_to_all(returned, 'rep', split_axis=0, concat_axis=0, tiled=True)  12.8 us
    all_to_all x1, blocking collectives, body(): lax.all_to_all(lowrank_delta, 'tp', split_axis=0, concat_axis=1, tiled=True)  11.3 us
    dot_general x1, matrix products, body(): jnp.dot(feature_rows, output_weight, preferred_element_type=jnp.float32)  8.95 us
    dot_general x1, matrix products, attend_local(): jnp.einsum('rgqd,rgld->rgql', grouped, cached_key_rows, preferred_element...  5.89 us
  transfers between devices with their start and end apart: 1, of which 0 were waited for; matrix products, arithmetic and copies ran while one was open for 1% of the time, Pallas kernels for 0%

commit v1 on v0

v1 whole, which is shorter than its diff:
```python
import math

import jax
import jax.numpy as jnp
import numpy as np
from jax import lax
from jax.experimental import pallas as pl
from jax.experimental.pallas import tpu as pltpu
from jax.sharding import PartitionSpec as P

F32 = jnp.float32
BF16 = jnp.bfloat16
BOTH = ("rep", "tp")
SIDE = 4
VMEM_BYTES = 40 * 1024 * 1024


def place(z, c, y, x):
    return ((z * 2 + c) * SIDE + y) * SIDE + x


PLACES = [
    (z, c, y, x) for z in range(SIDE) for c in range(2) for y in range(SIDE) for x in range(SIDE)
]


def pass_plane(value, axis_of_core, offset):
    pairs = []
    for z, c, y, x in PLACES:
        if axis_of_core[c] == "x":
            to = place(z, c, y, (x + offset) % SIDE)
        else:
            to = place(z, c, (y + offset) % SIDE, x)
        pairs.append((place(z, c, y, x), to))
    return lax.ppermute(value, BOTH, pairs)


def pass_z(value, offset):
    pairs = [(place(z, c, y, x), place((z + offset) % SIDE, c, y, x)) for z, c, y, x in PLACES]
    return lax.ppermute(value, BOTH, pairs)


def pass_core(value):
    return lax.ppermute(
        value, BOTH, [(place(z, c, y, x), place(z, 1 - c, y, x)) for z, c, y, x in PLACES]
    )


def row_order():
    table = np.zeros((len(PLACES), SIDE * SIDE), np.int32)
    for z, c, y, x in PLACES:
        for first in range(SIDE):
            for second in range(SIDE):
                dx, dy = (first, second) if c == 0 else (second, first)
                table[place(z, c, y, x), first * SIDE + second] = (
                    (y + dy) % SIDE * SIDE + (x + dx) % SIDE
                )
    return table


PER_STEP = 2


def attend_kernel(
    lengths_ref, q_ref, k_ref, v_ref, fk_ref, fv_ref, o_ref, mixed_ref, *, groups, fold, span
):
    step = pl.program_id(0)
    heads = groups * fold
    width = q_ref.shape[-1]
    factor = 1.0 / math.sqrt(width)
    position = lax.broadcasted_iota(jnp.int32, (heads, span), 1)
    nt = (((1,), (1,)), ((), ()))
    for item in range(PER_STEP):
        row = step * PER_STEP + item
        q = q_ref[item]
        parts = []
        for g in range(groups):
            two = q[(g // 2) * 2 * fold : (g // 2 + 1) * 2 * fold]
            got = lax.dot_general(two, k_ref[item, g], nt, preferred_element_type=F32)
            parts.append(got[(g % 2) * fold : (g % 2 + 1) * fold])
        scores = jnp.concatenate(parts, axis=0) * factor
        fresh_k = jnp.broadcast_to(
            fk_ref[item].astype(F32)[:, None, :], (groups, fold, width)
        ).reshape(heads, width)
        own = jnp.sum(q.astype(F32) * fresh_k, axis=-1, keepdims=True) * factor
        valid = position < lengths_ref[row]
        masked = jnp.where(valid, scores, -jnp.inf)
        top = jnp.maximum(jnp.max(masked, axis=-1, keepdims=True), own)
        expo = jnp.exp(masked - top)
        expo_own = jnp.exp(own - top)
        total = jnp.sum(expo, axis=-1, keepdims=True) + expo_own
        inverse = 1.0 / total
        probs = (expo * inverse).astype(BF16)
        probs_own = (expo_own * inverse).astype(BF16).astype(F32)
        parts = []
        for g in range(groups):
            two = probs[(g // 2) * 2 * fold : (g // 2 + 1) * 2 * fold]
            got = jnp.dot(two, v_ref[item, g], preferred_element_type=F32)
            parts.append(got[(g % 2) * fold : (g % 2 + 1) * fold])
        fresh_v = jnp.broadcast_to(
            fv_ref[item].astype(F32)[:, None, :], (groups, fold, width)
        ).reshape(heads, width)
        mixed = jnp.concatenate(parts, axis=0) + probs_own * fresh_v
        mixed_ref[pl.ds(pl.multiple_of(row * heads, heads), heads), :] = mixed

    @pl.when(step == pl.num_programs(0) - 1)
    def _():
        blocks, rows, cols = o_ref.shape
        per_block = cols // width
        for h in range(heads):
            tile = jnp.concatenate(
                [
                    mixed_ref[pl.ds(half * 8 * heads + h, 8, stride=heads), :]
                    for half in range(rows // 8)
                ],
                axis=0,
            )
            lane = (h % per_block) * width
            o_ref[h // per_block, :, lane : lane + width] = tile.astype(BF16)


def attend(queries, keys, values, fresh_key, fresh_value, lengths, blocks):
    rows, heads, width = queries.shape
    groups, span = keys.shape[1], keys.shape[2]
    body = lambda *refs: attend_kernel(*refs, groups=groups, fold=heads // groups, span=span)
    cols = heads * width // blocks
    return pl.pallas_call(
        body,
        name="attend",
        out_shape=jax.ShapeDtypeStruct((blocks, rows, cols), BF16),
        grid_spec=pltpu.PrefetchScalarGridSpec(
            num_scalar_prefetch=1,
            grid=(rows // PER_STEP,),
            in_specs=[
                pl.BlockSpec((PER_STEP, heads, width), lambda i, _: (i, 0, 0)),
                pl.BlockSpec((PER_STEP, groups, span, width), lambda i, _: (i, 0, 0, 0)),
                pl.BlockSpec((PER_STEP, groups, span, width), lambda i, _: (i, 0, 0, 0)),
                pl.BlockSpec((PER_STEP, groups, width), lambda i, _: (i, 0, 0)),
                pl.BlockSpec((PER_STEP, groups, width), lambda i, _: (i, 0, 0)),
            ],
            out_specs=pl.BlockSpec((blocks, rows, cols), lambda i, _: (0, 0, 0)),
            scratch_shapes=[pltpu.VMEM((rows * heads, width), F32)],
        ),
        compiler_params=pltpu.CompilerParams(vmem_limit_bytes=VMEM_BYTES),
        cost_estimate=pl.CostEstimate(
            flops=4 * rows * heads * span * width,
            bytes_accessed=4 * rows * groups * span * width,
            transcendentals=rows * heads * span,
        ),
    )(lengths, queries, keys, values, fresh_key, fresh_value)


def whole(count):
    return [pl.BlockSpec(memory_space=pltpu.VMEM)] * count


def project_kernel(order_ref, f_ref, w_ref, *refs):
    outs, rows_ref = refs[:SIDE], refs[SIDE]
    block = f_ref.shape[1]

    @pl.when(pl.program_id(0) == 0)
    def _():
        for k in range(SIDE * SIDE):
            rows_ref[k * block : (k + 1) * block, :] = f_ref[order_ref[k]]

    product = jnp.dot(rows_ref[...], w_ref[...], preferred_element_type=F32).astype(BF16)
    chunk = product.shape[0] // SIDE
    for k in range(SIDE):
        outs[k][...] = product[k * chunk : (k + 1) * chunk]


def project(order, features, weight):
    blocks, rows, depth = features.shape
    cols = weight.shape[1]
    tile = 1024
    chunk = blocks * rows // SIDE
    return pl.pallas_call(
        project_kernel,
        name="project",
        out_shape=[jax.ShapeDtypeStruct((chunk, cols), BF16)] * SIDE,
        grid_spec=pltpu.PrefetchScalarGridSpec(
            num_scalar_prefetch=1,
            grid=(cols // tile,),
            in_specs=[
                pl.BlockSpec((blocks, rows, depth), lambda i, _: (0, 0, 0)),
                pl.BlockSpec((depth, tile), lambda i, _: (0, i)),
            ],
            out_specs=[pl.BlockSpec((chunk, tile), lambda i, _: (0, i))] * SIDE,
            scratch_shapes=[pltpu.VMEM((blocks * rows, depth), BF16)],
        ),
        compiler_params=pltpu.CompilerParams(vmem_limit_bytes=VMEM_BYTES),
        cost_estimate=pl.CostEstimate(
            flops=2 * blocks * rows * depth * cols,
            bytes_accessed=2 * depth * cols + 2 * blocks * rows * cols,
            transcendentals=0,
        ),
    )(order, features, weight)


def dispatch_kernel(slot_ref, f_ref, *outs):
    count = outs[0].shape[0]
    rows = f_ref.shape[0]
    features = f_ref[...]
    for k in range(SIDE):
        slots = lax.broadcasted_iota(jnp.int32, (count, rows), 0) + k * count
        placing = (slots == slot_ref[...]).astype(F32).astype(BF16)
        outs[k][...] = jnp.dot(placing, features, preferred_element_type=F32).astype(BF16)


def dispatch(slot, features, count):
    rows, depth = features.shape
    return pl.pallas_call(
        dispatch_kernel,
        name="dispatch",
        out_shape=[jax.ShapeDtypeStruct((count, depth), BF16)] * SIDE,
        in_specs=whole(2),
        out_specs=whole(SIDE),
        compiler_params=pltpu.CompilerParams(vmem_limit_bytes=VMEM_BYTES),
        cost_estimate=pl.CostEstimate(
            flops=2 * SIDE * count * rows * depth,
            bytes_accessed=2 * (rows + SIDE * count) * depth,
            transcendentals=0,
        ),
    )(slot.reshape(1, rows), features)


QUAD = 4


def lanes_of(rows, rank, swapped):
    row = lax.broadcasted_iota(jnp.int32, (rows, 2 * rank), 0)
    lane = lax.broadcasted_iota(jnp.int32, (rows, 2 * rank), 1)
    member = (row % 16) // QUAD
    half = (lane // rank) ^ swapped
    return (member % 2) == half, member < 2


def shrink_kernel(s0, s1, s2, s3, own_ref, other_ref, o_ref):
    rank = o_ref.shape[1] // 2
    nt = (((1,), (1,)), ((), ()))
    quads = own_ref.shape[0] // (QUAD * rank)
    for pair in range(quads):
        total = None
        for swapped, weight_ref in ((0, own_ref), (1, other_ref)):
            quad = pair + swapped * quads
            rows = jnp.concatenate([s[quad * 16 : (quad + 1) * 16, :] for s in (s0, s1, s2, s3)])
            weight = weight_ref[pair * QUAD * rank : (pair + 1) * QUAD * rank, :]
            if swapped:
                weight = jnp.concatenate(
                    [weight[(m ^ 1) * rank : ((m ^ 1) + 1) * rank] for m in range(QUAD)]
                )
            got = lax.dot_general(rows, weight, nt, preferred_element_type=F32)
            mine, first = lanes_of(rows.shape[0], rank, swapped)
            kept = jnp.where(first, got[:, : 2 * rank], got[:, 2 * rank :])
            kept = jnp.where(mine, kept, 0.0)
            total = kept if total is None else total + kept
        o_ref[pair * 64 : (pair + 1) * 64, :] = total.astype(BF16)


def shrink(slots, own, other):
    rank = 64
    return pl.pallas_call(
        shrink_kernel,
        name="shrink",
        out_shape=jax.ShapeDtypeStruct((own.shape[0] // (QUAD * rank) * 64, 2 * rank), BF16),
        in_specs=whole(6),
        out_specs=whole(1)[0],
        compiler_params=pltpu.CompilerParams(vmem_limit_bytes=VMEM_BYTES),
        cost_estimate=pl.CostEstimate(flops=2**28, bytes_accessed=2**22, transcendentals=0),
    )(*slots, own, other)


def grow_kernel(h_ref, own_ref, other_ref, *outs):
    rank = h_ref.shape[1] // 2
    quads = own_ref.shape[0] // (QUAD * rank)
    for pair in range(quads):
        held = h_ref[pair * 64 : (pair + 1) * 64, :].astype(F32)
        for swapped, weight_ref in ((0, own_ref), (1, other_ref)):
            quad = pair + swapped * quads
            weight = weight_ref[pair * QUAD * rank : (pair + 1) * QUAD * rank, :]
            if swapped:
                weight = jnp.concatenate(
                    [weight[(m ^ 1) * rank : ((m ^ 1) + 1) * rank] for m in range(QUAD)]
                )
            mine, first = lanes_of(held.shape[0], rank, swapped)
            left = jnp.where(mine & first, held, 0.0).astype(BF16)
            right = jnp.where(mine & ~first, held, 0.0).astype(BF16)
            got = jnp.dot(
                jnp.concatenate([left, right], axis=1), weight, preferred_element_type=F32
            ).astype(BF16)
            for k in range(SIDE):
                outs[k][quad * 16 : (quad + 1) * 16, :] = got[k * 16 : (k + 1) * 16]


def grow(shrunk, own, other, count):
    return pl.pallas_call(
        grow_kernel,
        name="grow",
        out_shape=[jax.ShapeDtypeStruct((count, own.shape[1]), BF16)] * SIDE,
        in_specs=whole(3),
        out_specs=whole(SIDE),
        compiler_params=pltpu.CompilerParams(vmem_limit_bytes=VMEM_BYTES),
        cost_estimate=pl.CostEstimate(flops=2**28, bytes_accessed=2**22, transcendentals=0),
    )(shrunk, own, other)


def collect_kernel(slot_ref, r0, r1, r2, r3, o_ref):
    count = r0.shape[0]
    blocks, rows, cols = o_ref.shape
    total = jnp.zeros((blocks * rows, cols), F32)
    for k, ref in enumerate((r0, r1, r2, r3)):
        slots = lax.broadcasted_iota(jnp.int32, (blocks * rows, count), 1) + k * count
        placing = (slots == slot_ref[...]).astype(F32).astype(BF16)
        total = total + jnp.dot(placing, ref[...], preferred_element_type=F32)
    for t in range(blocks):
        o_ref[t] = total[t * rows : (t + 1) * rows].astype(BF16)


def collect(slot, returned, blocks):
    rows = slot.shape[0]
    cols = returned[0].shape[1]
    return pl.pallas_call(
        collect_kernel,
        name="collect",
        out_shape=jax.ShapeDtypeStruct((blocks, rows // blocks, cols), BF16),
        in_specs=whole(5),
        out_specs=whole(1)[0],
        compiler_params=pltpu.CompilerParams(vmem_limit_bytes=VMEM_BYTES),
        cost_estimate=pl.CostEstimate(flops=2**28, bytes_accessed=2**21, transcendentals=0),
    )(slot.reshape(rows, 1), *returned)


def finish_kernel(skip_ref, s_ref, a_ref, b_ref, c_ref, delta_ref, o_ref):
    blocks, _, cols = delta_ref.shape
    for t in range(blocks):
        at = slice(t * cols, (t + 1) * cols)
        base = (
            s_ref[:, at]
            + a_ref[:, at].astype(F32)
            + b_ref[:, at].astype(F32)
            + c_ref[:, at].astype(F32)
        )
        o_ref[:, at] = (
            skip_ref[:, at].astype(F32) + base + 2.0 * delta_ref[t].astype(F32)
        ).astype(BF16)


def finish(*operands):
    return pl.pallas_call(
        finish_kernel,
        name="finish",
        out_shape=jax.ShapeDtypeStruct(operands[0].shape, BF16),
        in_specs=whole(6),
        out_specs=whole(1)[0],
        compiler_params=pltpu.CompilerParams(vmem_limit_bytes=VMEM_BYTES),
        cost_estimate=pl.CostEstimate(flops=2**20, bytes_accessed=2**21, transcendentals=0),
    )(*operands)


def wide_sum(*terms):
    return sum(term.astype(F32) for term in terms)


def body(
    queries,
    cached_key_rows,
    cached_value_rows,
    fresh_key,
    fresh_value,
    lengths,
    adapter_index,
    skip_stream,
    output_weight,
    adapter_down_weight,
    adapter_up_weight,
):
    blocks = lax.axis_size("tp")
    rep, tp = lax.axis_index("rep"), lax.axis_index("tp")
    held, depth, rank = adapter_down_weight.shape
    width = output_weight.shape[1]

    down_own = jnp.swapaxes(adapter_down_weight, 1, 2).reshape(held * rank, depth)
    up_own = adapter_up_weight.reshape(held * rank, depth)
    down_other = pass_core(down_own)
    up_other = pass_core(up_own)

    adapter = adapter_index[:, 0]
    rows = adapter.shape[0]
    same = adapter[:, None] == adapter[None, :]
    count_up = jnp.arange(rows, dtype=jnp.int32)
    ranked = jnp.sum((same & (count_up[:, None] > count_up[None, :])).astype(jnp.int32), axis=1)
    owner = adapter // held
    cap = 4
    per_z = 2 * held * cap
    slot = (
        (owner // 2 - rep // 2) % SIDE * per_z
        + ((owner % 2) ^ (rep % 2)) * (held * cap)
        + (adapter % held) * cap
        + ranked
    )
    order = lax.dynamic_slice(jnp.asarray(row_order()), (rep * blocks + tp, 0), (1, blocks))[0]

    attended = attend(
        queries, cached_key_rows, cached_value_rows, fresh_key, fresh_value, lengths, blocks
    )
    features = lax.all_to_all(attended, "tp", split_axis=0, concat_axis=0, tiled=True)
    flat = features.reshape(rows, depth)

    placed = dispatch(slot, flat, per_z)
    arrived = [placed[0]] + [pass_z(placed[k], k) for k in range(1, SIDE)]

    partial = project(order, features, output_weight)
    first = [pass_plane(partial[k], "xy", k) for k in range(1, SIDE)]

    shrunk = shrink(arrived, down_own, down_other)
    for axis in ("xx", "yy"):
        shrunk = wide_sum(shrunk, *[pass_plane(shrunk, axis, k) for k in range(1, SIDE)]).astype(
            BF16
        )
    grown = grow(shrunk, up_own, up_other, per_z)
    returned = [grown[0]] + [pass_z(grown[k], -k) for k in range(1, SIDE)]
    delta = collect(slot, returned, blocks)

    summed = wide_sum(partial[0], *first).reshape(SIDE, rows // blocks, width)
    narrow = summed.astype(BF16)
    second = [pass_plane(narrow[k], "yx", k) for k in range(1, SIDE)]
    delta = lax.all_to_all(delta, "tp", split_axis=0, concat_axis=0, tiled=True)
    return finish(skip_stream, summed[0], *second, delta)


def solution(mesh):
    return jax.shard_map(
        body,
        mesh=mesh,
        in_specs=(
            P(BOTH, None, None),
            P(BOTH, None, None, None),
            P(BOTH, None, None, None),
            P(BOTH, None, None),
            P(BOTH, None, None),
            P(BOTH),
            P("rep", None),
            P(BOTH, None),
            P("tp", None),
            P("rep", "tp", None),
            P("rep", None, "tp"),
        ),
        out_specs=P(BOTH, None),
        check_vma=False,
    )
```

time: 168 us -> 126 us (0.75)
  the two profiles are of different devices: /device:TPU:0 before, /device:TPU:1 now
where the time goes in v1:
time: 126 us; the launch traced here: 125 us
  waiting for transfers between devices  50.8 us (40%)
  starting transfers between devices  33.3 us (26%)
  Pallas kernels  23.6 us (19%)
  local copies, waits for them, and re-layouts  12.2 us (10%)
  other arithmetic  5.36 us (4%)
    ppermute x12, waiting for transfers between devices, pass_plane(): return lax.ppermute(value, BOTH, pairs)  33.9 us
    pallas_call x1, Pallas kernels, attend(): pl.pallas_call(body, name='attend', out_shape=jax.ShapeDtypeStruct((block...  11.5 us
    ppermute x12, starting transfers between devices, pass_plane(): return lax.ppermute(value, BOTH, pairs)  10.5 us
    unnamed x23, local copies, waits for them, and re-layouts  10.1 us
    ppermute x6, starting transfers between devices, pass_z(): return lax.ppermute(value, BOTH, pairs)  8.73 us
    all_to_all x1, waiting for transfers between devices, body(): lax.all_to_all(attended, 'tp', split_axis=0, concat_axis=0, tiled=True)  8.29 us
    all_to_all x1, starting transfers between devices, body(): lax.all_to_all(attended, 'tp', split_axis=0, concat_axis=0, tiled=True)  6.84 us
    all_to_all x1, waiting for transfers between devices, body(): delta = lax.all_to_all(delta, 'tp', split_axis=0, concat_axis=0, tiled=True)  6.46 us
  transfers between devices with their start and end apart: 22, of which 7 were waited for; matrix products, arithmetic and copies ran while one was open for 6% of the time, Pallas kernels for 18%

profile of v1, /device:TPU:1, one launch (start us, length us, event | category | flops | bytes accessed | tf_op | source)
XLA Modules:
  0.0 125.3 jit_solution(6485759881048428422)
XLA Ops:
  0.0 1.4 %collective-permute-start.9 = (bf16[1024,512]{1,0:T(8,128)(2,1)}, bf16[1024,512]{1,0:T(8,128)(2,1)}, u32[]{:S(2)}, u32[]{:S(2)}) collective-permute-start(bf16[1024,512]{1,0:T(8,128)(2,1)} %bitcast.28), channel_id=1, source_target_pairs={{0,16},{1,17},{2,18},{3,19},{4,20},{5,21},{6,22},{7,23},{8,24},{9,... | collective-permute-start | bytes 3145736 | tf_op jit(solution)/shard_map/ppermute | solution.py:44
  1.4 3.4 %copy-done = bf16[16,8,256,128]{3,2,1,0:T(8,128)(2,1)S(1)} copy-done((bf16[16,8,256,128]{3,2,1,0:T(8,128)(2,1)S(1)}, bf16[16,8,256,128]{3,2,1,0:T(8,128)(2,1)}, u32[]{:S(2)}) %copy-start) | copy-done | bytes 8388632
  4.8 0.9 copy-done.4
  7.9 11.5 %attend.1 = bf16[16,16,512]{2,1,0:T(8,128)(2,1)} custom-call(s32[16]{0:T(128)S(1)} %copy-done.8, bf16[16,64,128]{2,1,0:T(8,128)(2,1)S(1)} %copy-done.4, bf16[16,8,256,128]{3,2,1,0:T(8,128)(2,1)S(1)} %copy-done, bf16[16,8,256,128]{3,2,1,0:T(8,128)(2,1)} %refs_3_.1, bf16[16,8,128]{2,1,0:T(8,128)(2,1)S(1)} %copy-done.6, bf16[16,8,128]{2,1,0:T(8,128)(2,1)S(1)} %copy-done.7), custom_call_target="tpu_custom_call" | custom-call | flops 134217728 | bytes 16777216 | tf_op jit(solution)/shard_map/attend/pallas_call | solution.py:127
  19.5 6.8 %all-to-all-start = ((bf16[16,16,512]{2,1,0:T(8,128)(2,1)}), bf16[16,16,512]{2,1,0:T(8,128)(2,1)S(1)}, u32[]{:S(2)}, u32[]{:S(2)}) async-start(bf16[16,16,512]{2,1,0:T(8,128)(2,1)} %attend.1), calls=%async_computation | async-start | bytes 524288 | tf_op jit(solution)/shard_map/all_to_all | solution.py:406
  26.6 8.3 %all-to-all-done.f_ref = bf16[16,16,512]{2,1,0:T(8,128)(2,1)S(1)} async-done(((bf16[16,16,512]{2,1,0:T(8,128)(2,1)}), bf16[16,16,512]{2,1,0:T(8,128)(2,1)S(1)}, u32[]{:S(2)}, u32[]{:S(2)}) %all-to-all-start) | async-done | bytes 262176 | tf_op jit(solution)/shard_map/all_to_all | solution.py:406
  34.8 1.0 dispatch.1
  35.8 1.6 %collective-permute-start.6 = (bf16[128,512]{1,0:T(8,128)(2,1)}, bf16[128,512]{1,0:T(8,128)(2,1)}, u32[]{:S(2)}, u32[]{:S(2)}) collective-permute-start(bf16[128,512]{1,0:T(8,128)(2,1)} %get-tuple-element.22), channel_id=1, source_target_pairs={{0,32},{1,33},{2,34},{3,35},{4,36},{5,37},{6,38},{7,39},{8,40},{9,... | collective-permute-start | bytes 393224 | tf_op jit(solution)/shard_map/ppermute | solution.py:40
  37.5 3.3 %collective-permute-start.7 = (bf16[128,512]{1,0:T(8,128)(2,1)}, bf16[128,512]{1,0:T(8,128)(2,1)}, u32[]{:S(2)}, u32[]{:S(2)}) collective-permute-start(bf16[128,512]{1,0:T(8,128)(2,1)} %get-tuple-element.23), channel_id=1, source_target_pairs={{0,64},{1,65},{2,66},{3,67},{4,68},{5,69},{6,70},{7,71},{8,72},{9,... | collective-permute-start | bytes 393224 | tf_op jit(solution)/shard_map/ppermute | solution.py:40
  41.5 1.9 %collective-permute-start.16 = (bf16[1024,512]{1,0:T(8,128)(2,1)S(1)}, bf16[1024,512]{1,0:T(8,128)(2,1)S(1)}, u32[]{:S(2)}, u32[]{:S(2)}) collective-permute-start(bf16[1024,512]{1,0:T(8,128)(2,1)S(1)} %bitcast.26), channel_id=1, source_target_pairs={{0,16},{1,17},{2,18},{3,19},{4,20},{5,21},{6,22},{7,23},{8,24},{9,... | collective-permute-start | bytes 3145736 | tf_op jit(solution)/shard_map/ppermute | solution.py:44
  44.1 1.9 %collective-permute-done.7.s2 = bf16[128,512]{1,0:T(8,128)(2,1)} collective-permute-done((bf16[128,512]{1,0:T(8,128)(2,1)}, bf16[128,512]{1,0:T(8,128)(2,1)}, u32[]{:S(2)}, u32[]{:S(2)}) %collective-permute-start.7) | collective-permute-done | bytes 131104 | tf_op jit(solution)/shard_map/ppermute | solution.py:40
  46.2 2.2 %shrink.1 = bf16[256,128]{1,0:T(8,128)(2,1)S(1)} custom-call(bf16[128,512]{1,0:T(8,128)(2,1)S(1)} %get-tuple-element.21.s0, bf16[128,512]{1,0:T(8,128)(2,1)} %collective-permute-done.6.s1, bf16[128,512]{1,0:T(8,128)(2,1)} %collective-permute-done.7.s2, bf16[128,512]{1,0:T(8,128)(2,1)} %collective-permute-done.8.s3, bf16[1024,512]{1,0:T(8,128)(2,1)S(1)} %bitcast.29, ...), custom_call_target="tpu_custom_call" | custom-call | flops 268435456 | bytes 4194304 | tf_op jit(solution)/shard_map/shrink/pallas_call | solution.py:262
  48.7 1.8 %collective-permute-start.11 = (bf16[256,128]{1,0:T(8,128)(2,1)S(1)}, bf16[256,128]{1,0:T(8,128)(2,1)S(1)}, u32[]{:S(2)}, u32[]{:S(2)}) collective-permute-start(bf16[256,128]{1,0:T(8,128)(2,1)S(1)} %shrink.1), channel_id=1, source_target_pairs={{0,2},{1,3},{2,0},{3,1},{4,6},{5,7},{6,4},{7,5},{8,10},{9,11},{10,... | collective-permute-start | bytes 196616 | tf_op jit(solution)/shard_map/ppermute | solution.py:35
  50.5 3.4 %copy-done.1 = bf16[512,8192]{1,0:T(8,128)(2,1)S(1)} copy-done((bf16[512,8192]{1,0:T(8,128)(2,1)S(1)}, bf16[512,8192]{1,0:T(8,128)(2,1)}, u32[]{:S(2)}) %copy-start.1) | copy-done | bytes 8388632
  53.9 6.3 %project.1 = (bf16[64,8192]{1,0:T(8,128)(2,1)S(1)}, bf16[64,8192]{1,0:T(8,128)(2,1)}, bf16[64,8192]{1,0:T(8,128)(2,1)}, bf16[64,8192]{1,0:T(8,128)(2,1)}) custom-call(s32[16]{0:T(128)S(1)} %dynamic-slice_bitcast_fusion.order_ref, bf16[16,16,512]{2,1,0:T(8,128)(2,1)S(1)} %all-to-all-done.f_ref, bf16[512,8192]{1,0:T(8,128)(2,1)S(1)} %copy-done.1), custom_call_target="tpu_custom_call" | custom-call | flops 2147483648 | bytes 12582912 | tf_op jit(solution)/shard_map/project/pallas_call | solution.py:177
  60.2 1.8 %collective-permute-start.1 = (bf16[64,8192]{1,0:T(8,128)(2,1)}, bf16[64,8192]{1,0:T(8,128)(2,1)}, u32[]{:S(2)}, u32[]{:S(2)}) collective-permute-start(bf16[64,8192]{1,0:T(8,128)(2,1)} %get-tuple-element.19), channel_id=1, source_target_pairs={{0,2},{1,3},{2,0},{3,1},{4,6},{5,7},{6,4},{7,5},{8,10},{9,11},{10,... | collective-permute-start | bytes 3145736 | tf_op jit(solution)/shard_map/ppermute | solution.py:35
  62.0 1.0 collective-permute-start.2
  63.7 26.0 %collective-permute-done.15 = bf16[256,128]{1,0:T(8,128)(2,1)S(1)} collective-permute-done((bf16[256,128]{1,0:T(8,128)(2,1)S(1)}, bf16[256,128]{1,0:T(8,128)(2,1)S(1)}, u32[]{:S(2)}, u32[]{:S(2)}) %collective-permute-start.15) | collective-permute-done | bytes 65568 | tf_op jit(solution)/shard_map/ppermute | solution.py:35
  90.8 3.6 %collective-permute-done.14 = bf16[256,128]{1,0:T(8,128)(2,1)} collective-permute-done((bf16[256,128]{1,0:T(8,128)(2,1)S(1)}, bf16[256,128]{1,0:T(8,128)(2,1)}, u32[]{:S(2)}, u32[]{:S(2)}) %collective-permute-start.14) | collective-permute-done | bytes 65568 | tf_op jit(solution)/shard_map/ppermute | solution.py:35
  94.7 4.3 %collective-permute-done.13 = bf16[256,128]{1,0:T(8,128)(2,1)S(1)} collective-permute-done((bf16[256,128]{1,0:T(8,128)(2,1)S(1)}, bf16[256,128]{1,0:T(8,128)(2,1)S(1)}, u32[]{:S(2)}, u32[]{:S(2)}) %collective-permute-start.13) | collective-permute-done | bytes 65568 | tf_op jit(solution)/shard_map/ppermute | solution.py:35
  99.0 0.9 add_convert_fusion.h_ref
  100.4 1.9 %collective-permute-start.17 = (bf16[128,512]{1,0:T(8,128)(2,1)S(1)}, bf16[128,512]{1,0:T(8,128)(2,1)S(1)}, u32[]{:S(2)}, u32[]{:S(2)}) collective-permute-start(bf16[128,512]{1,0:T(8,128)(2,1)S(1)} %get-tuple-element.26), channel_id=1, source_target_pairs={{0,96},{1,97},{2,98},{3,99},{4,100},{5,101},{6,102},{7,103},{8,104... | collective-permute-start | bytes 393224 | tf_op jit(solution)/shard_map/ppermute | solution.py:40
  102.3 1.1 collective-permute-start.18
  103.5 3.9 %fusion.20 = (bf16[64,8192]{1,0:T(8,128)(2,1)S(1)}, f32[64,8192]{1,0:T(8,128)}) fusion(bf16[64,8192]{1,0:T(8,128)(2,1)} %collective-permute-done.2, bf16[64,8192]{1,0:T(8,128)(2,1)} %collective-permute-done.1, bf16[64,8192]{1,0:T(8,128)(2,1)} %collective-permute-done, bf16[64,8192]{1,0:T(8,128)(2,1)S(1)} %get-tuple-element.17), kind=kLoop, calls=%fused_computation.56 | loop fusion | flops 4194304 | bytes 7340032 | tf_op jit(solution)/shard_map/convert_element_type | solution.py:425
  107.4 2.7 %collective-permute-start.5 = (bf16[16,8192]{1,0:T(8,128)(2,1)S(1)}, bf16[16,8192]{1,0:T(8,128)(2,1)S(1)}, u32[]{:S(2)}, u32[]{:S(2)}) collective-permute-start(bf16[16,8192]{1,0:T(8,128)(2,1)S(1)} %get-tuple-element.31), channel_id=1, source_target_pairs={{0,12},{1,13},{2,14},{3,15},{4,0},{5,1},{6,2},{7,3},{8,4},{9,5},{1... | collective-permute-start | bytes 786440 | tf_op jit(solution)/shard_map/ppermute | solution.py:35
  110.2 0.9 collective-permute-start.4
  111.0 0.8 collective-permute-start.3
  111.8 1.2 collect.1
  113.0 3.8 %all-to-all-start.1 = ((bf16[16,16,512]{2,1,0:T(8,128)(2,1)}), bf16[16,16,512]{2,1,0:T(8,128)(2,1)S(1)}, u32[]{:S(2)}, u32[]{:S(2)}) async-start(bf16[16,16,512]{2,1,0:T(8,128)(2,1)} %collect.1), calls=%async_computation.1 | async-start | bytes 524288 | tf_op jit(solution)/shard_map/all_to_all | solution.py:427
  116.8 1.1 slice.20.s_ref
  117.9 6.5 %all-to-all-done.1.delta_ref = bf16[16,16,512]{2,1,0:T(8,128)(2,1)S(1)} async-done(((bf16[16,16,512]{2,1,0:T(8,128)(2,1)}), bf16[16,16,512]{2,1,0:T(8,128)(2,1)S(1)}, u32[]{:S(2)}, u32[]{:S(2)}) %all-to-all-start.1) | async-done | bytes 262176 | tf_op jit(solution)/shard_map/all_to_all | solution.py:427
  124.4 0.9 finish.1
  (54 shorter events, 7.0 us)
Async XLA Ops:
  0.0 46.2 %collective-permute-start.9 = (bf16[1024,512]{1,0:T(8,128)(2,1)}, bf16[1024,512]{1,0:T(8,128)(2,1)}, u32[]{:S(2)}, u32[]{:S(2)}) collective-permute-start(bf16[1024,512]{1,0:T(8,128)(2,1)} %bitcast.28), channel_id=1, source_target_pairs={{0,16},{1,17},{2,18},{3,19},{4,20},{5,21},{6,22},{7,23},{8,24},{9,... | collective-permute-start | bytes 3145736 | tf_op jit(solution)/shard_map/ppermute | solution.py:44
  1.4 3.4 %copy-start = (bf16[16,8,256,128]{3,2,1,0:T(8,128)(2,1)S(1)}, bf16[16,8,256,128]{3,2,1,0:T(8,128)(2,1)}, u32[]{:S(2)}) copy-start(bf16[16,8,256,128]{3,2,1,0:T(8,128)(2,1)} %refs_2_.1) | copy-start | bytes 25165828
  4.8 0.9 copy-start.4
  5.8 0.8 copy-start.6
  6.5 0.8 copy-start.7
  7.3 0.7 copy-start.8
  7.9 18.4 %copy-start.10 = (s32[256,1]{0,1:T(1,128)S(1)}, s32[256,1]{0,1:T(1,128)}, u32[]{:S(2)}) copy-start(s32[256,1]{0,1:T(1,128)} %param.18) | copy-start | bytes 3076
  7.9 33.6 %copy-start.2 = (bf16[16,64,512]{2,1,0:T(8,128)(2,1)S(1)}, bf16[16,64,512]{2,1,0:T(8,128)(2,1)}, u32[]{:S(2)}) copy-start(bf16[16,64,512]{2,1,0:T(8,128)(2,1)} %param.22) | copy-start | bytes 3145732
  7.9 38.3 %copy-start.3 = (bf16[16,512,64]{1,2,0:T(8,128)(2,1)S(1)}, bf16[16,512,64]{1,2,0:T(8,128)(2,1)}, u32[]{:S(2)}) copy-start(bf16[16,512,64]{1,2,0:T(8,128)(2,1)} %param.21) | copy-start | bytes 3145732
  19.5 15.4 %all-to-all-start = ((bf16[16,16,512]{2,1,0:T(8,128)(2,1)}), bf16[16,16,512]{2,1,0:T(8,128)(2,1)S(1)}, u32[]{:S(2)}, u32[]{:S(2)}) async-start(bf16[16,16,512]{2,1,0:T(8,128)(2,1)} %attend.1), calls=%async_computation | async-start | bytes 524288 | tf_op jit(solution)/shard_map/all_to_all | solution.py:406
  35.8 8.3 %collective-permute-start.6 = (bf16[128,512]{1,0:T(8,128)(2,1)}, bf16[128,512]{1,0:T(8,128)(2,1)}, u32[]{:S(2)}, u32[]{:S(2)}) collective-permute-start(bf16[128,512]{1,0:T(8,128)(2,1)} %get-tuple-element.22), channel_id=1, source_target_pairs={{0,32},{1,33},{2,34},{3,35},{4,36},{5,37},{6,38},{7,39},{8,40},{9,... | collective-permute-start | bytes 393224 | tf_op jit(solution)/shard_map/ppermute | solution.py:40
  37.5 8.6 %collective-permute-start.7 = (bf16[128,512]{1,0:T(8,128)(2,1)}, bf16[128,512]{1,0:T(8,128)(2,1)}, u32[]{:S(2)}, u32[]{:S(2)}) collective-permute-start(bf16[128,512]{1,0:T(8,128)(2,1)} %get-tuple-element.23), channel_id=1, source_target_pairs={{0,64},{1,65},{2,66},{3,67},{4,68},{5,69},{6,70},{7,71},{8,72},{9,... | collective-permute-start | bytes 393224 | tf_op jit(solution)/shard_map/ppermute | solution.py:40
  40.8 5.4 %collective-permute-start.8 = (bf16[128,512]{1,0:T(8,128)(2,1)}, bf16[128,512]{1,0:T(8,128)(2,1)}, u32[]{:S(2)}, u32[]{:S(2)}) collective-permute-start(bf16[128,512]{1,0:T(8,128)(2,1)} %get-tuple-element.24), channel_id=1, source_target_pairs={{0,96},{1,97},{2,98},{3,99},{4,100},{5,101},{6,102},{7,103},{8,104... | collective-permute-start | bytes 393224 | tf_op jit(solution)/shard_map/ppermute | solution.py:40
  41.5 58.4 %collective-permute-start.16 = (bf16[1024,512]{1,0:T(8,128)(2,1)S(1)}, bf16[1024,512]{1,0:T(8,128)(2,1)S(1)}, u32[]{:S(2)}, u32[]{:S(2)}) collective-permute-start(bf16[1024,512]{1,0:T(8,128)(2,1)S(1)} %bitcast.26), channel_id=1, source_target_pairs={{0,16},{1,17},{2,18},{3,19},{4,20},{5,21},{6,22},{7,23},{8,24},{9,... | collective-permute-start | bytes 3145736 | tf_op jit(solution)/shard_map/ppermute | solution.py:44
  48.4 11.8 %collective-permute-start.12 = (bf16[256,128]{1,0:T(8,128)(2,1)S(1)}, bf16[256,128]{1,0:T(8,128)(2,1)S(1)}, u32[]{:S(2)}, u32[]{:S(2)}) collective-permute-start(bf16[256,128]{1,0:T(8,128)(2,1)S(1)} %shrink.1), channel_id=1, source_target_pairs={{0,3},{1,0},{2,1},{3,2},{4,7},{5,4},{6,5},{7,6},{8,11},{9,8},{10,9... | collective-permute-start | bytes 196616 | tf_op jit(solution)/shard_map/ppermute | solution.py:35
  48.7 13.2 %collective-permute-start.11 = (bf16[256,128]{1,0:T(8,128)(2,1)S(1)}, bf16[256,128]{1,0:T(8,128)(2,1)S(1)}, u32[]{:S(2)}, u32[]{:S(2)}) collective-permute-start(bf16[256,128]{1,0:T(8,128)(2,1)S(1)} %shrink.1), channel_id=1, source_target_pairs={{0,2},{1,3},{2,0},{3,1},{4,6},{5,7},{6,4},{7,5},{8,10},{9,11},{10,... | collective-permute-start | bytes 196616 | tf_op jit(solution)/shard_map/ppermute | solution.py:35
  50.5 12.4 %collective-permute-start.10 = (bf16[256,128]{1,0:T(8,128)(2,1)S(1)}, bf16[256,128]{1,0:T(8,128)(2,1)S(1)}, u32[]{:S(2)}, u32[]{:S(2)}) collective-permute-start(bf16[256,128]{1,0:T(8,128)(2,1)S(1)} %shrink.1), channel_id=1, source_target_pairs={{0,1},{1,2},{2,3},{3,0},{4,5},{5,6},{6,7},{7,4},{8,9},{9,10},{10,1... | collective-permute-start | bytes 196616 | tf_op jit(solution)/shard_map/ppermute | solution.py:35
  50.5 3.4 %copy-start.1 = (bf16[512,8192]{1,0:T(8,128)(2,1)S(1)}, bf16[512,8192]{1,0:T(8,128)(2,1)}, u32[]{:S(2)}) copy-start(bf16[512,8192]{1,0:T(8,128)(2,1)} %w_ref.1) | copy-start | bytes 25165828
  60.2 43.3 %collective-permute-start = (bf16[64,8192]{1,0:T(8,128)(2,1)}, bf16[64,8192]{1,0:T(8,128)(2,1)}, u32[]{:S(2)}, u32[]{:S(2)}) collective-permute-start(bf16[64,8192]{1,0:T(8,128)(2,1)} %get-tuple-element.18), channel_id=1, source_target_pairs={{0,1},{1,2},{2,3},{3,0},{4,5},{5,6},{6,7},{7,4},{8,9},{9,10},{10,1... | collective-permute-start | bytes 3145736 | tf_op jit(solution)/shard_map/ppermute | solution.py:35
  60.2 43.3 %collective-permute-start.1 = (bf16[64,8192]{1,0:T(8,128)(2,1)}, bf16[64,8192]{1,0:T(8,128)(2,1)}, u32[]{:S(2)}, u32[]{:S(2)}) collective-permute-start(bf16[64,8192]{1,0:T(8,128)(2,1)} %get-tuple-element.19), channel_id=1, source_target_pairs={{0,2},{1,3},{2,0},{3,1},{4,6},{5,7},{6,4},{7,5},{8,10},{9,11},{10,... | collective-permute-start | bytes 3145736 | tf_op jit(solution)/shard_map/ppermute | solution.py:35
  62.0 41.5 %collective-permute-start.2 = (bf16[64,8192]{1,0:T(8,128)(2,1)}, bf16[64,8192]{1,0:T(8,128)(2,1)}, u32[]{:S(2)}, u32[]{:S(2)}) collective-permute-start(bf16[64,8192]{1,0:T(8,128)(2,1)} %get-tuple-element.20), channel_id=1, source_target_pairs={{0,3},{1,0},{2,1},{3,2},{4,7},{5,4},{6,5},{7,6},{8,11},{9,8},{10,9... | collective-permute-start | bytes 3145736 | tf_op jit(solution)/shard_map/ppermute | solution.py:35
  63.0 26.6 %collective-permute-start.15 = (bf16[256,128]{1,0:T(8,128)(2,1)S(1)}, bf16[256,128]{1,0:T(8,128)(2,1)S(1)}, u32[]{:S(2)}, u32[]{:S(2)}) collective-permute-start(bf16[256,128]{1,0:T(8,128)(2,1)S(1)} %add_convert_fusion.1), channel_id=1, source_target_pairs={{0,12},{1,13},{2,14},{3,15},{4,0},{5,1},{6,2},{7,3},{8,4},{9,5},{1... | collective-permute-start | bytes 196616 | tf_op jit(solution)/shard_map/ppermute | solution.py:35
  89.6 4.7 %collective-permute-start.14 = (bf16[256,128]{1,0:T(8,128)(2,1)S(1)}, bf16[256,128]{1,0:T(8,128)(2,1)}, u32[]{:S(2)}, u32[]{:S(2)}) collective-permute-start(bf16[256,128]{1,0:T(8,128)(2,1)S(1)} %add_convert_fusion.1), channel_id=1, source_target_pairs={{0,8},{1,9},{2,10},{3,11},{4,12},{5,13},{6,14},{7,15},{8,0},{9,1},... | collective-permute-start | bytes 196616 | tf_op jit(solution)/shard_map/ppermute | solution.py:35
  94.4 4.6 %collective-permute-start.13 = (bf16[256,128]{1,0:T(8,128)(2,1)S(1)}, bf16[256,128]{1,0:T(8,128)(2,1)S(1)}, u32[]{:S(2)}, u32[]{:S(2)}) collective-permute-start(bf16[256,128]{1,0:T(8,128)(2,1)S(1)} %add_convert_fusion.1), channel_id=1, source_target_pairs={{0,4},{1,5},{2,6},{3,7},{4,8},{5,9},{6,10},{7,11},{8,12},{9,13},{1... | collective-permute-start | bytes 196616 | tf_op jit(solution)/shard_map/ppermute | solution.py:35
  100.4 10.6 %collective-permute-start.17 = (bf16[128,512]{1,0:T(8,128)(2,1)S(1)}, bf16[128,512]{1,0:T(8,128)(2,1)S(1)}, u32[]{:S(2)}, u32[]{:S(2)}) collective-permute-start(bf16[128,512]{1,0:T(8,128)(2,1)S(1)} %get-tuple-element.26), channel_id=1, source_target_pairs={{0,96},{1,97},{2,98},{3,99},{4,100},{5,101},{6,102},{7,103},{8,104... | collective-permute-start | bytes 393224 | tf_op jit(solution)/shard_map/ppermute | solution.py:40
  102.3 9.5 %collective-permute-start.18 = (bf16[128,512]{1,0:T(8,128)(2,1)S(1)}, bf16[128,512]{1,0:T(8,128)(2,1)S(1)}, u32[]{:S(2)}, u32[]{:S(2)}) collective-permute-start(bf16[128,512]{1,0:T(8,128)(2,1)S(1)} %get-tuple-element.27), channel_id=1, source_target_pairs={{0,64},{1,65},{2,66},{3,67},{4,68},{5,69},{6,70},{7,71},{8,72},{9,... | collective-permute-start | bytes 393224 | tf_op jit(solution)/shard_map/ppermute | solution.py:40
  103.5 8.3 %collective-permute-start.19 = (bf16[128,512]{1,0:T(8,128)(2,1)S(1)}, bf16[128,512]{1,0:T(8,128)(2,1)S(1)}, u32[]{:S(2)}, u32[]{:S(2)}) collective-permute-start(bf16[128,512]{1,0:T(8,128)(2,1)S(1)} %get-tuple-element.28), channel_id=1, source_target_pairs={{0,32},{1,33},{2,34},{3,35},{4,36},{5,37},{6,38},{7,39},{8,40},{9,... | collective-permute-start | bytes 393224 | tf_op jit(solution)/shard_map/ppermute | solution.py:40
  107.4 17.0 %copy-start.5 = (bf16[16,8192]{1,0:T(8,128)(2,1)S(1)}, bf16[16,8192]{1,0:T(8,128)(2,1)}, u32[]{:S(2)}) copy-start(bf16[16,8192]{1,0:T(8,128)(2,1)} %skip_ref.1) | copy-start | bytes 786436
  107.4 17.0 %collective-permute-start.5 = (bf16[16,8192]{1,0:T(8,128)(2,1)S(1)}, bf16[16,8192]{1,0:T(8,128)(2,1)S(1)}, u32[]{:S(2)}, u32[]{:S(2)}) collective-permute-start(bf16[16,8192]{1,0:T(8,128)(2,1)S(1)} %get-tuple-element.31), channel_id=1, source_target_pairs={{0,12},{1,13},{2,14},{3,15},{4,0},{5,1},{6,2},{7,3},{8,4},{9,5},{1... | collective-permute-start | bytes 786440 | tf_op jit(solution)/shard_map/ppermute | solution.py:35
  110.2 14.2 %collective-permute-start.4 = (bf16[16,8192]{1,0:T(8,128)(2,1)S(1)}, bf16[16,8192]{1,0:T(8,128)(2,1)S(1)}, u32[]{:S(2)}, u32[]{:S(2)}) collective-permute-start(bf16[16,8192]{1,0:T(8,128)(2,1)S(1)} %get-tuple-element.32), channel_id=1, source_target_pairs={{0,8},{1,9},{2,10},{3,11},{4,12},{5,13},{6,14},{7,15},{8,0},{9,1},... | collective-permute-start | bytes 786440 | tf_op jit(solution)/shard_map/ppermute | solution.py:35
  111.0 13.3 %collective-permute-start.3 = (bf16[16,8192]{1,0:T(8,128)(2,1)S(1)}, bf16[16,8192]{1,0:T(8,128)(2,1)S(1)}, u32[]{:S(2)}, u32[]{:S(2)}) collective-permute-start(bf16[16,8192]{1,0:T(8,128)(2,1)S(1)} %get-tuple-element.33), channel_id=1, source_target_pairs={{0,4},{1,5},{2,6},{3,7},{4,8},{5,9},{6,10},{7,11},{8,12},{9,13},{1... | collective-permute-start | bytes 786440 | tf_op jit(solution)/shard_map/ppermute | solution.py:35
  113.0 11.4 %all-to-all-start.1 = ((bf16[16,16,512]{2,1,0:T(8,128)(2,1)}), bf16[16,16,512]{2,1,0:T(8,128)(2,1)S(1)}, u32[]{:S(2)}, u32[]{:S(2)}) async-start(bf16[16,16,512]{2,1,0:T(8,128)(2,1)} %collect.1), calls=%async_computation.1 | async-start | bytes 524288 | tf_op jit(solution)/shard_map/all_to_all | solution.py:427
  (1 other events, 0.6 us)

commit v2 on v1

--- a/solution.py
+++ b/solution.py
@@ -12,7 +12,8 @@
 BF16 = jnp.bfloat16
 BOTH = ("rep", "tp")
 SIDE = 4
-VMEM_BYTES = 40 * 1024 * 1024
+VMEM_BYTES = 24 * 1024 * 1024
+FULL_VMEM = 60 * 1024 * 1024
 
 
 def place(z, c, y, x):
@@ -58,94 +59,103 @@
     return table
 
 
-PER_STEP = 2
+AT_ONCE = 4
 
 
 def attend_kernel(
-    lengths_ref, q_ref, k_ref, v_ref, fk_ref, fv_ref, o_ref, mixed_ref, *, groups, fold, span
+    lengths_ref, q_ref, k_hbm, v_hbm, fk_ref, fv_ref, o_ref, k_ref, v_ref, mixed_ref, k_sem, v_sem
 ):
-    step = pl.program_id(0)
-    heads = groups * fold
-    width = q_ref.shape[-1]
+    rows, heads, width = q_ref.shape
+    groups, span = k_ref.shape[1], k_ref.shape[2]
+    fold = heads // groups
+    steps = rows // AT_ONCE
     factor = 1.0 / math.sqrt(width)
-    position = lax.broadcasted_iota(jnp.int32, (heads, span), 1)
     nt = (((1,), (1,)), ((), ()))
-    for item in range(PER_STEP):
-        row = step * PER_STEP + item
-        q = q_ref[item]
-        parts = []
-        for g in range(groups):
-            two = q[(g // 2) * 2 * fold : (g // 2 + 1) * 2 * fold]
-            got = lax.dot_general(two, k_ref[item, g], nt, preferred_element_type=F32)
-            parts.append(got[(g % 2) * fold : (g % 2 + 1) * fold])
-        scores = jnp.concatenate(parts, axis=0) * factor
-        fresh_k = jnp.broadcast_to(
-            fk_ref[item].astype(F32)[:, None, :], (groups, fold, width)
-        ).reshape(heads, width)
-        own = jnp.sum(q.astype(F32) * fresh_k, axis=-1, keepdims=True) * factor
-        valid = position < lengths_ref[row]
-        masked = jnp.where(valid, scores, -jnp.inf)
-        top = jnp.maximum(jnp.max(masked, axis=-1, keepdims=True), own)
-        expo = jnp.exp(masked - top)
-        expo_own = jnp.exp(own - top)
-        total = jnp.sum(expo, axis=-1, keepdims=True) + expo_own
-        inverse = 1.0 / total
-        probs = (expo * inverse).astype(BF16)
-        probs_own = (expo_own * inverse).astype(BF16).astype(F32)
-        parts = []
-        for g in range(groups):
-            two = probs[(g // 2) * 2 * fold : (g // 2 + 1) * 2 * fold]
-            got = jnp.dot(two, v_ref[item, g], preferred_element_type=F32)
-            parts.append(got[(g % 2) * fold : (g % 2 + 1) * fold])
-        fresh_v = jnp.broadcast_to(
-            fv_ref[item].astype(F32)[:, None, :], (groups, fold, width)
-        ).reshape(heads, width)
-        mixed = jnp.concatenate(parts, axis=0) + probs_own * fresh_v
-        mixed_ref[pl.ds(pl.multiple_of(row * heads, heads), heads), :] = mixed
-
-    @pl.when(step == pl.num_programs(0) - 1)
-    def _():
-        blocks, rows, cols = o_ref.shape
-        per_block = cols // width
-        for h in range(heads):
-            tile = jnp.concatenate(
-                [
-                    mixed_ref[pl.ds(half * 8 * heads + h, 8, stride=heads), :]
-                    for half in range(rows // 8)
-                ],
-                axis=0,
-            )
-            lane = (h % per_block) * width
-            o_ref[h // per_block, :, lane : lane + width] = tile.astype(BF16)
+
+    def copy(step, far, near, sem):
+        at = pl.ds(step * AT_ONCE, AT_ONCE)
+        return pltpu.make_async_copy(far.at[at], near.at[at], sem.at[step])
+
+    for step in range(steps):
+        copy(step, k_hbm, k_ref, k_sem).start()
+        copy(step, v_hbm, v_ref, v_sem).start()
+
+    def one_step(step, carry):
+        copy(step, k_hbm, k_ref, k_sem).wait()
+        all_scores = []
+        for item in range(AT_ONCE):
+            row = step * AT_ONCE + item
+            q = q_ref[row]
+            parts = []
+            for g in range(groups):
+                two = q[(g // 2) * 2 * fold : (g // 2 + 1) * 2 * fold]
+                got = lax.dot_general(two, k_ref[row, g], nt, preferred_element_type=F32)
+                parts.append(got[(g % 2) * fold : (g % 2 + 1) * fold])
+            all_scores.append(jnp.concatenate(parts, axis=0) * factor)
+        copy(step, v_hbm, v_ref, v_sem).wait()
+        for item in range(AT_ONCE):
+            row = step * AT_ONCE + item
+            scores = all_scores[item]
+            fresh_k = jnp.broadcast_to(
+                fk_ref[row].astype(F32)[:, None, :], (groups, fold, width)
+            ).reshape(heads, width)
+            own = jnp.sum(q_ref[row].astype(F32) * fresh_k, axis=-1, keepdims=True) * factor
+            position = lax.broadcasted_iota(jnp.int32, (heads, span), 1)
+            masked = jnp.where(position < lengths_ref[row], scores, -jnp.inf)
+            top = jnp.maximum(jnp.max(masked, axis=-1, keepdims=True), own)
+            expo = jnp.exp(masked - top)
+            expo_own = jnp.exp(own - top)
+            inverse = 1.0 / (jnp.sum(expo, axis=-1, keepdims=True) + expo_own)
+            probs = (expo * inverse).astype(BF16)
+            probs_own = (expo_own * inverse).astype(BF16).astype(F32)
+            parts = []
+            for g in range(groups):
+                two = probs[(g // 2) * 2 * fold : (g // 2 + 1) * 2 * fold]
+                got = jnp.dot(two, v_ref[row, g], preferred_element_type=F32)
+                parts.append(got[(g % 2) * fold : (g % 2 + 1) * fold])
+            fresh_v = jnp.broadcast_to(
+                fv_ref[row].astype(F32)[:, None, :], (groups, fold, width)
+            ).reshape(heads, width)
+            mixed = jnp.concatenate(parts, axis=0) + probs_own * fresh_v
+            mixed_ref[pl.ds(pl.multiple_of(row * heads, heads), heads), :] = mixed
+        return carry
+
+    lax.fori_loop(0, steps, one_step, 0)
+    per_block = o_ref.shape[2] // width
+    for h in range(heads):
+        tile = jnp.concatenate(
+            [
+                mixed_ref[pl.ds(half * 8 * heads + h, 8, stride=heads), :]
+                for half in range(rows // 8)
+            ],
+            axis=0,
+        )
+        lane = (h % per_block) * width
+        o_ref[h // per_block, :, lane : lane + width] = tile.astype(BF16)
 
 
 def attend(queries, keys, values, fresh_key, fresh_value, lengths, blocks):
     rows, heads, width = queries.shape
-    groups, span = keys.shape[1], keys.shape[2]
-    body = lambda *refs: attend_kernel(*refs, groups=groups, fold=heads // groups, span=span)
-    cols = heads * width // blocks
-    return pl.pallas_call(
-        body,
+    vmem = pl.BlockSpec(memory_space=pltpu.VMEM)
+    far = pl.BlockSpec(memory_space=pl.ANY)
+    return pl.pallas_call(
+        attend_kernel,
         name="attend",
-        out_shape=jax.ShapeDtypeStruct((blocks, rows, cols), BF16),
-        grid_spec=pltpu.PrefetchScalarGridSpec(
-            num_scalar_prefetch=1,
-            grid=(rows // PER_STEP,),
-            in_specs=[
-                pl.BlockSpec((PER_STEP, heads, width), lambda i, _: (i, 0, 0)),
-                pl.BlockSpec((PER_STEP, groups, span, width), lambda i, _: (i, 0, 0, 0)),
-                pl.BlockSpec((PER_STEP, groups, span, width), lambda i, _: (i, 0, 0, 0)),
-                pl.BlockSpec((PER_STEP, groups, width), lambda i, _: (i, 0, 0)),
-                pl.BlockSpec((PER_STEP, groups, width), lambda i, _: (i, 0, 0)),
-            ],
-            out_specs=pl.BlockSpec((blocks, rows, cols), lambda i, _: (0, 0, 0)),
-            scratch_shapes=[pltpu.VMEM((rows * heads, width), F32)],
-        ),
-        compiler_params=pltpu.CompilerParams(vmem_limit_bytes=VMEM_BYTES),
+        out_shape=jax.ShapeDtypeStruct((blocks, rows, heads * width // blocks), BF16),
+        in_specs=[pl.BlockSpec(memory_space=pltpu.SMEM), vmem, far, far, vmem, vmem],
+        out_specs=vmem,
+        scratch_shapes=[
+            pltpu.VMEM(keys.shape, BF16),
+            pltpu.VMEM(values.shape, BF16),
+            pltpu.VMEM((rows * heads, width), F32),
+            pltpu.SemaphoreType.DMA((rows // AT_ONCE,)),
+            pltpu.SemaphoreType.DMA((rows // AT_ONCE,)),
+        ],
+        compiler_params=pltpu.CompilerParams(vmem_limit_bytes=FULL_VMEM),
         cost_estimate=pl.CostEstimate(
-            flops=4 * rows * heads * span * width,
-            bytes_accessed=4 * rows * groups * span * width,
-            transcendentals=rows * heads * span,
+            flops=4 * keys.size * heads // keys.shape[1],
+            bytes_accessed=4 * keys.size,
+            transcendentals=0,
         ),
     )(lengths, queries, keys, values, fresh_key, fresh_value)
 
@@ -154,40 +164,67 @@
     return [pl.BlockSpec(memory_space=pltpu.VMEM)] * count
 
 
-def project_kernel(order_ref, f_ref, w_ref, *refs):
-    outs, rows_ref = refs[:SIDE], refs[SIDE]
+TILES = 8
+
+
+def project_kernel(order_ref, f_ref, w_ref, own, ahead, back, ahead_last, back_last, *scratch):
+    rows_ref, out_ref, o_sem = scratch
     block = f_ref.shape[1]
-
-    @pl.when(pl.program_id(0) == 0)
-    def _():
-        for k in range(SIDE * SIDE):
-            rows_ref[k * block : (k + 1) * block, :] = f_ref[order_ref[k]]
-
-    product = jnp.dot(rows_ref[...], w_ref[...], preferred_element_type=F32).astype(BF16)
-    chunk = product.shape[0] // SIDE
-    for k in range(SIDE):
-        outs[k][...] = product[k * chunk : (k + 1) * chunk]
+    tile = w_ref.shape[1] // TILES
+    chunk = rows_ref.shape[0] // SIDE
+    half = TILES // 2
+
+    def departure(k, part):
+        low = k < half
+        to = (
+            own,
+            ahead_last if low else ahead,
+            ahead if low else back,
+            back if low else back_last,
+        )[part]
+        column = (k if to.shape[1] == tile * TILES else k % half) * tile
+        return pltpu.make_async_copy(
+            out_ref.at[k, pl.ds(part * chunk, chunk)],
+            to.at[:, pl.ds(column, tile)],
+            o_sem.at[k, part],
+        )
+
+    for k in range(SIDE * SIDE):
+        rows_ref[k * block : (k + 1) * block, :] = f_ref[order_ref[k]]
+    for k in range(TILES):
+        out_ref[k] = jnp.dot(
+            rows_ref[...], w_ref[:, k * tile : (k + 1) * tile], preferred_element_type=F32
+        ).astype(BF16)
+        for part in range(SIDE):
+            departure(k, part).start()
+    for k in range(TILES):
+        for part in range(SIDE):
+            departure(k, part).wait()
 
 
 def project(order, features, weight):
     blocks, rows, depth = features.shape
     cols = weight.shape[1]
-    tile = 1024
+    tile = cols // TILES
     chunk = blocks * rows // SIDE
+    far = pl.BlockSpec(memory_space=pl.ANY)
+    full = jax.ShapeDtypeStruct((chunk, cols), BF16)
+    part = jax.ShapeDtypeStruct((chunk, cols // 2), BF16)
     return pl.pallas_call(
         project_kernel,
         name="project",
-        out_shape=[jax.ShapeDtypeStruct((chunk, cols), BF16)] * SIDE,
-        grid_spec=pltpu.PrefetchScalarGridSpec(
-            num_scalar_prefetch=1,
-            grid=(cols // tile,),
-            in_specs=[
-                pl.BlockSpec((blocks, rows, depth), lambda i, _: (0, 0, 0)),
-                pl.BlockSpec((depth, tile), lambda i, _: (0, i)),
-            ],
-            out_specs=[pl.BlockSpec((chunk, tile), lambda i, _: (0, i))] * SIDE,
-            scratch_shapes=[pltpu.VMEM((blocks * rows, depth), BF16)],
-        ),
+        out_shape=[full, full, full, part, part],
+        in_specs=[
+            pl.BlockSpec(memory_space=pltpu.SMEM),
+            pl.BlockSpec(memory_space=pltpu.VMEM),
+            pl.BlockSpec(memory_space=pltpu.VMEM),
+        ],
+        out_specs=[far] * 5,
+        scratch_shapes=[
+            pltpu.VMEM((blocks * rows, depth), BF16),
+            pltpu.VMEM((TILES, blocks * rows, tile), BF16),
+            pltpu.SemaphoreType.DMA((TILES, SIDE)),
+        ],
         compiler_params=pltpu.CompilerParams(vmem_limit_bytes=VMEM_BYTES),
         cost_estimate=pl.CostEstimate(
             flops=2 * blocks * rows * depth * cols,
@@ -197,7 +234,53 @@
     )(order, features, weight)
 
 
-def dispatch_kernel(slot_ref, f_ref, *outs):
+def meet_kernel(ahead_last, back_last, came_ahead, came_back, ahead_ref, back_ref):
+    half = ahead_ref.shape[1]
+    ahead_ref[...] = (ahead_last[...].astype(F32) + came_ahead[:, :half].astype(F32)).astype(BF16)
+    back_ref[...] = (back_last[...].astype(F32) + came_back[:, half:].astype(F32)).astype(BF16)
+
+
+def meet(*operands):
+    return pl.pallas_call(
+        meet_kernel,
+        name="meet",
+        out_shape=[jax.ShapeDtypeStruct(operands[0].shape, BF16)] * 2,
+        in_specs=whole(4),
+        out_specs=whole(2),
+        compiler_params=pltpu.CompilerParams(vmem_limit_bytes=VMEM_BYTES),
+        cost_estimate=pl.CostEstimate(flops=2**20, bytes_accessed=2**22, transcendentals=0),
+    )(*operands)
+
+
+def join_kernel(own, came_ahead, came_back, ahead_last, back_last, *outs):
+    rows = outs[0].shape[0]
+    half = ahead_last.shape[1]
+    for k in range(SIDE):
+        at = slice(k * rows, (k + 1) * rows)
+        for right in range(2):
+            cols = slice(right * half, (right + 1) * half)
+            total = own[at, cols].astype(F32)
+            if right:
+                total = total + came_ahead[at, cols].astype(F32) + back_last[at].astype(F32)
+            else:
+                total = total + ahead_last[at].astype(F32) + came_back[at, cols].astype(F32)
+            outs[k][:, cols] = total.astype(BF16)
+
+
+def join(*operands):
+    rows, cols = operands[0].shape
+    return pl.pallas_call(
+        join_kernel,
+        name="join",
+        out_shape=[jax.ShapeDtypeStruct((rows // SIDE, cols), BF16)] * SIDE,
+        in_specs=whole(5),
+        out_specs=whole(SIDE),
+        compiler_params=pltpu.CompilerParams(vmem_limit_bytes=VMEM_BYTES),
+        cost_estimate=pl.CostEstimate(flops=2**20, bytes_accessed=2**22, transcendentals=0),
+    )(*operands)
+
+
+def dispatch_kernel(slot_ref, f_ref, _down, _up, *outs):
     count = outs[0].shape[0]
     rows = f_ref.shape[0]
     features = f_ref[...]
@@ -207,13 +290,13 @@
         outs[k][...] = jnp.dot(placing, features, preferred_element_type=F32).astype(BF16)
 
 
-def dispatch(slot, features, count):
+def dispatch(slot, features, count, down, up):
     rows, depth = features.shape
     return pl.pallas_call(
         dispatch_kernel,
         name="dispatch",
         out_shape=[jax.ShapeDtypeStruct((count, depth), BF16)] * SIDE,
-        in_specs=whole(2),
+        in_specs=whole(2) + [pl.BlockSpec(memory_space=pl.ANY)] * 2,
         out_specs=whole(SIDE),
         compiler_params=pltpu.CompilerParams(vmem_limit_bytes=VMEM_BYTES),
         cost_estimate=pl.CostEstimate(
@@ -221,7 +304,7 @@
             bytes_accessed=2 * (rows + SIDE * count) * depth,
             transcendentals=0,
         ),
-    )(slot.reshape(1, rows), features)
+    )(slot, features, down, up)
 
 
 QUAD = 4
@@ -309,15 +392,17 @@
     blocks, rows, cols = o_ref.shape
     total = jnp.zeros((blocks * rows, cols), F32)
     for k, ref in enumerate((r0, r1, r2, r3)):
-        slots = lax.broadcasted_iota(jnp.int32, (blocks * rows, count), 1) + k * count
+        slots = lax.broadcasted_iota(jnp.int32, (count, blocks * rows), 0) + k * count
         placing = (slots == slot_ref[...]).astype(F32).astype(BF16)
-        total = total + jnp.dot(placing, ref[...], preferred_element_type=F32)
+        total = total + lax.dot_general(
+            placing, ref[...], (((0,), (0,)), ((), ())), preferred_element_type=F32
+        )
     for t in range(blocks):
         o_ref[t] = total[t * rows : (t + 1) * rows].astype(BF16)
 
 
 def collect(slot, returned, blocks):
-    rows = slot.shape[0]
+    rows = slot.shape[1]
     cols = returned[0].shape[1]
     return pl.pallas_call(
         collect_kernel,
@@ -327,7 +412,7 @@
         out_specs=whole(1)[0],
         compiler_params=pltpu.CompilerParams(vmem_limit_bytes=VMEM_BYTES),
         cost_estimate=pl.CostEstimate(flops=2**28, bytes_accessed=2**21, transcendentals=0),
-    )(slot.reshape(rows, 1), *returned)
+    )(slot, *returned)
 
 
 def finish_kernel(skip_ref, s_ref, a_ref, b_ref, c_ref, delta_ref, o_ref):
@@ -335,7 +420,7 @@
     for t in range(blocks):
         at = slice(t * cols, (t + 1) * cols)
         base = (
-            s_ref[:, at]
+            s_ref[:, at].astype(F32)
             + a_ref[:, at].astype(F32)
             + b_ref[:, at].astype(F32)
             + c_ref[:, at].astype(F32)
@@ -346,12 +431,21 @@
 
 
 def finish(*operands):
+    rows_of = operands[0].shape
     return pl.pallas_call(
         finish_kernel,
         name="finish",
         out_shape=jax.ShapeDtypeStruct(operands[0].shape, BF16),
-        in_specs=whole(6),
-        out_specs=whole(1)[0],
+        grid=(1,),
+        in_specs=[
+            pl.BlockSpec(rows_of, lambda i: (0, 0)),
+            pl.BlockSpec(rows_of, lambda i: (0, 0)),
+            pl.BlockSpec(rows_of, lambda i: (0, 0)),
+            pl.BlockSpec(rows_of, lambda i: (0, 0)),
+            pl.BlockSpec(rows_of, lambda i: (0, 0)),
+            pl.BlockSpec(operands[5].shape, lambda i: (0, 0, 0)),
+        ],
+        out_specs=pl.BlockSpec(rows_of, lambda i: (0, 0)),
         compiler_params=pltpu.CompilerParams(vmem_limit_bytes=VMEM_BYTES),
         cost_estimate=pl.CostEstimate(flops=2**20, bytes_accessed=2**21, transcendentals=0),
     )(*operands)
@@ -397,7 +491,7 @@
         + ((owner % 2) ^ (rep % 2)) * (held * cap)
         + (adapter % held) * cap
         + ranked
-    )
+    ).reshape(1, rows)
     order = lax.dynamic_slice(jnp.asarray(row_order()), (rep * blocks + tp, 0), (1, blocks))[0]
 
     attended = attend(
@@ -406,24 +500,27 @@
     features = lax.all_to_all(attended, "tp", split_axis=0, concat_axis=0, tiled=True)
     flat = features.reshape(rows, depth)
 
-    placed = dispatch(slot, flat, per_z)
+    placed = dispatch(slot, flat, per_z, down_other, up_other)
     arrived = [placed[0]] + [pass_z(placed[k], k) for k in range(1, SIDE)]
 
-    partial = project(order, features, output_weight)
-    first = [pass_plane(partial[k], "xy", k) for k in range(1, SIDE)]
+    own, ahead, back, ahead_last, back_last = project(order, features, output_weight)
+    ahead, *arrived = lax.optimization_barrier((ahead, *arrived))
+    came_ahead, came_back = pass_plane(ahead, "xy", 1), pass_plane(back, "xy", -1)
 
     shrunk = shrink(arrived, down_own, down_other)
-    for axis in ("xx", "yy"):
-        shrunk = wide_sum(shrunk, *[pass_plane(shrunk, axis, k) for k in range(1, SIDE)]).astype(
-            BF16
-        )
+    near = [pass_plane(shrunk, "yx", k) for k in range(1, SIDE)]
+    shrunk = wide_sum(shrunk, *near).astype(BF16)
+    near = [pass_plane(shrunk, "xy", k) for k in range(1, SIDE)]
+    *near, ahead_last, back_last = lax.optimization_barrier((*near, ahead_last, back_last))
+    shrunk = wide_sum(shrunk, *near).astype(BF16)
+    ahead_last, back_last = meet(ahead_last, back_last, came_ahead, came_back)
+    ahead_last, back_last = pass_plane(ahead_last, "xy", 1), pass_plane(back_last, "xy", -1)
     grown = grow(shrunk, up_own, up_other, per_z)
     returned = [grown[0]] + [pass_z(grown[k], -k) for k in range(1, SIDE)]
     delta = collect(slot, returned, blocks)
 
-    summed = wide_sum(partial[0], *first).reshape(SIDE, rows // blocks, width)
-    narrow = summed.astype(BF16)
-    second = [pass_plane(narrow[k], "yx", k) for k in range(1, SIDE)]
+    summed = join(own, came_ahead, came_back, ahead_last, back_last)
+    second = [pass_plane(summed[k], "yx", k) for k in range(1, SIDE)]
     delta = lax.all_to_all(delta, "tp", split_axis=0, concat_axis=0, tiled=True)
     return finish(skip_stream, summed[0], *second, delta)
 

time: 126 us -> 96.8 us (0.77)
  the two profiles are of different devices: /device:TPU:1 before, /device:TPU:0 now
where the time goes in v2:
time: 96.8 us; the launch traced here: 96.5 us
  starting transfers between devices  32.6 us (34%)
  waiting for transfers between devices  25.8 us (27%)
  Pallas kernels  18.1 us (19%)
  blocking collectives  15.4 us (16%)
  local copies, waits for them, and re-layouts  4.1 us (4%)
    ppermute x13, waiting for transfers between devices, pass_plane(): return lax.ppermute(value, BOTH, pairs)  17.8 us
    all_to_all x1, blocking collectives, body(): delta = lax.all_to_all(delta, 'tp', split_axis=0, concat_axis=0, tiled=True)  15.4 us
    ppermute x13, starting transfers between devices, pass_plane(): return lax.ppermute(value, BOTH, pairs)  15.1 us
    ppermute x6, starting transfers between devices, pass_z(): return lax.ppermute(value, BOTH, pairs)  9.73 us
    pallas_call x1, Pallas kernels, attend(): pl.pallas_call(attend_kernel, name='attend', out_shape=jax.ShapeDtypeStru...  9.3 us
    all_to_all x1, waiting for transfers between devices, body(): lax.all_to_all(attended, 'tp', split_axis=0, concat_axis=0, tiled=True)  8 us
    all_to_all x1, starting transfers between devices, body(): lax.all_to_all(attended, 'tp', split_axis=0, concat_axis=0, tiled=True)  7.26 us
    pallas_call x1, Pallas kernels, project(): pl.pallas_call(project_kernel, name='project', out_shape=[full, full, ful...  5.26 us
  transfers between devices with their start and end apart: 22, of which 9 were waited for; matrix products, arithmetic and copies ran while one was open for 1% of the time, Pallas kernels for 17%

profile of v2, /device:TPU:0, one launch (start us, length us, event | category | flops | bytes accessed | tf_op | source)
XLA Modules:
  0.0 96.5 jit_solution(5112212337016578345)
XLA Ops:
  0.0 0.5 collective-permute-start.1
  0.5 9.3 %attend.1 = bf16[16,16,512]{2,1,0:T(8,128)(2,1)} custom-call(s32[16]{0:T(128)} %lengths_ref.1, bf16[16,64,128]{2,1,0:T(8,128)(2,1)} %q_ref.1, bf16[16,8,256,128]{3,2,1,0:T(8,128)(2,1)} %k_hbm.1, bf16[16,8,256,128]{3,2,1,0:T(8,128)(2,1)} %v_hbm.1, bf16[16,8,128]{2,1,0:T(8,128)(2,1)} %fk_ref.1, bf16[16,8,128]{2,1,0:T(8,128)(2,1)} %fv_ref.1), custom_call_target="tpu_custom_call" | custom-call | flops 134217728 | bytes 16777216 | tf_op jit(solution)/shard_map/attend/pallas_call | solution.py:141
  9.8 7.3 %all-to-all-start = ((bf16[16,16,512]{2,1,0:T(8,128)(2,1)}), bf16[16,16,512]{2,1,0:T(8,128)(2,1)S(1)}, u32[]{:S(2)}, u32[]{:S(2)}) async-start(bf16[16,16,512]{2,1,0:T(8,128)(2,1)} %attend.1), calls=%async_computation | async-start | bytes 524288 | tf_op jit(solution)/shard_map/all_to_all | solution.py:500
  17.3 0.7 dynamic-slice_bitcast_fusion.order_ref
  18.0 8.0 %all-to-all-done.f_ref = bf16[16,16,512]{2,1,0:T(8,128)(2,1)S(1)} async-done(((bf16[16,16,512]{2,1,0:T(8,128)(2,1)}), bf16[16,16,512]{2,1,0:T(8,128)(2,1)S(1)}, u32[]{:S(2)}, u32[]{:S(2)}) %all-to-all-start) | async-done | bytes 262176 | tf_op jit(solution)/shard_map/all_to_all | solution.py:500
  26.4 2.0 %collective-permute-start.2 = (bf16[128,512]{1,0:T(8,128)(2,1)S(1)}, bf16[128,512]{1,0:T(8,128)(2,1)S(1)}, u32[]{:S(2)}, u32[]{:S(2)}) collective-permute-start(bf16[128,512]{1,0:T(8,128)(2,1)S(1)} %get-tuple-element.37), channel_id=1, source_target_pairs={{0,32},{1,33},{2,34},{3,35},{4,36},{5,37},{6,38},{7,39},{8,40},{9,... | collective-permute-start | bytes 393224 | tf_op jit(solution)/shard_map/ppermute | solution.py:41
  28.3 3.6 %collective-permute-start.3 = (bf16[128,512]{1,0:T(8,128)(2,1)S(1)}, bf16[128,512]{1,0:T(8,128)(2,1)S(1)}, u32[]{:S(2)}, u32[]{:S(2)}) collective-permute-start(bf16[128,512]{1,0:T(8,128)(2,1)S(1)} %get-tuple-element.38), channel_id=1, source_target_pairs={{0,64},{1,65},{2,66},{3,67},{4,68},{5,69},{6,70},{7,71},{8,72},{9,... | collective-permute-start | bytes 393224 | tf_op jit(solution)/shard_map/ppermute | solution.py:41
  31.9 1.0 %collective-permute-start.4 = (bf16[128,512]{1,0:T(8,128)(2,1)S(1)}, bf16[128,512]{1,0:T(8,128)(2,1)S(1)}, u32[]{:S(2)}, u32[]{:S(2)}) collective-permute-start(bf16[128,512]{1,0:T(8,128)(2,1)S(1)} %get-tuple-element.39), channel_id=1, source_target_pairs={{0,96},{1,97},{2,98},{3,99},{4,100},{5,101},{6,102},{7,103},{8,104... | collective-permute-start | bytes 393224 | tf_op jit(solution)/shard_map/ppermute | solution.py:41
  32.9 3.4 %copy-done = bf16[512,8192]{1,0:T(8,128)(2,1)S(1)} copy-done((bf16[512,8192]{1,0:T(8,128)(2,1)S(1)}, bf16[512,8192]{1,0:T(8,128)(2,1)}, u32[]{:S(2)}) %copy-start) | copy-done | bytes 8388632
  36.3 5.3 %project.1 = (bf16[64,8192]{1,0:T(8,128)(2,1)S(1)}, bf16[64,8192]{1,0:T(8,128)(2,1)S(1)}, bf16[64,8192]{1,0:T(8,128)(2,1)S(1)}, bf16[64,4096]{1,0:T(8,128)(2,1)S(1)}, bf16[64,4096]{1,0:T(8,128)(2,1)S(1)}) custom-call(s32[16]{0:T(128)S(1)} %dynamic-slice_bitcast_fusion.order_ref, bf16[16,16,512]{2,1,0:T(8,128)(2,1)S(1)} %all-to-all-done.f_ref, ...), custom_call_target="tpu_custom_call" | custom-call | flops 2147483648 | bytes 12582912 | tf_op jit(solution)/shard_map/project/pallas_call | solution.py:213
  41.6 0.8 collective-permute-start.6
  42.4 1.3 %collective-permute-start.5 = (bf16[64,8192]{1,0:T(8,128)(2,1)S(1)}, bf16[64,8192]{1,0:T(8,128)(2,1)S(1)}, u32[]{:S(2)}, u32[]{:S(2)}) collective-permute-start(bf16[64,8192]{1,0:T(8,128)(2,1)S(1)} %get-tuple-element.40), channel_id=1, source_target_pairs={{0,1},{1,2},{2,3},{3,0},{4,5},{5,6},{6,7},{7,4},{8,9},{9,10},{10,1... | collective-permute-start | bytes 3145736 | tf_op jit(solution)/shard_map/ppermute | solution.py:36
  43.8 0.8 shrink.1
  44.5 0.9 collective-permute-start.9
  45.5 1.3 %collective-permute-start.8 = (bf16[256,128]{1,0:T(8,128)(2,1)S(1)}, bf16[256,128]{1,0:T(8,128)(2,1)S(1)}, u32[]{:S(2)}, u32[]{:S(2)}) collective-permute-start(bf16[256,128]{1,0:T(8,128)(2,1)S(1)} %shrink.1), channel_id=1, source_target_pairs={{0,8},{1,9},{2,10},{3,11},{4,12},{5,13},{6,14},{7,15},{8,0},{9,1},... | collective-permute-start | bytes 196616 | tf_op jit(solution)/shard_map/ppermute | solution.py:36
  46.9 2.8 %collective-permute-done.9 = bf16[256,128]{1,0:T(8,128)(2,1)S(1)} collective-permute-done((bf16[256,128]{1,0:T(8,128)(2,1)S(1)}, bf16[256,128]{1,0:T(8,128)(2,1)S(1)}, u32[]{:S(2)}, u32[]{:S(2)}) %collective-permute-start.9) | collective-permute-done | bytes 65568 | tf_op jit(solution)/shard_map/ppermute | solution.py:36
  49.6 2.4 %collective-permute-done.8 = bf16[256,128]{1,0:T(8,128)(2,1)S(1)} collective-permute-done((bf16[256,128]{1,0:T(8,128)(2,1)S(1)}, bf16[256,128]{1,0:T(8,128)(2,1)S(1)}, u32[]{:S(2)}, u32[]{:S(2)}) %collective-permute-start.8) | collective-permute-done | bytes 65568 | tf_op jit(solution)/shard_map/ppermute | solution.py:36
  52.0 1.2 %collective-permute-done.7 = bf16[256,128]{1,0:T(8,128)(2,1)S(1)} collective-permute-done((bf16[256,128]{1,0:T(8,128)(2,1)S(1)}, bf16[256,128]{1,0:T(8,128)(2,1)S(1)}, u32[]{:S(2)}, u32[]{:S(2)}) %collective-permute-start.7) | collective-permute-done | bytes 65568 | tf_op jit(solution)/shard_map/ppermute | solution.py:36
  53.3 2.4 %collective-permute-start.12 = (bf16[256,128]{1,0:T(8,128)(2,1)S(1)}, bf16[256,128]{1,0:T(8,128)(2,1)S(1)}, u32[]{:S(2)}, u32[]{:S(2)}) collective-permute-start(bf16[256,128]{1,0:T(8,128)(2,1)S(1)} %add_convert_fusion.1), channel_id=1, source_target_pairs={{0,3},{1,0},{2,1},{3,2},{4,7},{5,4},{6,5},{7,6},{8,11},{9,8},{10,9... | collective-permute-start | bytes 196616 | tf_op jit(solution)/shard_map/ppermute | solution.py:36
  55.8 0.8 collective-permute-start.10
  56.6 1.6 %collective-permute-done.12 = bf16[256,128]{1,0:T(8,128)(2,1)S(1)} collective-permute-done((bf16[256,128]{1,0:T(8,128)(2,1)S(1)}, bf16[256,128]{1,0:T(8,128)(2,1)S(1)}, u32[]{:S(2)}, u32[]{:S(2)}) %collective-permute-start.12) | collective-permute-done | bytes 65568 | tf_op jit(solution)/shard_map/ppermute | solution.py:36
  58.2 3.4 %collective-permute-done.11 = bf16[256,128]{1,0:T(8,128)(2,1)S(1)} collective-permute-done((bf16[256,128]{1,0:T(8,128)(2,1)S(1)}, bf16[256,128]{1,0:T(8,128)(2,1)S(1)}, u32[]{:S(2)}, u32[]{:S(2)}) %collective-permute-start.11) | collective-permute-done | bytes 65568 | tf_op jit(solution)/shard_map/ppermute | solution.py:36
  62.3 3.2 %collective-permute-start.14 = (bf16[64,4096]{1,0:T(8,128)(2,1)S(1)}, bf16[64,4096]{1,0:T(8,128)(2,1)S(1)}, u32[]{:S(2)}, u32[]{:S(2)}) collective-permute-start(bf16[64,4096]{1,0:T(8,128)(2,1)S(1)} %get-tuple-element.51), channel_id=1, source_target_pairs={{0,3},{1,0},{2,1},{3,2},{4,7},{5,4},{6,5},{7,6},{8,11},{9,8},{10,9... | collective-permute-start | bytes 1572872 | tf_op jit(solution)/shard_map/ppermute | solution.py:36
  65.6 0.5 grow.1
  66.1 3.1 %collective-permute-start.19 = (bf16[128,512]{1,0:T(8,128)(2,1)S(1)}, bf16[128,512]{1,0:T(8,128)(2,1)S(1)}, u32[]{:S(2)}, u32[]{:S(2)}) collective-permute-start(bf16[128,512]{1,0:T(8,128)(2,1)S(1)} %get-tuple-element.61), channel_id=1, source_target_pairs={{0,64},{1,65},{2,66},{3,67},{4,68},{5,69},{6,70},{7,71},{8,72},{9,... | collective-permute-start | bytes 393224 | tf_op jit(solution)/shard_map/ppermute | solution.py:41
  69.2 3.6 %collective-permute-done.13.ahead_last = bf16[64,4096]{1,0:T(8,128)(2,1)S(1)} collective-permute-done((bf16[64,4096]{1,0:T(8,128)(2,1)S(1)}, bf16[64,4096]{1,0:T(8,128)(2,1)S(1)}, u32[]{:S(2)}, u32[]{:S(2)}) %collective-permute-start.13) | collective-permute-done | bytes 524320 | tf_op jit(solution)/shard_map/ppermute | solution.py:36
  72.8 2.5 %collective-permute-done.14.back_last = bf16[64,4096]{1,0:T(8,128)(2,1)S(1)} collective-permute-done((bf16[64,4096]{1,0:T(8,128)(2,1)S(1)}, bf16[64,4096]{1,0:T(8,128)(2,1)S(1)}, u32[]{:S(2)}, u32[]{:S(2)}) %collective-permute-start.14) | collective-permute-done | bytes 524320 | tf_op jit(solution)/shard_map/ppermute | solution.py:36
  75.7 1.2 %collective-permute-start.15 = (bf16[16,8192]{1,0:T(8,128)(2,1)S(1)}, bf16[16,8192]{1,0:T(8,128)(2,1)S(1)}, u32[]{:S(2)}, u32[]{:S(2)}) collective-permute-start(bf16[16,8192]{1,0:T(8,128)(2,1)S(1)} %get-tuple-element.53), channel_id=1, source_target_pairs={{0,4},{1,5},{2,6},{3,7},{4,8},{5,9},{6,10},{7,11},{8,12},{9,13},{1... | collective-permute-start | bytes 786440 | tf_op jit(solution)/shard_map/ppermute | solution.py:36
  76.8 2.8 %collective-permute-start.17 = (bf16[16,8192]{1,0:T(8,128)(2,1)S(1)}, bf16[16,8192]{1,0:T(8,128)(2,1)S(1)}, u32[]{:S(2)}, u32[]{:S(2)}) collective-permute-start(bf16[16,8192]{1,0:T(8,128)(2,1)S(1)} %get-tuple-element.55), channel_id=1, source_target_pairs={{0,12},{1,13},{2,14},{3,15},{4,0},{5,1},{6,2},{7,3},{8,4},{9,5},{1... | collective-permute-start | bytes 786440 | tf_op jit(solution)/shard_map/ppermute | solution.py:36
  79.6 0.5 collect.1
  80.1 15.4 %all_to_all.10.delta_ref = bf16[16,16,512]{2,1,0:T(8,128)(2,1)S(1)} all-to-all(bf16[16,16,512]{2,1,0:T(8,128)(2,1)S(1)} %collect.1), channel_id=1, replica_groups=mesh['rep'=8,'tp'=16] {'tp'}, dimensions={0} | all-to-all | bytes 524288 | tf_op jit(solution)/shard_map/all_to_all | solution.py:524
  95.5 0.9 finish.1
  (37 shorter events, 2.2 us)
Async XLA Ops:
  0.0 26.0 %collective-permute-start = (bf16[1024,512]{1,0:T(8,128)(2,1)}, bf16[1024,512]{1,0:T(8,128)(2,1)S(1)}, u32[]{:S(2)}, u32[]{:S(2)}) collective-permute-start(bf16[1024,512]{1,0:T(8,128)(2,1)} %bitcast.27), channel_id=1, source_target_pairs={{0,16},{1,17},{2,18},{3,19},{4,20},{5,21},{6,22},{7,23},{8,24},{9,... | collective-permute-start | bytes 3145736 | tf_op jit(solution)/shard_map/ppermute | solution.py:45
  0.0 17.1 %copy-start.4 = (s32[256,1]{0,1:T(1,128)S(1)}, s32[256,1]{0,1:T(1,128)}, u32[]{:S(2)}) copy-start(s32[256,1]{0,1:T(1,128)} %param.18) | copy-start | bytes 3076
  0.0 26.0 %collective-permute-start.1 = (bf16[1024,512]{1,0:T(8,128)(2,1)}, bf16[1024,512]{1,0:T(8,128)(2,1)S(1)}, u32[]{:S(2)}, u32[]{:S(2)}) collective-permute-start(bf16[1024,512]{1,0:T(8,128)(2,1)} %bitcast.25), channel_id=1, source_target_pairs={{0,16},{1,17},{2,18},{3,19},{4,20},{5,21},{6,22},{7,23},{8,24},{9,... | collective-permute-start | bytes 3145736 | tf_op jit(solution)/shard_map/ppermute | solution.py:45
  9.8 34.0 %copy-start.2 = (bf16[16,512,64]{1,2,0:T(8,128)(2,1)S(1)}, bf16[16,512,64]{1,2,0:T(8,128)(2,1)}, u32[]{:S(2)}) copy-start(bf16[16,512,64]{1,2,0:T(8,128)(2,1)} %param.21) | copy-start | bytes 3145732
  9.8 16.2 %all-to-all-start = ((bf16[16,16,512]{2,1,0:T(8,128)(2,1)}), bf16[16,16,512]{2,1,0:T(8,128)(2,1)S(1)}, u32[]{:S(2)}, u32[]{:S(2)}) async-start(bf16[16,16,512]{2,1,0:T(8,128)(2,1)} %attend.1), calls=%async_computation | async-start | bytes 524288 | tf_op jit(solution)/shard_map/all_to_all | solution.py:500
  26.0 39.5 %copy-start.1 = (bf16[16,64,512]{2,1,0:T(8,128)(2,1)S(1)}, bf16[16,64,512]{2,1,0:T(8,128)(2,1)}, u32[]{:S(2)}) copy-start(bf16[16,64,512]{2,1,0:T(8,128)(2,1)} %param.22) | copy-start | bytes 3145732
  26.4 16.1 %collective-permute-start.2 = (bf16[128,512]{1,0:T(8,128)(2,1)S(1)}, bf16[128,512]{1,0:T(8,128)(2,1)S(1)}, u32[]{:S(2)}, u32[]{:S(2)}) collective-permute-start(bf16[128,512]{1,0:T(8,128)(2,1)S(1)} %get-tuple-element.37), channel_id=1, source_target_pairs={{0,32},{1,33},{2,34},{3,35},{4,36},{5,37},{6,38},{7,39},{8,40},{9,... | collective-permute-start | bytes 393224 | tf_op jit(solution)/shard_map/ppermute | solution.py:41
  28.3 14.1 %collective-permute-start.3 = (bf16[128,512]{1,0:T(8,128)(2,1)S(1)}, bf16[128,512]{1,0:T(8,128)(2,1)S(1)}, u32[]{:S(2)}, u32[]{:S(2)}) collective-permute-start(bf16[128,512]{1,0:T(8,128)(2,1)S(1)} %get-tuple-element.38), channel_id=1, source_target_pairs={{0,64},{1,65},{2,66},{3,67},{4,68},{5,69},{6,70},{7,71},{8,72},{9,... | collective-permute-start | bytes 393224 | tf_op jit(solution)/shard_map/ppermute | solution.py:41
  31.9 10.5 %collective-permute-start.4 = (bf16[128,512]{1,0:T(8,128)(2,1)S(1)}, bf16[128,512]{1,0:T(8,128)(2,1)S(1)}, u32[]{:S(2)}, u32[]{:S(2)}) collective-permute-start(bf16[128,512]{1,0:T(8,128)(2,1)S(1)} %get-tuple-element.39), channel_id=1, source_target_pairs={{0,96},{1,97},{2,98},{3,99},{4,100},{5,101},{6,102},{7,103},{8,104... | collective-permute-start | bytes 393224 | tf_op jit(solution)/shard_map/ppermute | solution.py:41
  32.9 3.4 %copy-start = (bf16[512,8192]{1,0:T(8,128)(2,1)S(1)}, bf16[512,8192]{1,0:T(8,128)(2,1)}, u32[]{:S(2)}) copy-start(bf16[512,8192]{1,0:T(8,128)(2,1)} %w_ref.1) | copy-start | bytes 25165828
  41.6 53.9 %copy-start.3 = (bf16[16,8192]{1,0:T(8,128)(2,1)S(1)}, bf16[16,8192]{1,0:T(8,128)(2,1)}, u32[]{:S(2)}) copy-start(bf16[16,8192]{1,0:T(8,128)(2,1)} %skip_ref.1) | copy-start | bytes 786436
  41.6 20.4 %collective-permute-start.6 = (bf16[64,8192]{1,0:T(8,128)(2,1)S(1)}, bf16[64,8192]{1,0:T(8,128)(2,1)S(1)}, u32[]{:S(2)}, u32[]{:S(2)}) collective-permute-start(bf16[64,8192]{1,0:T(8,128)(2,1)S(1)} %get-tuple-element.41), channel_id=1, source_target_pairs={{0,3},{1,0},{2,1},{3,2},{4,7},{5,4},{6,5},{7,6},{8,11},{9,8},{10,9... | collective-permute-start | bytes 3145736 | tf_op jit(solution)/shard_map/ppermute | solution.py:36
  42.4 19.5 %collective-permute-start.5 = (bf16[64,8192]{1,0:T(8,128)(2,1)S(1)}, bf16[64,8192]{1,0:T(8,128)(2,1)S(1)}, u32[]{:S(2)}, u32[]{:S(2)}) collective-permute-start(bf16[64,8192]{1,0:T(8,128)(2,1)S(1)} %get-tuple-element.40), channel_id=1, source_target_pairs={{0,1},{1,2},{2,3},{3,0},{4,5},{5,6},{6,7},{7,4},{8,9},{9,10},{10,1... | collective-permute-start | bytes 3145736 | tf_op jit(solution)/shard_map/ppermute | solution.py:36
  44.5 5.1 %collective-permute-start.9 = (bf16[256,128]{1,0:T(8,128)(2,1)S(1)}, bf16[256,128]{1,0:T(8,128)(2,1)S(1)}, u32[]{:S(2)}, u32[]{:S(2)}) collective-permute-start(bf16[256,128]{1,0:T(8,128)(2,1)S(1)} %shrink.1), channel_id=1, source_target_pairs={{0,12},{1,13},{2,14},{3,15},{4,0},{5,1},{6,2},{7,3},{8,4},{9,5},{1... | collective-permute-start | bytes 196616 | tf_op jit(solution)/shard_map/ppermute | solution.py:36
  45.5 6.5 %collective-permute-start.8 = (bf16[256,128]{1,0:T(8,128)(2,1)S(1)}, bf16[256,128]{1,0:T(8,128)(2,1)S(1)}, u32[]{:S(2)}, u32[]{:S(2)}) collective-permute-start(bf16[256,128]{1,0:T(8,128)(2,1)S(1)} %shrink.1), channel_id=1, source_target_pairs={{0,8},{1,9},{2,10},{3,11},{4,12},{5,13},{6,14},{7,15},{8,0},{9,1},... | collective-permute-start | bytes 196616 | tf_op jit(solution)/shard_map/ppermute | solution.py:36
  46.7 6.5 %collective-permute-start.7 = (bf16[256,128]{1,0:T(8,128)(2,1)S(1)}, bf16[256,128]{1,0:T(8,128)(2,1)S(1)}, u32[]{:S(2)}, u32[]{:S(2)}) collective-permute-start(bf16[256,128]{1,0:T(8,128)(2,1)S(1)} %shrink.1), channel_id=1, source_target_pairs={{0,4},{1,5},{2,6},{3,7},{4,8},{5,9},{6,10},{7,11},{8,12},{9,13},{1... | collective-permute-start | bytes 196616 | tf_op jit(solution)/shard_map/ppermute | solution.py:36
  53.3 4.9 %collective-permute-start.12 = (bf16[256,128]{1,0:T(8,128)(2,1)S(1)}, bf16[256,128]{1,0:T(8,128)(2,1)S(1)}, u32[]{:S(2)}, u32[]{:S(2)}) collective-permute-start(bf16[256,128]{1,0:T(8,128)(2,1)S(1)} %add_convert_fusion.1), channel_id=1, source_target_pairs={{0,3},{1,0},{2,1},{3,2},{4,7},{5,4},{6,5},{7,6},{8,11},{9,8},{10,9... | collective-permute-start | bytes 196616 | tf_op jit(solution)/shard_map/ppermute | solution.py:36
  55.6 5.9 %collective-permute-start.11 = (bf16[256,128]{1,0:T(8,128)(2,1)S(1)}, bf16[256,128]{1,0:T(8,128)(2,1)S(1)}, u32[]{:S(2)}, u32[]{:S(2)}) collective-permute-start(bf16[256,128]{1,0:T(8,128)(2,1)S(1)} %add_convert_fusion.1), channel_id=1, source_target_pairs={{0,2},{1,3},{2,0},{3,1},{4,6},{5,7},{6,4},{7,5},{8,10},{9,11},{10,... | collective-permute-start | bytes 196616 | tf_op jit(solution)/shard_map/ppermute | solution.py:36
  55.8 6.2 %collective-permute-start.10 = (bf16[256,128]{1,0:T(8,128)(2,1)S(1)}, bf16[256,128]{1,0:T(8,128)(2,1)S(1)}, u32[]{:S(2)}, u32[]{:S(2)}) collective-permute-start(bf16[256,128]{1,0:T(8,128)(2,1)S(1)} %add_convert_fusion.1), channel_id=1, source_target_pairs={{0,1},{1,2},{2,3},{3,0},{4,5},{5,6},{6,7},{7,4},{8,9},{9,10},{10,1... | collective-permute-start | bytes 196616 | tf_op jit(solution)/shard_map/ppermute | solution.py:36
  62.2 10.6 %collective-permute-start.13 = (bf16[64,4096]{1,0:T(8,128)(2,1)S(1)}, bf16[64,4096]{1,0:T(8,128)(2,1)S(1)}, u32[]{:S(2)}, u32[]{:S(2)}) collective-permute-start(bf16[64,4096]{1,0:T(8,128)(2,1)S(1)} %get-tuple-element.50), channel_id=1, source_target_pairs={{0,1},{1,2},{2,3},{3,0},{4,5},{5,6},{6,7},{7,4},{8,9},{9,10},{10,1... | collective-permute-start | bytes 1572872 | tf_op jit(solution)/shard_map/ppermute | solution.py:36
  62.3 13.0 %collective-permute-start.14 = (bf16[64,4096]{1,0:T(8,128)(2,1)S(1)}, bf16[64,4096]{1,0:T(8,128)(2,1)S(1)}, u32[]{:S(2)}, u32[]{:S(2)}) collective-permute-start(bf16[64,4096]{1,0:T(8,128)(2,1)S(1)} %get-tuple-element.51), channel_id=1, source_target_pairs={{0,3},{1,0},{2,1},{3,2},{4,7},{5,4},{6,5},{7,6},{8,11},{9,8},{10,9... | collective-permute-start | bytes 1572872 | tf_op jit(solution)/shard_map/ppermute | solution.py:36
  66.1 10.8 %collective-permute-start.18 = (bf16[128,512]{1,0:T(8,128)(2,1)S(1)}, bf16[128,512]{1,0:T(8,128)(2,1)S(1)}, u32[]{:S(2)}, u32[]{:S(2)}) collective-permute-start(bf16[128,512]{1,0:T(8,128)(2,1)S(1)} %get-tuple-element.60), channel_id=1, source_target_pairs={{0,96},{1,97},{2,98},{3,99},{4,100},{5,101},{6,102},{7,103},{8,104... | collective-permute-start | bytes 393224 | tf_op jit(solution)/shard_map/ppermute | solution.py:41
  66.1 13.5 %collective-permute-start.19 = (bf16[128,512]{1,0:T(8,128)(2,1)S(1)}, bf16[128,512]{1,0:T(8,128)(2,1)S(1)}, u32[]{:S(2)}, u32[]{:S(2)}) collective-permute-start(bf16[128,512]{1,0:T(8,128)(2,1)S(1)} %get-tuple-element.61), channel_id=1, source_target_pairs={{0,64},{1,65},{2,66},{3,67},{4,68},{5,69},{6,70},{7,71},{8,72},{9,... | collective-permute-start | bytes 393224 | tf_op jit(solution)/shard_map/ppermute | solution.py:41
  69.2 10.4 %collective-permute-start.20 = (bf16[128,512]{1,0:T(8,128)(2,1)S(1)}, bf16[128,512]{1,0:T(8,128)(2,1)S(1)}, u32[]{:S(2)}, u32[]{:S(2)}) collective-permute-start(bf16[128,512]{1,0:T(8,128)(2,1)S(1)} %get-tuple-element.62), channel_id=1, source_target_pairs={{0,32},{1,33},{2,34},{3,35},{4,36},{5,37},{6,38},{7,39},{8,40},{9,... | collective-permute-start | bytes 393224 | tf_op jit(solution)/shard_map/ppermute | solution.py:41
  75.7 19.9 %collective-permute-start.15 = (bf16[16,8192]{1,0:T(8,128)(2,1)S(1)}, bf16[16,8192]{1,0:T(8,128)(2,1)S(1)}, u32[]{:S(2)}, u32[]{:S(2)}) collective-permute-start(bf16[16,8192]{1,0:T(8,128)(2,1)S(1)} %get-tuple-element.53), channel_id=1, source_target_pairs={{0,4},{1,5},{2,6},{3,7},{4,8},{5,9},{6,10},{7,11},{8,12},{9,13},{1... | collective-permute-start | bytes 786440 | tf_op jit(solution)/shard_map/ppermute | solution.py:36
  76.8 18.7 %collective-permute-start.16 = (bf16[16,8192]{1,0:T(8,128)(2,1)S(1)}, bf16[16,8192]{1,0:T(8,128)(2,1)S(1)}, u32[]{:S(2)}, u32[]{:S(2)}) collective-permute-start(bf16[16,8192]{1,0:T(8,128)(2,1)S(1)} %get-tuple-element.54), channel_id=1, source_target_pairs={{0,8},{1,9},{2,10},{3,11},{4,12},{5,13},{6,14},{7,15},{8,0},{9,1},... | collective-permute-start | bytes 786440 | tf_op jit(solution)/shard_map/ppermute | solution.py:36
  76.8 18.7 %collective-permute-start.17 = (bf16[16,8192]{1,0:T(8,128)(2,1)S(1)}, bf16[16,8192]{1,0:T(8,128)(2,1)S(1)}, u32[]{:S(2)}, u32[]{:S(2)}) collective-permute-start(bf16[16,8192]{1,0:T(8,128)(2,1)S(1)} %get-tuple-element.55), channel_id=1, source_target_pairs={{0,12},{1,13},{2,14},{3,15},{4,0},{5,1},{6,2},{7,3},{8,4},{9,5},{1... | collective-permute-start | bytes 786440 | tf_op jit(solution)/shard_map/ppermute | solution.py:36

commit v3 on v2

--- a/solution.py
+++ b/solution.py
@@ -520,6 +520,7 @@
     delta = collect(slot, returned, blocks)
 
     summed = join(own, came_ahead, came_back, ahead_last, back_last)
+    *summed, delta = lax.optimization_barrier((*summed, delta))
     second = [pass_plane(summed[k], "yx", k) for k in range(1, SIDE)]
     delta = lax.all_to_all(delta, "tp", split_axis=0, concat_axis=0, tiled=True)
     return finish(skip_stream, summed[0], *second, delta)

time: 96.8 us -> 93.6 us (0.967)
  blocking collectives: 15.4 us -> 12.2 us
    ppermute x6, waiting for transfers between devices: 0.02 us -> 6.18 us  [pass_z(): return lax.ppermute(value, BOTH, pairs)]
    ppermute x13, waiting for transfers between devices: 17.8 us -> 11.7 us  [pass_plane(): return lax.ppermute(value, BOTH, pairs)]
    all_to_all x1, blocking collectives: 15.4 us -> 12.2 us  [body(): delta = lax.all_to_all(delta, 'tp', split_axis=0, concat_axis=0, tiled=True)]
  transfers between devices with their start and end apart: 22 -> 22, of which waited for: 9 -> 10; matrix products, arithmetic and copies ran while one was open for 1% -> 1% of each run, Pallas kernels for 17% -> 17%
where the time goes in v3:
time: 93.6 us; the launch traced here: 93.3 us
  starting transfers between devices  32.5 us (35%)
  waiting for transfers between devices  25.9 us (28%)
  Pallas kernels  18.1 us (19%)
  blocking collectives  12.2 us (13%)
  local copies, waits for them, and re-layouts  4.1 us (4%)
    ppermute x13, starting transfers between devices, pass_plane(): return lax.ppermute(value, BOTH, pairs)  15 us
    all_to_all x1, blocking collectives, body(): delta = lax.all_to_all(delta, 'tp', split_axis=0, concat_axis=0, tiled=True)  12.2 us
    ppermute x13, waiting for transfers between devices, pass_plane(): return lax.ppermute(value, BOTH, pairs)  11.7 us
    ppermute x6, starting transfers between devices, pass_z(): return lax.ppermute(value, BOTH, pairs)  9.73 us
    pallas_call x1, Pallas kernels, attend(): pl.pallas_call(attend_kernel, name='attend', out_shape=jax.ShapeDtypeStru...  9.3 us
    all_to_all x1, waiting for transfers between devices, body(): lax.all_to_all(attended, 'tp', split_axis=0, concat_axis=0, tiled=True)  8 us
    all_to_all x1, starting transfers between devices, body(): lax.all_to_all(attended, 'tp', split_axis=0, concat_axis=0, tiled=True)  7.26 us
    ppermute x6, waiting for transfers between devices, pass_z(): return lax.ppermute(value, BOTH, pairs)  6.18 us
  transfers between devices with their start and end apart: 22, of which 10 were waited for; matrix products, arithmetic and copies ran while one was open for 1% of the time, Pallas kernels for 17%

profile of v3, /device:TPU:0, one launch (start us, length us, event | category | flops | bytes accessed | tf_op | source)
XLA Modules:
  0.0 93.3 jit_solution(18268137778373519972)
XLA Ops:
  0.0 0.5 collective-permute-start.1
  0.5 9.3 %attend.1 = bf16[16,16,512]{2,1,0:T(8,128)(2,1)} custom-call(s32[16]{0:T(128)} %lengths_ref.1, bf16[16,64,128]{2,1,0:T(8,128)(2,1)} %q_ref.1, bf16[16,8,256,128]{3,2,1,0:T(8,128)(2,1)} %k_hbm.1, bf16[16,8,256,128]{3,2,1,0:T(8,128)(2,1)} %v_hbm.1, bf16[16,8,128]{2,1,0:T(8,128)(2,1)} %fk_ref.1, bf16[16,8,128]{2,1,0:T(8,128)(2,1)} %fv_ref.1), custom_call_target="tpu_custom_call" | custom-call | flops 134217728 | bytes 16777216 | tf_op jit(solution)/shard_map/attend/pallas_call | solution.py:141
  9.8 7.3 %all-to-all-start = ((bf16[16,16,512]{2,1,0:T(8,128)(2,1)}), bf16[16,16,512]{2,1,0:T(8,128)(2,1)S(1)}, u32[]{:S(2)}, u32[]{:S(2)}) async-start(bf16[16,16,512]{2,1,0:T(8,128)(2,1)} %attend.1), calls=%async_computation | async-start | bytes 524288 | tf_op jit(solution)/shard_map/all_to_all | solution.py:500
  17.3 0.7 dynamic-slice_bitcast_fusion.order_ref
  18.0 8.0 %all-to-all-done.f_ref = bf16[16,16,512]{2,1,0:T(8,128)(2,1)S(1)} async-done(((bf16[16,16,512]{2,1,0:T(8,128)(2,1)}), bf16[16,16,512]{2,1,0:T(8,128)(2,1)S(1)}, u32[]{:S(2)}, u32[]{:S(2)}) %all-to-all-start) | async-done | bytes 262176 | tf_op jit(solution)/shard_map/all_to_all | solution.py:500
  26.4 2.0 %collective-permute-start.2 = (bf16[128,512]{1,0:T(8,128)(2,1)S(1)}, bf16[128,512]{1,0:T(8,128)(2,1)S(1)}, u32[]{:S(2)}, u32[]{:S(2)}) collective-permute-start(bf16[128,512]{1,0:T(8,128)(2,1)S(1)} %get-tuple-element.42), channel_id=1, source_target_pairs={{0,32},{1,33},{2,34},{3,35},{4,36},{5,37},{6,38},{7,39},{8,40},{9,... | collective-permute-start | bytes 393224 | tf_op jit(solution)/shard_map/ppermute | solution.py:41
  28.3 3.6 %collective-permute-start.3 = (bf16[128,512]{1,0:T(8,128)(2,1)S(1)}, bf16[128,512]{1,0:T(8,128)(2,1)S(1)}, u32[]{:S(2)}, u32[]{:S(2)}) collective-permute-start(bf16[128,512]{1,0:T(8,128)(2,1)S(1)} %get-tuple-element.43), channel_id=1, source_target_pairs={{0,64},{1,65},{2,66},{3,67},{4,68},{5,69},{6,70},{7,71},{8,72},{9,... | collective-permute-start | bytes 393224 | tf_op jit(solution)/shard_map/ppermute | solution.py:41
  31.9 1.0 %collective-permute-start.4 = (bf16[128,512]{1,0:T(8,128)(2,1)S(1)}, bf16[128,512]{1,0:T(8,128)(2,1)S(1)}, u32[]{:S(2)}, u32[]{:S(2)}) collective-permute-start(bf16[128,512]{1,0:T(8,128)(2,1)S(1)} %get-tuple-element.44), channel_id=1, source_target_pairs={{0,96},{1,97},{2,98},{3,99},{4,100},{5,101},{6,102},{7,103},{8,104... | collective-permute-start | bytes 393224 | tf_op jit(solution)/shard_map/ppermute | solution.py:41
  32.9 3.4 %copy-done = bf16[512,8192]{1,0:T(8,128)(2,1)S(1)} copy-done((bf16[512,8192]{1,0:T(8,128)(2,1)S(1)}, bf16[512,8192]{1,0:T(8,128)(2,1)}, u32[]{:S(2)}) %copy-start) | copy-done | bytes 8388632
  36.3 5.3 %project.1 = (bf16[64,8192]{1,0:T(8,128)(2,1)S(1)}, bf16[64,8192]{1,0:T(8,128)(2,1)S(1)}, bf16[64,8192]{1,0:T(8,128)(2,1)S(1)}, bf16[64,4096]{1,0:T(8,128)(2,1)S(1)}, bf16[64,4096]{1,0:T(8,128)(2,1)S(1)}) custom-call(s32[16]{0:T(128)S(1)} %dynamic-slice_bitcast_fusion.order_ref, bf16[16,16,512]{2,1,0:T(8,128)(2,1)S(1)} %all-to-all-done.f_ref, ...), custom_call_target="tpu_custom_call" | custom-call | flops 2147483648 | bytes 12582912 | tf_op jit(solution)/shard_map/project/pallas_call | solution.py:213
  41.6 0.8 collective-permute-start.6
  42.4 1.3 %collective-permute-start.5 = (bf16[64,8192]{1,0:T(8,128)(2,1)S(1)}, bf16[64,8192]{1,0:T(8,128)(2,1)S(1)}, u32[]{:S(2)}, u32[]{:S(2)}) collective-permute-start(bf16[64,8192]{1,0:T(8,128)(2,1)S(1)} %get-tuple-element.45), channel_id=1, source_target_pairs={{0,1},{1,2},{2,3},{3,0},{4,5},{5,6},{6,7},{7,4},{8,9},{9,10},{10,1... | collective-permute-start | bytes 3145736 | tf_op jit(solution)/shard_map/ppermute | solution.py:36
  43.8 0.7 shrink.1
  44.5 0.9 collective-permute-start.9
  45.5 1.3 %collective-permute-start.8 = (bf16[256,128]{1,0:T(8,128)(2,1)S(1)}, bf16[256,128]{1,0:T(8,128)(2,1)S(1)}, u32[]{:S(2)}, u32[]{:S(2)}) collective-permute-start(bf16[256,128]{1,0:T(8,128)(2,1)S(1)} %shrink.1), channel_id=1, source_target_pairs={{0,8},{1,9},{2,10},{3,11},{4,12},{5,13},{6,14},{7,15},{8,0},{9,1},... | collective-permute-start | bytes 196616 | tf_op jit(solution)/shard_map/ppermute | solution.py:36
  46.9 2.8 %collective-permute-done.9 = bf16[256,128]{1,0:T(8,128)(2,1)S(1)} collective-permute-done((bf16[256,128]{1,0:T(8,128)(2,1)S(1)}, bf16[256,128]{1,0:T(8,128)(2,1)S(1)}, u32[]{:S(2)}, u32[]{:S(2)}) %collective-permute-start.9) | collective-permute-done | bytes 65568 | tf_op jit(solution)/shard_map/ppermute | solution.py:36
  49.6 2.4 %collective-permute-done.8 = bf16[256,128]{1,0:T(8,128)(2,1)S(1)} collective-permute-done((bf16[256,128]{1,0:T(8,128)(2,1)S(1)}, bf16[256,128]{1,0:T(8,128)(2,1)S(1)}, u32[]{:S(2)}, u32[]{:S(2)}) %collective-permute-start.8) | collective-permute-done | bytes 65568 | tf_op jit(solution)/shard_map/ppermute | solution.py:36
  52.0 1.2 %collective-permute-done.7 = bf16[256,128]{1,0:T(8,128)(2,1)S(1)} collective-permute-done((bf16[256,128]{1,0:T(8,128)(2,1)S(1)}, bf16[256,128]{1,0:T(8,128)(2,1)S(1)}, u32[]{:S(2)}, u32[]{:S(2)}) %collective-permute-start.7) | collective-permute-done | bytes 65568 | tf_op jit(solution)/shard_map/ppermute | solution.py:36
  53.2 2.4 %collective-permute-start.12 = (bf16[256,128]{1,0:T(8,128)(2,1)S(1)}, bf16[256,128]{1,0:T(8,128)(2,1)S(1)}, u32[]{:S(2)}, u32[]{:S(2)}) collective-permute-start(bf16[256,128]{1,0:T(8,128)(2,1)S(1)} %add_convert_fusion.1), channel_id=1, source_target_pairs={{0,3},{1,0},{2,1},{3,2},{4,7},{5,4},{6,5},{7,6},{8,11},{9,8},{10,9... | collective-permute-start | bytes 196616 | tf_op jit(solution)/shard_map/ppermute | solution.py:36
  55.8 0.8 collective-permute-start.10
  56.6 1.6 %collective-permute-done.12 = bf16[256,128]{1,0:T(8,128)(2,1)S(1)} collective-permute-done((bf16[256,128]{1,0:T(8,128)(2,1)S(1)}, bf16[256,128]{1,0:T(8,128)(2,1)S(1)}, u32[]{:S(2)}, u32[]{:S(2)}) %collective-permute-start.12) | collective-permute-done | bytes 65568 | tf_op jit(solution)/shard_map/ppermute | solution.py:36
  58.1 3.4 %collective-permute-done.11 = bf16[256,128]{1,0:T(8,128)(2,1)S(1)} collective-permute-done((bf16[256,128]{1,0:T(8,128)(2,1)S(1)}, bf16[256,128]{1,0:T(8,128)(2,1)S(1)}, u32[]{:S(2)}, u32[]{:S(2)}) %collective-permute-start.11) | collective-permute-done | bytes 65568 | tf_op jit(solution)/shard_map/ppermute | solution.py:36
  62.3 3.2 %collective-permute-start.14 = (bf16[64,4096]{1,0:T(8,128)(2,1)S(1)}, bf16[64,4096]{1,0:T(8,128)(2,1)S(1)}, u32[]{:S(2)}, u32[]{:S(2)}) collective-permute-start(bf16[64,4096]{1,0:T(8,128)(2,1)S(1)} %get-tuple-element.56), channel_id=1, source_target_pairs={{0,3},{1,0},{2,1},{3,2},{4,7},{5,4},{6,5},{7,6},{8,11},{9,8},{10,9... | collective-permute-start | bytes 1572872 | tf_op jit(solution)/shard_map/ppermute | solution.py:36
  65.6 0.5 grow.1
  66.1 3.1 %collective-permute-start.16 = (bf16[128,512]{1,0:T(8,128)(2,1)S(1)}, bf16[128,512]{1,0:T(8,128)(2,1)S(1)}, u32[]{:S(2)}, u32[]{:S(2)}) collective-permute-start(bf16[128,512]{1,0:T(8,128)(2,1)S(1)} %get-tuple-element.66), channel_id=1, source_target_pairs={{0,64},{1,65},{2,66},{3,67},{4,68},{5,69},{6,70},{7,71},{8,72},{9,... | collective-permute-start | bytes 393224 | tf_op jit(solution)/shard_map/ppermute | solution.py:41
  69.2 1.9 %collective-permute-done.15.r1 = bf16[128,512]{1,0:T(8,128)(2,1)S(1)} collective-permute-done((bf16[128,512]{1,0:T(8,128)(2,1)S(1)}, bf16[128,512]{1,0:T(8,128)(2,1)S(1)}, u32[]{:S(2)}, u32[]{:S(2)}) %collective-permute-start.15) | collective-permute-done | bytes 131104 | tf_op jit(solution)/shard_map/ppermute | solution.py:41
  71.1 1.6 %collective-permute-done.16.r2 = bf16[128,512]{1,0:T(8,128)(2,1)S(1)} collective-permute-done((bf16[128,512]{1,0:T(8,128)(2,1)S(1)}, bf16[128,512]{1,0:T(8,128)(2,1)S(1)}, u32[]{:S(2)}, u32[]{:S(2)}) %collective-permute-start.16) | collective-permute-done | bytes 131104 | tf_op jit(solution)/shard_map/ppermute | solution.py:41
  72.7 2.7 %collective-permute-done.17.r3 = bf16[128,512]{1,0:T(8,128)(2,1)S(1)} collective-permute-done((bf16[128,512]{1,0:T(8,128)(2,1)S(1)}, bf16[128,512]{1,0:T(8,128)(2,1)S(1)}, u32[]{:S(2)}, u32[]{:S(2)}) %collective-permute-start.17) | collective-permute-done | bytes 131104 | tf_op jit(solution)/shard_map/ppermute | solution.py:41
  76.5 2.3 %collective-permute-start.19 = (bf16[16,8192]{1,0:T(8,128)(2,1)S(1)}, bf16[16,8192]{1,0:T(8,128)(2,1)S(1)}, u32[]{:S(2)}, u32[]{:S(2)}) collective-permute-start(bf16[16,8192]{1,0:T(8,128)(2,1)S(1)} %get-tuple-element.70), channel_id=1, source_target_pairs={{0,8},{1,9},{2,10},{3,11},{4,12},{5,13},{6,14},{7,15},{8,0},{9,1},... | collective-permute-start | bytes 786440 | tf_op jit(solution)/shard_map/ppermute | solution.py:36
  78.7 1.4 %collective-permute-start.20 = (bf16[16,8192]{1,0:T(8,128)(2,1)S(1)}, bf16[16,8192]{1,0:T(8,128)(2,1)S(1)}, u32[]{:S(2)}, u32[]{:S(2)}) collective-permute-start(bf16[16,8192]{1,0:T(8,128)(2,1)S(1)} %get-tuple-element.71), channel_id=1, source_target_pairs={{0,12},{1,13},{2,14},{3,15},{4,0},{5,1},{6,2},{7,3},{8,4},{9,5},{1... | collective-permute-start | bytes 786440 | tf_op jit(solution)/shard_map/ppermute | solution.py:36
  80.1 12.2 %all_to_all.10.delta_ref = bf16[16,16,512]{2,1,0:T(8,128)(2,1)S(1)} all-to-all(bf16[16,16,512]{2,1,0:T(8,128)(2,1)S(1)} %collect.1), channel_id=1, replica_groups=mesh['rep'=8,'tp'=16] {'tp'}, dimensions={0} | all-to-all | bytes 524288 | tf_op jit(solution)/shard_map/all_to_all | solution.py:525
  92.4 0.9 finish.1
  (37 shorter events, 2.8 us)
Async XLA Ops:
  0.0 26.0 %collective-permute-start = (bf16[1024,512]{1,0:T(8,128)(2,1)}, bf16[1024,512]{1,0:T(8,128)(2,1)S(1)}, u32[]{:S(2)}, u32[]{:S(2)}) collective-permute-start(bf16[1024,512]{1,0:T(8,128)(2,1)} %bitcast.27), channel_id=1, source_target_pairs={{0,16},{1,17},{2,18},{3,19},{4,20},{5,21},{6,22},{7,23},{8,24},{9,... | collective-permute-start | bytes 3145736 | tf_op jit(solution)/shard_map/ppermute | solution.py:45
  0.0 17.1 %copy-start.4 = (s32[256,1]{0,1:T(1,128)S(1)}, s32[256,1]{0,1:T(1,128)}, u32[]{:S(2)}) copy-start(s32[256,1]{0,1:T(1,128)} %param.18) | copy-start | bytes 3076
  0.0 26.0 %collective-permute-start.1 = (bf16[1024,512]{1,0:T(8,128)(2,1)}, bf16[1024,512]{1,0:T(8,128)(2,1)S(1)}, u32[]{:S(2)}, u32[]{:S(2)}) collective-permute-start(bf16[1024,512]{1,0:T(8,128)(2,1)} %bitcast.25), channel_id=1, source_target_pairs={{0,16},{1,17},{2,18},{3,19},{4,20},{5,21},{6,22},{7,23},{8,24},{9,... | collective-permute-start | bytes 3145736 | tf_op jit(solution)/shard_map/ppermute | solution.py:45
  9.8 34.0 %copy-start.2 = (bf16[16,512,64]{1,2,0:T(8,128)(2,1)S(1)}, bf16[16,512,64]{1,2,0:T(8,128)(2,1)}, u32[]{:S(2)}) copy-start(bf16[16,512,64]{1,2,0:T(8,128)(2,1)} %param.21) | copy-start | bytes 3145732
  9.8 16.2 %all-to-all-start = ((bf16[16,16,512]{2,1,0:T(8,128)(2,1)}), bf16[16,16,512]{2,1,0:T(8,128)(2,1)S(1)}, u32[]{:S(2)}, u32[]{:S(2)}) async-start(bf16[16,16,512]{2,1,0:T(8,128)(2,1)} %attend.1), calls=%async_computation | async-start | bytes 524288 | tf_op jit(solution)/shard_map/all_to_all | solution.py:500
  26.0 39.5 %copy-start.1 = (bf16[16,64,512]{2,1,0:T(8,128)(2,1)S(1)}, bf16[16,64,512]{2,1,0:T(8,128)(2,1)}, u32[]{:S(2)}) copy-start(bf16[16,64,512]{2,1,0:T(8,128)(2,1)} %param.22) | copy-start | bytes 3145732
  26.4 16.1 %collective-permute-start.2 = (bf16[128,512]{1,0:T(8,128)(2,1)S(1)}, bf16[128,512]{1,0:T(8,128)(2,1)S(1)}, u32[]{:S(2)}, u32[]{:S(2)}) collective-permute-start(bf16[128,512]{1,0:T(8,128)(2,1)S(1)} %get-tuple-element.42), channel_id=1, source_target_pairs={{0,32},{1,33},{2,34},{3,35},{4,36},{5,37},{6,38},{7,39},{8,40},{9,... | collective-permute-start | bytes 393224 | tf_op jit(solution)/shard_map/ppermute | solution.py:41
  28.3 14.1 %collective-permute-start.3 = (bf16[128,512]{1,0:T(8,128)(2,1)S(1)}, bf16[128,512]{1,0:T(8,128)(2,1)S(1)}, u32[]{:S(2)}, u32[]{:S(2)}) collective-permute-start(bf16[128,512]{1,0:T(8,128)(2,1)S(1)} %get-tuple-element.43), channel_id=1, source_target_pairs={{0,64},{1,65},{2,66},{3,67},{4,68},{5,69},{6,70},{7,71},{8,72},{9,... | collective-permute-start | bytes 393224 | tf_op jit(solution)/shard_map/ppermute | solution.py:41
  31.9 10.5 %collective-permute-start.4 = (bf16[128,512]{1,0:T(8,128)(2,1)S(1)}, bf16[128,512]{1,0:T(8,128)(2,1)S(1)}, u32[]{:S(2)}, u32[]{:S(2)}) collective-permute-start(bf16[128,512]{1,0:T(8,128)(2,1)S(1)} %get-tuple-element.44), channel_id=1, source_target_pairs={{0,96},{1,97},{2,98},{3,99},{4,100},{5,101},{6,102},{7,103},{8,104... | collective-permute-start | bytes 393224 | tf_op jit(solution)/shard_map/ppermute | solution.py:41
  32.9 3.4 %copy-start = (bf16[512,8192]{1,0:T(8,128)(2,1)S(1)}, bf16[512,8192]{1,0:T(8,128)(2,1)}, u32[]{:S(2)}) copy-start(bf16[512,8192]{1,0:T(8,128)(2,1)} %w_ref.1) | copy-start | bytes 25165828
  41.6 50.8 %copy-start.3 = (bf16[16,8192]{1,0:T(8,128)(2,1)S(1)}, bf16[16,8192]{1,0:T(8,128)(2,1)}, u32[]{:S(2)}) copy-start(bf16[16,8192]{1,0:T(8,128)(2,1)} %skip_ref.1) | copy-start | bytes 786436
  41.6 20.4 %collective-permute-start.6 = (bf16[64,8192]{1,0:T(8,128)(2,1)S(1)}, bf16[64,8192]{1,0:T(8,128)(2,1)S(1)}, u32[]{:S(2)}, u32[]{:S(2)}) collective-permute-start(bf16[64,8192]{1,0:T(8,128)(2,1)S(1)} %get-tuple-element.46), channel_id=1, source_target_pairs={{0,3},{1,0},{2,1},{3,2},{4,7},{5,4},{6,5},{7,6},{8,11},{9,8},{10,9... | collective-permute-start | bytes 3145736 | tf_op jit(solution)/shard_map/ppermute | solution.py:36
  42.4 19.5 %collective-permute-start.5 = (bf16[64,8192]{1,0:T(8,128)(2,1)S(1)}, bf16[64,8192]{1,0:T(8,128)(2,1)S(1)}, u32[]{:S(2)}, u32[]{:S(2)}) collective-permute-start(bf16[64,8192]{1,0:T(8,128)(2,1)S(1)} %get-tuple-element.45), channel_id=1, source_target_pairs={{0,1},{1,2},{2,3},{3,0},{4,5},{5,6},{6,7},{7,4},{8,9},{9,10},{10,1... | collective-permute-start | bytes 3145736 | tf_op jit(solution)/shard_map/ppermute | solution.py:36
  44.5 5.1 %collective-permute-start.9 = (bf16[256,128]{1,0:T(8,128)(2,1)S(1)}, bf16[256,128]{1,0:T(8,128)(2,1)S(1)}, u32[]{:S(2)}, u32[]{:S(2)}) collective-permute-start(bf16[256,128]{1,0:T(8,128)(2,1)S(1)} %shrink.1), channel_id=1, source_target_pairs={{0,12},{1,13},{2,14},{3,15},{4,0},{5,1},{6,2},{7,3},{8,4},{9,5},{1... | collective-permute-start | bytes 196616 | tf_op jit(solution)/shard_map/ppermute | solution.py:36
  45.5 6.5 %collective-permute-start.8 = (bf16[256,128]{1,0:T(8,128)(2,1)S(1)}, bf16[256,128]{1,0:T(8,128)(2,1)S(1)}, u32[]{:S(2)}, u32[]{:S(2)}) collective-permute-start(bf16[256,128]{1,0:T(8,128)(2,1)S(1)} %shrink.1), channel_id=1, source_target_pairs={{0,8},{1,9},{2,10},{3,11},{4,12},{5,13},{6,14},{7,15},{8,0},{9,1},... | collective-permute-start | bytes 196616 | tf_op jit(solution)/shard_map/ppermute | solution.py:36
  46.7 6.5 %collective-permute-start.7 = (bf16[256,128]{1,0:T(8,128)(2,1)S(1)}, bf16[256,128]{1,0:T(8,128)(2,1)S(1)}, u32[]{:S(2)}, u32[]{:S(2)}) collective-permute-start(bf16[256,128]{1,0:T(8,128)(2,1)S(1)} %shrink.1), channel_id=1, source_target_pairs={{0,4},{1,5},{2,6},{3,7},{4,8},{5,9},{6,10},{7,11},{8,12},{9,13},{1... | collective-permute-start | bytes 196616 | tf_op jit(solution)/shard_map/ppermute | solution.py:36
  53.2 4.9 %collective-permute-start.12 = (bf16[256,128]{1,0:T(8,128)(2,1)S(1)}, bf16[256,128]{1,0:T(8,128)(2,1)S(1)}, u32[]{:S(2)}, u32[]{:S(2)}) collective-permute-start(bf16[256,128]{1,0:T(8,128)(2,1)S(1)} %add_convert_fusion.1), channel_id=1, source_target_pairs={{0,3},{1,0},{2,1},{3,2},{4,7},{5,4},{6,5},{7,6},{8,11},{9,8},{10,9... | collective-permute-start | bytes 196616 | tf_op jit(solution)/shard_map/ppermute | solution.py:36
  55.6 5.9 %collective-permute-start.11 = (bf16[256,128]{1,0:T(8,128)(2,1)S(1)}, bf16[256,128]{1,0:T(8,128)(2,1)S(1)}, u32[]{:S(2)}, u32[]{:S(2)}) collective-permute-start(bf16[256,128]{1,0:T(8,128)(2,1)S(1)} %add_convert_fusion.1), channel_id=1, source_target_pairs={{0,2},{1,3},{2,0},{3,1},{4,6},{5,7},{6,4},{7,5},{8,10},{9,11},{10,... | collective-permute-start | bytes 196616 | tf_op jit(solution)/shard_map/ppermute | solution.py:36
  55.8 6.2 %collective-permute-start.10 = (bf16[256,128]{1,0:T(8,128)(2,1)S(1)}, bf16[256,128]{1,0:T(8,128)(2,1)S(1)}, u32[]{:S(2)}, u32[]{:S(2)}) collective-permute-start(bf16[256,128]{1,0:T(8,128)(2,1)S(1)} %add_convert_fusion.1), channel_id=1, source_target_pairs={{0,1},{1,2},{2,3},{3,0},{4,5},{5,6},{6,7},{7,4},{8,9},{9,10},{10,1... | collective-permute-start | bytes 196616 | tf_op jit(solution)/shard_map/ppermute | solution.py:36
  62.2 13.6 %collective-permute-start.13 = (bf16[64,4096]{1,0:T(8,128)(2,1)S(1)}, bf16[64,4096]{1,0:T(8,128)(2,1)S(1)}, u32[]{:S(2)}, u32[]{:S(2)}) collective-permute-start(bf16[64,4096]{1,0:T(8,128)(2,1)S(1)} %get-tuple-element.55), channel_id=1, source_target_pairs={{0,1},{1,2},{2,3},{3,0},{4,5},{5,6},{6,7},{7,4},{8,9},{9,10},{10,1... | collective-permute-start | bytes 1572872 | tf_op jit(solution)/shard_map/ppermute | solution.py:36
  62.3 13.6 %collective-permute-start.14 = (bf16[64,4096]{1,0:T(8,128)(2,1)S(1)}, bf16[64,4096]{1,0:T(8,128)(2,1)S(1)}, u32[]{:S(2)}, u32[]{:S(2)}) collective-permute-start(bf16[64,4096]{1,0:T(8,128)(2,1)S(1)} %get-tuple-element.56), channel_id=1, source_target_pairs={{0,3},{1,0},{2,1},{3,2},{4,7},{5,4},{6,5},{7,6},{8,11},{9,8},{10,9... | collective-permute-start | bytes 1572872 | tf_op jit(solution)/shard_map/ppermute | solution.py:36
  66.0 5.0 %collective-permute-start.15 = (bf16[128,512]{1,0:T(8,128)(2,1)S(1)}, bf16[128,512]{1,0:T(8,128)(2,1)S(1)}, u32[]{:S(2)}, u32[]{:S(2)}) collective-permute-start(bf16[128,512]{1,0:T(8,128)(2,1)S(1)} %get-tuple-element.65), channel_id=1, source_target_pairs={{0,96},{1,97},{2,98},{3,99},{4,100},{5,101},{6,102},{7,103},{8,104... | collective-permute-start | bytes 393224 | tf_op jit(solution)/shard_map/ppermute | solution.py:41
  66.1 6.6 %collective-permute-start.16 = (bf16[128,512]{1,0:T(8,128)(2,1)S(1)}, bf16[128,512]{1,0:T(8,128)(2,1)S(1)}, u32[]{:S(2)}, u32[]{:S(2)}) collective-permute-start(bf16[128,512]{1,0:T(8,128)(2,1)S(1)} %get-tuple-element.66), channel_id=1, source_target_pairs={{0,64},{1,65},{2,66},{3,67},{4,68},{5,69},{6,70},{7,71},{8,72},{9,... | collective-permute-start | bytes 393224 | tf_op jit(solution)/shard_map/ppermute | solution.py:41
  69.2 6.2 %collective-permute-start.17 = (bf16[128,512]{1,0:T(8,128)(2,1)S(1)}, bf16[128,512]{1,0:T(8,128)(2,1)S(1)}, u32[]{:S(2)}, u32[]{:S(2)}) collective-permute-start(bf16[128,512]{1,0:T(8,128)(2,1)S(1)} %get-tuple-element.67), channel_id=1, source_target_pairs={{0,32},{1,33},{2,34},{3,35},{4,36},{5,37},{6,38},{7,39},{8,40},{9,... | collective-permute-start | bytes 393224 | tf_op jit(solution)/shard_map/ppermute | solution.py:41
  76.3 16.1 %collective-permute-start.18 = (bf16[16,8192]{1,0:T(8,128)(2,1)S(1)}, bf16[16,8192]{1,0:T(8,128)(2,1)S(1)}, u32[]{:S(2)}, u32[]{:S(2)}) collective-permute-start(bf16[16,8192]{1,0:T(8,128)(2,1)S(1)} %get-tuple-element.69), channel_id=1, source_target_pairs={{0,4},{1,5},{2,6},{3,7},{4,8},{5,9},{6,10},{7,11},{8,12},{9,13},{1... | collective-permute-start | bytes 786440 | tf_op jit(solution)/shard_map/ppermute | solution.py:36
  76.5 15.9 %collective-permute-start.19 = (bf16[16,8192]{1,0:T(8,128)(2,1)S(1)}, bf16[16,8192]{1,0:T(8,128)(2,1)S(1)}, u32[]{:S(2)}, u32[]{:S(2)}) collective-permute-start(bf16[16,8192]{1,0:T(8,128)(2,1)S(1)} %get-tuple-element.70), channel_id=1, source_target_pairs={{0,8},{1,9},{2,10},{3,11},{4,12},{5,13},{6,14},{7,15},{8,0},{9,1},... | collective-permute-start | bytes 786440 | tf_op jit(solution)/shard_map/ppermute | solution.py:36
  78.7 13.7 %collective-permute-start.20 = (bf16[16,8192]{1,0:T(8,128)(2,1)S(1)}, bf16[16,8192]{1,0:T(8,128)(2,1)S(1)}, u32[]{:S(2)}, u32[]{:S(2)}) collective-permute-start(bf16[16,8192]{1,0:T(8,128)(2,1)S(1)} %get-tuple-element.71), channel_id=1, source_target_pairs={{0,12},{1,13},{2,14},{3,15},{4,0},{5,1},{6,2},{7,3},{8,4},{9,5},{1... | collective-permute-start | bytes 786440 | tf_op jit(solution)/shard_map/ppermute | solution.py:36

commit v4 on v2

--- a/solution.py
+++ b/solution.py
@@ -164,15 +164,18 @@
     return [pl.BlockSpec(memory_space=pltpu.VMEM)] * count
 
 
-TILES = 8
-
-
-def project_kernel(order_ref, f_ref, w_ref, own, ahead, back, ahead_last, back_last, *scratch):
-    rows_ref, out_ref, o_sem = scratch
+TILES = 4
+
+
+def project_kernel(order_ref, f_ref, w_hbm, own, ahead, back, ahead_last, back_last, *scratch):
+    rows_ref, w_ref, out_ref, w_sem, o_sem = scratch
     block = f_ref.shape[1]
-    tile = w_ref.shape[1] // TILES
+    tile = w_ref.shape[2]
     chunk = rows_ref.shape[0] // SIDE
     half = TILES // 2
+
+    def arrival(k):
+        return pltpu.make_async_copy(w_hbm.at[:, pl.ds(k * tile, tile)], w_ref.at[k], w_sem.at[k])
 
     def departure(k, part):
         low = k < half
@@ -189,12 +192,13 @@
             o_sem.at[k, part],
         )
 
+    for k in range(TILES):
+        arrival(k).start()
     for k in range(SIDE * SIDE):
         rows_ref[k * block : (k + 1) * block, :] = f_ref[order_ref[k]]
     for k in range(TILES):
-        out_ref[k] = jnp.dot(
-            rows_ref[...], w_ref[:, k * tile : (k + 1) * tile], preferred_element_type=F32
-        ).astype(BF16)
+        arrival(k).wait()
+        out_ref[k] = jnp.dot(rows_ref[...], w_ref[k], preferred_element_type=F32).astype(BF16)
         for part in range(SIDE):
             departure(k, part).start()
     for k in range(TILES):
@@ -217,15 +221,17 @@
         in_specs=[
             pl.BlockSpec(memory_space=pltpu.SMEM),
             pl.BlockSpec(memory_space=pltpu.VMEM),
-            pl.BlockSpec(memory_space=pltpu.VMEM),
+            far,
         ],
         out_specs=[far] * 5,
         scratch_shapes=[
             pltpu.VMEM((blocks * rows, depth), BF16),
+            pltpu.VMEM((TILES, depth, tile), BF16),
             pltpu.VMEM((TILES, blocks * rows, tile), BF16),
+            pltpu.SemaphoreType.DMA((TILES,)),
             pltpu.SemaphoreType.DMA((TILES, SIDE)),
         ],
-        compiler_params=pltpu.CompilerParams(vmem_limit_bytes=VMEM_BYTES),
+        compiler_params=pltpu.CompilerParams(vmem_limit_bytes=56 * 1024 * 1024),
         cost_estimate=pl.CostEstimate(
             flops=2 * blocks * rows * depth * cols,
             bytes_accessed=2 * depth * cols + 2 * blocks * rows * cols,
@@ -234,19 +240,34 @@
     )(order, features, weight)
 
 
-def meet_kernel(ahead_last, back_last, came_ahead, came_back, ahead_ref, back_ref):
+def meet_kernel(ahead_hbm, back_hbm, came_ahead, came_back, ahead_ref, back_ref, *scratch):
+    ahead_last, back_last, sem = scratch
     half = ahead_ref.shape[1]
+    copies = (
+        pltpu.make_async_copy(ahead_hbm, ahead_last, sem.at[0]),
+        pltpu.make_async_copy(back_hbm, back_last, sem.at[1]),
+    )
+    for copy in copies:
+        copy.start()
+    copies[0].wait()
     ahead_ref[...] = (ahead_last[...].astype(F32) + came_ahead[:, :half].astype(F32)).astype(BF16)
+    copies[1].wait()
     back_ref[...] = (back_last[...].astype(F32) + came_back[:, half:].astype(F32)).astype(BF16)
 
 
 def meet(*operands):
+    half = operands[0]
     return pl.pallas_call(
         meet_kernel,
         name="meet",
-        out_shape=[jax.ShapeDtypeStruct(operands[0].shape, BF16)] * 2,
-        in_specs=whole(4),
+        out_shape=[jax.ShapeDtypeStruct(half.shape, BF16)] * 2,
+        in_specs=[pl.BlockSpec(memory_space=pl.ANY)] * 2 + whole(2),
         out_specs=whole(2),
+        scratch_shapes=[
+            pltpu.VMEM(half.shape, BF16),
+            pltpu.VMEM(half.shape, BF16),
+            pltpu.SemaphoreType.DMA((2,)),
+        ],
         compiler_params=pltpu.CompilerParams(vmem_limit_bytes=VMEM_BYTES),
         cost_estimate=pl.CostEstimate(flops=2**20, bytes_accessed=2**22, transcendentals=0),
     )(*operands)
@@ -511,15 +532,16 @@
     near = [pass_plane(shrunk, "yx", k) for k in range(1, SIDE)]
     shrunk = wide_sum(shrunk, *near).astype(BF16)
     near = [pass_plane(shrunk, "xy", k) for k in range(1, SIDE)]
+    ahead_last, back_last = meet(ahead_last, back_last, came_ahead, came_back)
     *near, ahead_last, back_last = lax.optimization_barrier((*near, ahead_last, back_last))
     shrunk = wide_sum(shrunk, *near).astype(BF16)
-    ahead_last, back_last = meet(ahead_last, back_last, came_ahead, came_back)
     ahead_last, back_last = pass_plane(ahead_last, "xy", 1), pass_plane(back_last, "xy", -1)
     grown = grow(shrunk, up_own, up_other, per_z)
     returned = [grown[0]] + [pass_z(grown[k], -k) for k in range(1, SIDE)]
+    returned[1], returned[2], back_last = lax.optimization_barrier((returned[1], returned[2], back_last))
+    summed = join(own, came_ahead, came_back, ahead_last, back_last)
     delta = collect(slot, returned, blocks)
 
-    summed = join(own, came_ahead, came_back, ahead_last, back_last)
     second = [pass_plane(summed[k], "yx", k) for k in range(1, SIDE)]
     delta = lax.all_to_all(delta, "tp", split_axis=0, concat_axis=0, tiled=True)
     return finish(skip_stream, summed[0], *second, delta)

time: 96.8 us -> 89.4 us (0.924)
  waiting for transfers between devices: 25.8 us -> 22 us
  blocking collectives: 15.4 us -> 12.2 us
  Pallas kernels: 18.1 us -> 19.6 us
  starting transfers between devices: 32.6 us -> 31.3 us
    ppermute x13, waiting for transfers between devices: 17.8 us -> 10.8 us  [pass_plane(): return lax.ppermute(value, BOTH, pairs)]
    ppermute x6, waiting for transfers between devices: 0.02 us -> 3.82 us  [pass_z(): return lax.ppermute(value, BOTH, pairs)]
    all_to_all x1, blocking collectives: 15.4 us -> 12.2 us  [body(): delta = lax.all_to_all(delta, 'tp', split_axis=0, concat_axis=0, tiled=True)]
    pallas_call x1, Pallas kernels: 5.26 us -> 6.67 us  [project(): pl.pallas_call(project_kernel, name='project', out_shape=[full, full, ful...]
    unnamed x10 -> x16, local copies, waits for them, and re-layouts: 3.4 us -> 2.11 us
    ppermute x13, starting transfers between devices: 15.1 us -> 13.8 us  [pass_plane(): return lax.ppermute(value, BOTH, pairs)]
  transfers between devices with their start and end apart: 22 -> 22, of which waited for: 9 -> 9; matrix products, arithmetic and copies ran while one was open for 1% -> 2% of each run, Pallas kernels for 17% -> 21%
where the time goes in v4:
time: 89.4 us; the launch traced here: 89 us
  starting transfers between devices  31.3 us (35%)
  waiting for transfers between devices  22 us (25%)
  Pallas kernels  19.6 us (22%)
  blocking collectives  12.2 us (14%)
  local copies, waits for them, and re-layouts  3.38 us (4%)
    ppermute x13, starting transfers between devices, pass_plane(): return lax.ppermute(value, BOTH, pairs)  13.8 us
    all_to_all x1, blocking collectives, body(): delta = lax.all_to_all(delta, 'tp', split_axis=0, concat_axis=0, tiled=True)  12.2 us
    ppermute x13, waiting for transfers between devices, pass_plane(): return lax.ppermute(value, BOTH, pairs)  10.8 us
    ppermute x6, starting transfers between devices, pass_z(): return lax.ppermute(value, BOTH, pairs)  9.73 us
    pallas_call x1, Pallas kernels, attend(): pl.pallas_call(attend_kernel, name='attend', out_shape=jax.ShapeDtypeStru...  9.3 us
    all_to_all x1, waiting for transfers between devices, body(): lax.all_to_all(attended, 'tp', split_axis=0, concat_axis=0, tiled=True)  7.43 us
    all_to_all x1, starting transfers between devices, body(): lax.all_to_all(attended, 'tp', split_axis=0, concat_axis=0, tiled=True)  7.26 us
    pallas_call x1, Pallas kernels, project(): pl.pallas_call(project_kernel, name='project', out_shape=[full, full, ful...  6.67 us
  transfers between devices with their start and end apart: 22, of which 9 were waited for; matrix products, arithmetic and copies ran while one was open for 2% of the time, Pallas kernels for 21%

profile of v4, /device:TPU:0, one launch (start us, length us, event | category | flops | bytes accessed | tf_op | source)
XLA Modules:
  0.0 89.0 jit_solution(610567879538857321)
XLA Ops:
  0.5 9.3 %attend.1 = bf16[16,16,512]{2,1,0:T(8,128)(2,1)} custom-call(s32[16]{0:T(128)} %lengths_ref.1, bf16[16,64,128]{2,1,0:T(8,128)(2,1)} %q_ref.1, bf16[16,8,256,128]{3,2,1,0:T(8,128)(2,1)} %k_hbm.1, bf16[16,8,256,128]{3,2,1,0:T(8,128)(2,1)} %v_hbm.1, bf16[16,8,128]{2,1,0:T(8,128)(2,1)} %fk_ref.1, bf16[16,8,128]{2,1,0:T(8,128)(2,1)} %fv_ref.1), custom_call_target="tpu_custom_call" | custom-call | flops 134217728 | bytes 16777216 | tf_op jit(solution)/shard_map/attend/pallas_call | solution.py:141
  9.8 7.3 %all-to-all-start = ((bf16[16,16,512]{2,1,0:T(8,128)(2,1)}), bf16[16,16,512]{2,1,0:T(8,128)(2,1)S(1)}, u32[]{:S(2)}, u32[]{:S(2)}) async-start(bf16[16,16,512]{2,1,0:T(8,128)(2,1)} %attend.1), calls=%async_computation | async-start | bytes 524288 | tf_op jit(solution)/shard_map/all_to_all | solution.py:521
  17.3 1.3 %dynamic-slice_bitcast_fusion.order_ref = s32[16]{0:T(128)} fusion(s32[128,16]{1,0:T(8,128)} %constant.89.clone, s32[]{:T(128)S(6)} %select_n.71), kind=kLoop, calls=%fused_computation.27 | loop fusion | bytes 132 | tf_op jit(solution)/shard_map/squeeze | solution.py:516
  18.6 7.4 %all-to-all-done.f_ref = bf16[16,16,512]{2,1,0:T(8,128)(2,1)S(1)} async-done(((bf16[16,16,512]{2,1,0:T(8,128)(2,1)}), bf16[16,16,512]{2,1,0:T(8,128)(2,1)S(1)}, u32[]{:S(2)}, u32[]{:S(2)}) %all-to-all-start) | async-done | bytes 262176 | tf_op jit(solution)/shard_map/all_to_all | solution.py:521
  26.4 2.0 %collective-permute-start.2 = (bf16[128,512]{1,0:T(8,128)(2,1)S(1)}, bf16[128,512]{1,0:T(8,128)(2,1)S(1)}, u32[]{:S(2)}, u32[]{:S(2)}) collective-permute-start(bf16[128,512]{1,0:T(8,128)(2,1)S(1)} %get-tuple-element.40), channel_id=1, source_target_pairs={{0,32},{1,33},{2,34},{3,35},{4,36},{5,37},{6,38},{7,39},{8,40},{9,... | collective-permute-start | bytes 393224 | tf_op jit(solution)/shard_map/ppermute | solution.py:41
  28.4 3.6 %collective-permute-start.3 = (bf16[128,512]{1,0:T(8,128)(2,1)S(1)}, bf16[128,512]{1,0:T(8,128)(2,1)S(1)}, u32[]{:S(2)}, u32[]{:S(2)}) collective-permute-start(bf16[128,512]{1,0:T(8,128)(2,1)S(1)} %get-tuple-element.41), channel_id=1, source_target_pairs={{0,64},{1,65},{2,66},{3,67},{4,68},{5,69},{6,70},{7,71},{8,72},{9,... | collective-permute-start | bytes 393224 | tf_op jit(solution)/shard_map/ppermute | solution.py:41
  31.9 1.0 %collective-permute-start.4 = (bf16[128,512]{1,0:T(8,128)(2,1)S(1)}, bf16[128,512]{1,0:T(8,128)(2,1)S(1)}, u32[]{:S(2)}, u32[]{:S(2)}) collective-permute-start(bf16[128,512]{1,0:T(8,128)(2,1)S(1)} %get-tuple-element.42), channel_id=1, source_target_pairs={{0,96},{1,97},{2,98},{3,99},{4,100},{5,101},{6,102},{7,103},{8,104... | collective-permute-start | bytes 393224 | tf_op jit(solution)/shard_map/ppermute | solution.py:41
  33.0 6.7 %project.1 = (bf16[64,8192]{1,0:T(8,128)(2,1)}, bf16[64,8192]{1,0:T(8,128)(2,1)}, bf16[64,8192]{1,0:T(8,128)(2,1)}, bf16[64,4096]{1,0:T(8,128)(2,1)}, bf16[64,4096]{1,0:T(8,128)(2,1)}) custom-call(s32[16]{0:T(128)} %dynamic-slice_bitcast_fusion.order_ref, bf16[16,16,512]{2,1,0:T(8,128)(2,1)} %copy-done, bf16[512,8192]{1,0:T(8,128)(2,1)} %w_hbm.1), custom_call_target="tpu_custom_call" | custom-call | flops 2147483648 | bytes 12582912 | tf_op jit(solution)/shard_map/project/pallas_call | solution.py:217
  39.6 0.8 collective-permute-start.6
  40.5 1.3 %collective-permute-start.5 = (bf16[64,8192]{1,0:T(8,128)(2,1)}, bf16[64,8192]{1,0:T(8,128)(2,1)S(1)}, u32[]{:S(2)}, u32[]{:S(2)}) collective-permute-start(bf16[64,8192]{1,0:T(8,128)(2,1)} %get-tuple-element.43), channel_id=1, source_target_pairs={{0,1},{1,2},{2,3},{3,0},{4,5},{5,6},{6,7},{7,4},{8,9},{9,10},{10,1... | collective-permute-start | bytes 3145736 | tf_op jit(solution)/shard_map/ppermute | solution.py:36
  41.8 0.8 shrink.1
  42.6 0.9 %collective-permute-start.9 = (bf16[256,128]{1,0:T(8,128)(2,1)S(1)}, bf16[256,128]{1,0:T(8,128)(2,1)S(1)}, u32[]{:S(2)}, u32[]{:S(2)}) collective-permute-start(bf16[256,128]{1,0:T(8,128)(2,1)S(1)} %shrink.1), channel_id=1, source_target_pairs={{0,12},{1,13},{2,14},{3,15},{4,0},{5,1},{6,2},{7,3},{8,4},{9,5},{1... | collective-permute-start | bytes 196616 | tf_op jit(solution)/shard_map/ppermute | solution.py:36
  43.5 1.3 %collective-permute-start.8 = (bf16[256,128]{1,0:T(8,128)(2,1)S(1)}, bf16[256,128]{1,0:T(8,128)(2,1)S(1)}, u32[]{:S(2)}, u32[]{:S(2)}) collective-permute-start(bf16[256,128]{1,0:T(8,128)(2,1)S(1)} %shrink.1), channel_id=1, source_target_pairs={{0,8},{1,9},{2,10},{3,11},{4,12},{5,13},{6,14},{7,15},{8,0},{9,1},... | collective-permute-start | bytes 196616 | tf_op jit(solution)/shard_map/ppermute | solution.py:36
  44.9 2.8 %collective-permute-done.9 = bf16[256,128]{1,0:T(8,128)(2,1)S(1)} collective-permute-done((bf16[256,128]{1,0:T(8,128)(2,1)S(1)}, bf16[256,128]{1,0:T(8,128)(2,1)S(1)}, u32[]{:S(2)}, u32[]{:S(2)}) %collective-permute-start.9) | collective-permute-done | bytes 65568 | tf_op jit(solution)/shard_map/ppermute | solution.py:36
  47.7 2.4 %collective-permute-done.8 = bf16[256,128]{1,0:T(8,128)(2,1)S(1)} collective-permute-done((bf16[256,128]{1,0:T(8,128)(2,1)S(1)}, bf16[256,128]{1,0:T(8,128)(2,1)S(1)}, u32[]{:S(2)}, u32[]{:S(2)}) %collective-permute-start.8) | collective-permute-done | bytes 65568 | tf_op jit(solution)/shard_map/ppermute | solution.py:36
  50.0 1.2 %collective-permute-done.7 = bf16[256,128]{1,0:T(8,128)(2,1)S(1)} collective-permute-done((bf16[256,128]{1,0:T(8,128)(2,1)S(1)}, bf16[256,128]{1,0:T(8,128)(2,1)S(1)}, u32[]{:S(2)}, u32[]{:S(2)}) %collective-permute-start.7) | collective-permute-done | bytes 65568 | tf_op jit(solution)/shard_map/ppermute | solution.py:36
  51.3 2.4 %collective-permute-start.12 = (bf16[256,128]{1,0:T(8,128)(2,1)S(1)}, bf16[256,128]{1,0:T(8,128)(2,1)S(1)}, u32[]{:S(2)}, u32[]{:S(2)}) collective-permute-start(bf16[256,128]{1,0:T(8,128)(2,1)S(1)} %add_convert_fusion.1), channel_id=1, source_target_pairs={{0,3},{1,0},{2,1},{3,2},{4,7},{5,4},{6,5},{7,6},{8,11},{9,8},{10,9... | collective-permute-start | bytes 196616 | tf_op jit(solution)/shard_map/ppermute | solution.py:36
  53.8 0.8 collective-permute-start.10
  54.6 0.8 collective-permute-done.6.came_back
  55.4 2.1 %collective-permute-done.5.came_ahead = bf16[64,8192]{1,0:T(8,128)(2,1)S(1)} collective-permute-done((bf16[64,8192]{1,0:T(8,128)(2,1)}, bf16[64,8192]{1,0:T(8,128)(2,1)S(1)}, u32[]{:S(2)}, u32[]{:S(2)}) %collective-permute-start.5) | collective-permute-done | bytes 1048608 | tf_op jit(solution)/shard_map/ppermute | solution.py:36
  57.6 1.0 %copy-done.4 = bf16[64,4096]{1,0:T(8,128)(2,1)S(1)} copy-done((bf16[64,4096]{1,0:T(8,128)(2,1)S(1)}, bf16[64,4096]{1,0:T(8,128)(2,1)}, u32[]{:S(2)}) %copy-start.4) | copy-done | bytes 524312
  58.6 1.0 %copy-done.5 = bf16[64,4096]{1,0:T(8,128)(2,1)S(1)} copy-done((bf16[64,4096]{1,0:T(8,128)(2,1)S(1)}, bf16[64,4096]{1,0:T(8,128)(2,1)}, u32[]{:S(2)}) %copy-start.5) | copy-done | bytes 524312
  60.0 0.7 collective-permute-start.16
  60.7 1.4 %collective-permute-start.13 = (bf16[64,4096]{1,0:T(8,128)(2,1)S(1)}, bf16[64,4096]{1,0:T(8,128)(2,1)S(1)}, u32[]{:S(2)}, u32[]{:S(2)}) collective-permute-start(bf16[64,4096]{1,0:T(8,128)(2,1)S(1)} %get-tuple-element.53), channel_id=1, source_target_pairs={{0,1},{1,2},{2,3},{3,0},{4,5},{5,6},{6,7},{7,4},{8,9},{9,10},{10,1... | collective-permute-start | bytes 1572872 | tf_op jit(solution)/shard_map/ppermute | solution.py:36
  62.9 2.9 %collective-permute-start.15 = (bf16[128,512]{1,0:T(8,128)(2,1)S(1)}, bf16[128,512]{1,0:T(8,128)(2,1)S(1)}, u32[]{:S(2)}, u32[]{:S(2)}) collective-permute-start(bf16[128,512]{1,0:T(8,128)(2,1)S(1)} %get-tuple-element.58), channel_id=1, source_target_pairs={{0,64},{1,65},{2,66},{3,67},{4,68},{5,69},{6,70},{7,71},{8,72},{9,... | collective-permute-start | bytes 393224 | tf_op jit(solution)/shard_map/ppermute | solution.py:41
  65.8 1.9 %collective-permute-done.14.r1 = bf16[128,512]{1,0:T(8,128)(2,1)S(1)} collective-permute-done((bf16[128,512]{1,0:T(8,128)(2,1)S(1)}, bf16[128,512]{1,0:T(8,128)(2,1)S(1)}, u32[]{:S(2)}, u32[]{:S(2)}) %collective-permute-start.14) | collective-permute-done | bytes 131104 | tf_op jit(solution)/shard_map/ppermute | solution.py:41
  67.7 1.9 %collective-permute-done.15.r2 = bf16[128,512]{1,0:T(8,128)(2,1)S(1)} collective-permute-done((bf16[128,512]{1,0:T(8,128)(2,1)S(1)}, bf16[128,512]{1,0:T(8,128)(2,1)S(1)}, u32[]{:S(2)}, u32[]{:S(2)}) %collective-permute-start.15) | collective-permute-done | bytes 131104 | tf_op jit(solution)/shard_map/ppermute | solution.py:41
  69.6 1.5 %collective-permute-done.13.ahead_last = bf16[64,4096]{1,0:T(8,128)(2,1)S(1)} collective-permute-done((bf16[64,4096]{1,0:T(8,128)(2,1)S(1)}, bf16[64,4096]{1,0:T(8,128)(2,1)S(1)}, u32[]{:S(2)}, u32[]{:S(2)}) %collective-permute-start.13) | collective-permute-done | bytes 524320 | tf_op jit(solution)/shard_map/ppermute | solution.py:36
  71.6 2.6 %collective-permute-start.18 = (bf16[16,8192]{1,0:T(8,128)(2,1)S(1)}, bf16[16,8192]{1,0:T(8,128)(2,1)S(1)}, u32[]{:S(2)}, u32[]{:S(2)}) collective-permute-start(bf16[16,8192]{1,0:T(8,128)(2,1)S(1)} %get-tuple-element.63), channel_id=1, source_target_pairs={{0,8},{1,9},{2,10},{3,11},{4,12},{5,13},{6,14},{7,15},{8,0},{9,1},... | collective-permute-start | bytes 786440 | tf_op jit(solution)/shard_map/ppermute | solution.py:36
  74.2 1.2 %collective-permute-start.19 = (bf16[16,8192]{1,0:T(8,128)(2,1)S(1)}, bf16[16,8192]{1,0:T(8,128)(2,1)S(1)}, u32[]{:S(2)}, u32[]{:S(2)}) collective-permute-start(bf16[16,8192]{1,0:T(8,128)(2,1)S(1)} %get-tuple-element.64), channel_id=1, source_target_pairs={{0,12},{1,13},{2,14},{3,15},{4,0},{5,1},{6,2},{7,3},{8,4},{9,5},{1... | collective-permute-start | bytes 786440 | tf_op jit(solution)/shard_map/ppermute | solution.py:36
  75.8 12.2 %all_to_all.10.delta_ref = bf16[16,16,512]{2,1,0:T(8,128)(2,1)S(1)} all-to-all(bf16[16,16,512]{2,1,0:T(8,128)(2,1)S(1)} %collect.1), channel_id=1, replica_groups=mesh['rep'=8,'tp'=16] {'tp'}, dimensions={0} | all-to-all | bytes 524288 | tf_op jit(solution)/shard_map/all_to_all | solution.py:546
  88.1 0.9 %finish.1 = bf16[16,8192]{1,0:T(8,128)(2,1)} custom-call(bf16[16,8192]{1,0:T(8,128)(2,1)S(1)} %copy-done.6, bf16[16,8192]{1,0:T(8,128)(2,1)S(1)} %get-tuple-element.61.s_ref, bf16[16,8192]{1,0:T(8,128)(2,1)S(1)} %collective-permute-done.17.a_ref, bf16[16,8192]{1,0:T(8,128)(2,1)S(1)} %collective-permute-done.18.b_ref, ...), custom_call_target="tpu_custom_call" | custom-call | flops 1048576 | bytes 2097152 | tf_op jit(solution)/shard_map/finish/pallas_call | solution.py:456
  (43 shorter events, 3.5 us)
Async XLA Ops:
  0.0 26.0 %collective-permute-start = (bf16[1024,512]{1,0:T(8,128)(2,1)}, bf16[1024,512]{1,0:T(8,128)(2,1)S(1)}, u32[]{:S(2)}, u32[]{:S(2)}) collective-permute-start(bf16[1024,512]{1,0:T(8,128)(2,1)} %bitcast.27), channel_id=1, source_target_pairs={{0,16},{1,17},{2,18},{3,19},{4,20},{5,21},{6,22},{7,23},{8,24},{9,... | collective-permute-start | bytes 3145736 | tf_op jit(solution)/shard_map/ppermute | solution.py:45
  0.0 17.1 %copy-start.7 = (s32[256,1]{0,1:T(1,128)S(1)}, s32[256,1]{0,1:T(1,128)}, u32[]{:S(2)}) copy-start(s32[256,1]{0,1:T(1,128)} %param.18) | copy-start | bytes 3076
  0.0 26.0 %collective-permute-start.1 = (bf16[1024,512]{1,0:T(8,128)(2,1)}, bf16[1024,512]{1,0:T(8,128)(2,1)S(1)}, u32[]{:S(2)}, u32[]{:S(2)}) collective-permute-start(bf16[1024,512]{1,0:T(8,128)(2,1)} %bitcast.25), channel_id=1, source_target_pairs={{0,16},{1,17},{2,18},{3,19},{4,20},{5,21},{6,22},{7,23},{8,24},{9,... | collective-permute-start | bytes 3145736 | tf_op jit(solution)/shard_map/ppermute | solution.py:45
  9.8 32.0 %copy-start.2 = (bf16[16,512,64]{1,2,0:T(8,128)(2,1)S(1)}, bf16[16,512,64]{1,2,0:T(8,128)(2,1)}, u32[]{:S(2)}) copy-start(bf16[16,512,64]{1,2,0:T(8,128)(2,1)} %param.21) | copy-start | bytes 3145732
  9.8 16.2 %all-to-all-start = ((bf16[16,16,512]{2,1,0:T(8,128)(2,1)}), bf16[16,16,512]{2,1,0:T(8,128)(2,1)S(1)}, u32[]{:S(2)}, u32[]{:S(2)}) async-start(bf16[16,16,512]{2,1,0:T(8,128)(2,1)} %attend.1), calls=%async_computation | async-start | bytes 524288 | tf_op jit(solution)/shard_map/all_to_all | solution.py:521
  26.0 6.9 %copy-start = (bf16[16,16,512]{2,1,0:T(8,128)(2,1)}, bf16[16,16,512]{2,1,0:T(8,128)(2,1)S(1)}, u32[]{:S(2)}) copy-start(bf16[16,16,512]{2,1,0:T(8,128)(2,1)S(1)} %all-to-all-done.f_ref) | copy-start | bytes 786436
  26.0 36.1 %copy-start.1 = (bf16[16,64,512]{2,1,0:T(8,128)(2,1)S(1)}, bf16[16,64,512]{2,1,0:T(8,128)(2,1)}, u32[]{:S(2)}) copy-start(bf16[16,64,512]{2,1,0:T(8,128)(2,1)} %param.22) | copy-start | bytes 3145732
  26.4 14.1 %collective-permute-start.2 = (bf16[128,512]{1,0:T(8,128)(2,1)S(1)}, bf16[128,512]{1,0:T(8,128)(2,1)S(1)}, u32[]{:S(2)}, u32[]{:S(2)}) collective-permute-start(bf16[128,512]{1,0:T(8,128)(2,1)S(1)} %get-tuple-element.40), channel_id=1, source_target_pairs={{0,32},{1,33},{2,34},{3,35},{4,36},{5,37},{6,38},{7,39},{8,40},{9,... | collective-permute-start | bytes 393224 | tf_op jit(solution)/shard_map/ppermute | solution.py:41
  28.4 12.1 %collective-permute-start.3 = (bf16[128,512]{1,0:T(8,128)(2,1)S(1)}, bf16[128,512]{1,0:T(8,128)(2,1)S(1)}, u32[]{:S(2)}, u32[]{:S(2)}) collective-permute-start(bf16[128,512]{1,0:T(8,128)(2,1)S(1)} %get-tuple-element.41), channel_id=1, source_target_pairs={{0,64},{1,65},{2,66},{3,67},{4,68},{5,69},{6,70},{7,71},{8,72},{9,... | collective-permute-start | bytes 393224 | tf_op jit(solution)/shard_map/ppermute | solution.py:41
  31.9 8.5 %collective-permute-start.4 = (bf16[128,512]{1,0:T(8,128)(2,1)S(1)}, bf16[128,512]{1,0:T(8,128)(2,1)S(1)}, u32[]{:S(2)}, u32[]{:S(2)}) collective-permute-start(bf16[128,512]{1,0:T(8,128)(2,1)S(1)} %get-tuple-element.42), channel_id=1, source_target_pairs={{0,96},{1,97},{2,98},{3,99},{4,100},{5,101},{6,102},{7,103},{8,104... | collective-permute-start | bytes 393224 | tf_op jit(solution)/shard_map/ppermute | solution.py:41
  39.6 31.5 %copy-start.3 = (bf16[64,8192]{1,0:T(8,128)(2,1)S(1)}, bf16[64,8192]{1,0:T(8,128)(2,1)}, u32[]{:S(2)}) copy-start(bf16[64,8192]{1,0:T(8,128)(2,1)} %get-tuple-element.37.own) | copy-start | bytes 3145732
  39.6 48.4 %copy-start.6 = (bf16[16,8192]{1,0:T(8,128)(2,1)S(1)}, bf16[16,8192]{1,0:T(8,128)(2,1)}, u32[]{:S(2)}) copy-start(bf16[16,8192]{1,0:T(8,128)(2,1)} %skip_ref.1) | copy-start | bytes 786436
  39.6 15.8 %collective-permute-start.6 = (bf16[64,8192]{1,0:T(8,128)(2,1)}, bf16[64,8192]{1,0:T(8,128)(2,1)S(1)}, u32[]{:S(2)}, u32[]{:S(2)}) collective-permute-start(bf16[64,8192]{1,0:T(8,128)(2,1)} %get-tuple-element.44), channel_id=1, source_target_pairs={{0,3},{1,0},{2,1},{3,2},{4,7},{5,4},{6,5},{7,6},{8,11},{9,8},{10,9... | collective-permute-start | bytes 3145736 | tf_op jit(solution)/shard_map/ppermute | solution.py:36
  40.5 17.1 %collective-permute-start.5 = (bf16[64,8192]{1,0:T(8,128)(2,1)}, bf16[64,8192]{1,0:T(8,128)(2,1)S(1)}, u32[]{:S(2)}, u32[]{:S(2)}) collective-permute-start(bf16[64,8192]{1,0:T(8,128)(2,1)} %get-tuple-element.43), channel_id=1, source_target_pairs={{0,1},{1,2},{2,3},{3,0},{4,5},{5,6},{6,7},{7,4},{8,9},{9,10},{10,1... | collective-permute-start | bytes 3145736 | tf_op jit(solution)/shard_map/ppermute | solution.py:36
  42.6 5.1 %collective-permute-start.9 = (bf16[256,128]{1,0:T(8,128)(2,1)S(1)}, bf16[256,128]{1,0:T(8,128)(2,1)S(1)}, u32[]{:S(2)}, u32[]{:S(2)}) collective-permute-start(bf16[256,128]{1,0:T(8,128)(2,1)S(1)} %shrink.1), channel_id=1, source_target_pairs={{0,12},{1,13},{2,14},{3,15},{4,0},{5,1},{6,2},{7,3},{8,4},{9,5},{1... | collective-permute-start | bytes 196616 | tf_op jit(solution)/shard_map/ppermute | solution.py:36
  43.5 6.5 %collective-permute-start.8 = (bf16[256,128]{1,0:T(8,128)(2,1)S(1)}, bf16[256,128]{1,0:T(8,128)(2,1)S(1)}, u32[]{:S(2)}, u32[]{:S(2)}) collective-permute-start(bf16[256,128]{1,0:T(8,128)(2,1)S(1)} %shrink.1), channel_id=1, source_target_pairs={{0,8},{1,9},{2,10},{3,11},{4,12},{5,13},{6,14},{7,15},{8,0},{9,1},... | collective-permute-start | bytes 196616 | tf_op jit(solution)/shard_map/ppermute | solution.py:36
  44.8 6.5 %collective-permute-start.7 = (bf16[256,128]{1,0:T(8,128)(2,1)S(1)}, bf16[256,128]{1,0:T(8,128)(2,1)S(1)}, u32[]{:S(2)}, u32[]{:S(2)}) collective-permute-start(bf16[256,128]{1,0:T(8,128)(2,1)S(1)} %shrink.1), channel_id=1, source_target_pairs={{0,4},{1,5},{2,6},{3,7},{4,8},{5,9},{6,10},{7,11},{8,12},{9,13},{1... | collective-permute-start | bytes 196616 | tf_op jit(solution)/shard_map/ppermute | solution.py:36
  51.3 8.7 %collective-permute-start.12 = (bf16[256,128]{1,0:T(8,128)(2,1)S(1)}, bf16[256,128]{1,0:T(8,128)(2,1)S(1)}, u32[]{:S(2)}, u32[]{:S(2)}) collective-permute-start(bf16[256,128]{1,0:T(8,128)(2,1)S(1)} %add_convert_fusion.1), channel_id=1, source_target_pairs={{0,3},{1,0},{2,1},{3,2},{4,7},{5,4},{6,5},{7,6},{8,11},{9,8},{10,9... | collective-permute-start | bytes 196616 | tf_op jit(solution)/shard_map/ppermute | solution.py:36
  53.7 6.3 %collective-permute-start.11 = (bf16[256,128]{1,0:T(8,128)(2,1)S(1)}, bf16[256,128]{1,0:T(8,128)(2,1)S(1)}, u32[]{:S(2)}, u32[]{:S(2)}) collective-permute-start(bf16[256,128]{1,0:T(8,128)(2,1)S(1)} %add_convert_fusion.1), channel_id=1, source_target_pairs={{0,2},{1,3},{2,0},{3,1},{4,6},{5,7},{6,4},{7,5},{8,10},{9,11},{10,... | collective-permute-start | bytes 196616 | tf_op jit(solution)/shard_map/ppermute | solution.py:36
  53.8 6.2 %collective-permute-start.10 = (bf16[256,128]{1,0:T(8,128)(2,1)S(1)}, bf16[256,128]{1,0:T(8,128)(2,1)S(1)}, u32[]{:S(2)}, u32[]{:S(2)}) collective-permute-start(bf16[256,128]{1,0:T(8,128)(2,1)S(1)} %add_convert_fusion.1), channel_id=1, source_target_pairs={{0,1},{1,2},{2,3},{3,0},{4,5},{5,6},{6,7},{7,4},{8,9},{9,10},{10,1... | collective-permute-start | bytes 196616 | tf_op jit(solution)/shard_map/ppermute | solution.py:36
  57.5 1.0 %copy-start.4 = (bf16[64,4096]{1,0:T(8,128)(2,1)S(1)}, bf16[64,4096]{1,0:T(8,128)(2,1)}, u32[]{:S(2)}) copy-start(bf16[64,4096]{1,0:T(8,128)(2,1)} %get-tuple-element.49.ahead_hbm) | copy-start | bytes 1572868
  58.6 1.0 %copy-start.5 = (bf16[64,4096]{1,0:T(8,128)(2,1)S(1)}, bf16[64,4096]{1,0:T(8,128)(2,1)}, u32[]{:S(2)}) copy-start(bf16[64,4096]{1,0:T(8,128)(2,1)} %get-tuple-element.50.back_hbm) | copy-start | bytes 1572868
  60.0 9.6 %collective-permute-start.16 = (bf16[64,4096]{1,0:T(8,128)(2,1)S(1)}, bf16[64,4096]{1,0:T(8,128)(2,1)S(1)}, u32[]{:S(2)}, u32[]{:S(2)}) collective-permute-start(bf16[64,4096]{1,0:T(8,128)(2,1)S(1)} %get-tuple-element.59), channel_id=1, source_target_pairs={{0,3},{1,0},{2,1},{3,2},{4,7},{5,4},{6,5},{7,6},{8,11},{9,8},{10,9... | collective-permute-start | bytes 1572872 | tf_op jit(solution)/shard_map/ppermute | solution.py:36
  60.7 10.4 %collective-permute-start.13 = (bf16[64,4096]{1,0:T(8,128)(2,1)S(1)}, bf16[64,4096]{1,0:T(8,128)(2,1)S(1)}, u32[]{:S(2)}, u32[]{:S(2)}) collective-permute-start(bf16[64,4096]{1,0:T(8,128)(2,1)S(1)} %get-tuple-element.53), channel_id=1, source_target_pairs={{0,1},{1,2},{2,3},{3,0},{4,5},{5,6},{6,7},{7,4},{8,9},{9,10},{10,1... | collective-permute-start | bytes 1572872 | tf_op jit(solution)/shard_map/ppermute | solution.py:36
  62.6 5.0 %collective-permute-start.14 = (bf16[128,512]{1,0:T(8,128)(2,1)S(1)}, bf16[128,512]{1,0:T(8,128)(2,1)S(1)}, u32[]{:S(2)}, u32[]{:S(2)}) collective-permute-start(bf16[128,512]{1,0:T(8,128)(2,1)S(1)} %get-tuple-element.57), channel_id=1, source_target_pairs={{0,96},{1,97},{2,98},{3,99},{4,100},{5,101},{6,102},{7,103},{8,104... | collective-permute-start | bytes 393224 | tf_op jit(solution)/shard_map/ppermute | solution.py:41
  62.9 6.7 %collective-permute-start.15 = (bf16[128,512]{1,0:T(8,128)(2,1)S(1)}, bf16[128,512]{1,0:T(8,128)(2,1)S(1)}, u32[]{:S(2)}, u32[]{:S(2)}) collective-permute-start(bf16[128,512]{1,0:T(8,128)(2,1)S(1)} %get-tuple-element.58), channel_id=1, source_target_pairs={{0,64},{1,65},{2,66},{3,67},{4,68},{5,69},{6,70},{7,71},{8,72},{9,... | collective-permute-start | bytes 393224 | tf_op jit(solution)/shard_map/ppermute | solution.py:41
  65.8 9.6 %collective-permute-start.20 = (bf16[128,512]{1,0:T(8,128)(2,1)S(1)}, bf16[128,512]{1,0:T(8,128)(2,1)S(1)}, u32[]{:S(2)}, u32[]{:S(2)}) collective-permute-start(bf16[128,512]{1,0:T(8,128)(2,1)S(1)} %get-tuple-element.68), channel_id=1, source_target_pairs={{0,32},{1,33},{2,34},{3,35},{4,36},{5,37},{6,38},{7,39},{8,40},{9,... | collective-permute-start | bytes 393224 | tf_op jit(solution)/shard_map/ppermute | solution.py:41
  71.5 16.6 %collective-permute-start.17 = (bf16[16,8192]{1,0:T(8,128)(2,1)S(1)}, bf16[16,8192]{1,0:T(8,128)(2,1)S(1)}, u32[]{:S(2)}, u32[]{:S(2)}) collective-permute-start(bf16[16,8192]{1,0:T(8,128)(2,1)S(1)} %get-tuple-element.62), channel_id=1, source_target_pairs={{0,4},{1,5},{2,6},{3,7},{4,8},{5,9},{6,10},{7,11},{8,12},{9,13},{1... | collective-permute-start | bytes 786440 | tf_op jit(solution)/shard_map/ppermute | solution.py:36
  71.6 16.5 %collective-permute-start.18 = (bf16[16,8192]{1,0:T(8,128)(2,1)S(1)}, bf16[16,8192]{1,0:T(8,128)(2,1)S(1)}, u32[]{:S(2)}, u32[]{:S(2)}) collective-permute-start(bf16[16,8192]{1,0:T(8,128)(2,1)S(1)} %get-tuple-element.63), channel_id=1, source_target_pairs={{0,8},{1,9},{2,10},{3,11},{4,12},{5,13},{6,14},{7,15},{8,0},{9,1},... | collective-permute-start | bytes 786440 | tf_op jit(solution)/shard_map/ppermute | solution.py:36
  74.2 13.9 %collective-permute-start.19 = (bf16[16,8192]{1,0:T(8,128)(2,1)S(1)}, bf16[16,8192]{1,0:T(8,128)(2,1)S(1)}, u32[]{:S(2)}, u32[]{:S(2)}) collective-permute-start(bf16[16,8192]{1,0:T(8,128)(2,1)S(1)} %get-tuple-element.64), channel_id=1, source_target_pairs={{0,12},{1,13},{2,14},{3,15},{4,0},{5,1},{6,2},{7,3},{8,4},{9,5},{1... | collective-permute-start | bytes 786440 | tf_op jit(solution)/shard_map/ppermute | solution.py:36

commit v5 on v4

--- a/solution.py
+++ b/solution.py
@@ -76,12 +76,18 @@
         at = pl.ds(step * AT_ONCE, AT_ONCE)
         return pltpu.make_async_copy(far.at[at], near.at[at], sem.at[step])
 
-    for step in range(steps):
+    for step in range(steps - 1):
         copy(step, k_hbm, k_ref, k_sem).start()
         copy(step, v_hbm, v_ref, v_sem).start()
 
     def one_step(step, carry):
         copy(step, k_hbm, k_ref, k_sem).wait()
+
+        @pl.when(step == 0)
+        def _():
+            copy(steps - 1, k_hbm, k_ref, k_sem).start()
+            copy(steps - 1, v_hbm, v_ref, v_sem).start()
+
         all_scores = []
         for item in range(AT_ONCE):
             row = step * AT_ONCE + item
@@ -240,37 +246,21 @@
     )(order, features, weight)
 
 
-def meet_kernel(ahead_hbm, back_hbm, came_ahead, came_back, ahead_ref, back_ref, *scratch):
-    ahead_last, back_last, sem = scratch
-    half = ahead_ref.shape[1]
-    copies = (
-        pltpu.make_async_copy(ahead_hbm, ahead_last, sem.at[0]),
-        pltpu.make_async_copy(back_hbm, back_last, sem.at[1]),
-    )
-    for copy in copies:
-        copy.start()
-    copies[0].wait()
-    ahead_ref[...] = (ahead_last[...].astype(F32) + came_ahead[:, :half].astype(F32)).astype(BF16)
-    copies[1].wait()
-    back_ref[...] = (back_last[...].astype(F32) + came_back[:, half:].astype(F32)).astype(BF16)
-
-
-def meet(*operands):
-    half = operands[0]
-    return pl.pallas_call(
-        meet_kernel,
+def meet_kernel(last, came, o_ref, *, first):
+    came_half = came[:, first : first + o_ref.shape[1]]
+    o_ref[...] = (last[...].astype(F32) + came_half.astype(F32)).astype(BF16)
+
+
+def meet(last, came, first):
+    return pl.pallas_call(
+        lambda *refs: meet_kernel(*refs, first=first),
         name="meet",
-        out_shape=[jax.ShapeDtypeStruct(half.shape, BF16)] * 2,
-        in_specs=[pl.BlockSpec(memory_space=pl.ANY)] * 2 + whole(2),
-        out_specs=whole(2),
-        scratch_shapes=[
-            pltpu.VMEM(half.shape, BF16),
-            pltpu.VMEM(half.shape, BF16),
-            pltpu.SemaphoreType.DMA((2,)),
-        ],
+        out_shape=jax.ShapeDtypeStruct(last.shape, BF16),
+        in_specs=whole(2),
+        out_specs=whole(1)[0],
         compiler_params=pltpu.CompilerParams(vmem_limit_bytes=VMEM_BYTES),
         cost_estimate=pl.CostEstimate(flops=2**20, bytes_accessed=2**22, transcendentals=0),
-    )(*operands)
+    )(last, came)
 
 
 def join_kernel(own, came_ahead, came_back, ahead_last, back_last, *outs):
@@ -532,8 +522,9 @@
     near = [pass_plane(shrunk, "yx", k) for k in range(1, SIDE)]
     shrunk = wide_sum(shrunk, *near).astype(BF16)
     near = [pass_plane(shrunk, "xy", k) for k in range(1, SIDE)]
-    ahead_last, back_last = meet(ahead_last, back_last, came_ahead, came_back)
-    *near, ahead_last, back_last = lax.optimization_barrier((*near, ahead_last, back_last))
+    back_last = meet(back_last, came_back, back_last.shape[1])
+    ahead_last = meet(ahead_last, came_ahead, 0)
+    *near, ahead_last = lax.optimization_barrier((*near, ahead_last))
     shrunk = wide_sum(shrunk, *near).astype(BF16)
     ahead_last, back_last = pass_plane(ahead_last, "xy", 1), pass_plane(back_last, "xy", -1)
     grown = grow(shrunk, up_own, up_other, per_z)

time: 89.4 us -> 89 us (level)
  starting transfers between devices: 31.3 us -> 32.4 us
  blocking collectives: 12.2 us -> 11.3 us
    ppermute x6, waiting for transfers between devices: 3.82 us -> 1.59 us  [pass_z(): return lax.ppermute(value, BOTH, pairs)]
    ppermute x13, waiting for transfers between devices: 10.8 us -> 12.4 us  [pass_plane(): return lax.ppermute(value, BOTH, pairs)]
    ppermute x13, starting transfers between devices: 13.8 us -> 14.9 us  [pass_plane(): return lax.ppermute(value, BOTH, pairs)]
    all_to_all x1, blocking collectives: 12.2 us -> 11.3 us  [body(): delta = lax.all_to_all(delta, 'tp', split_axis=0, concat_axis=0, tiled=True)]
where the time goes in v5:
time: 89 us; the launch traced here: 88.6 us
  starting transfers between devices  32.4 us (36%)
  waiting for transfers between devices  21.5 us (24%)
  Pallas kernels  19.6 us (22%)
  blocking collectives  11.3 us (13%)
  local copies, waits for them, and re-layouts  3.39 us (4%)
    ppermute x13, starting transfers between devices, pass_plane(): return lax.ppermute(value, BOTH, pairs)  14.9 us
    ppermute x13, waiting for transfers between devices, pass_plane(): return lax.ppermute(value, BOTH, pairs)  12.4 us
    all_to_all x1, blocking collectives, body(): delta = lax.all_to_all(delta, 'tp', split_axis=0, concat_axis=0, tiled=True)  11.3 us
    ppermute x6, starting transfers between devices, pass_z(): return lax.ppermute(value, BOTH, pairs)  9.73 us
    pallas_call x1, Pallas kernels, attend(): pl.pallas_call(attend_kernel, name='attend', out_shape=jax.ShapeDtypeStru...  9.3 us
    all_to_all x1, waiting for transfers between devices, body(): lax.all_to_all(attended, 'tp', split_axis=0, concat_axis=0, tiled=True)  7.42 us
    all_to_all x1, starting transfers between devices, body(): lax.all_to_all(attended, 'tp', split_axis=0, concat_axis=0, tiled=True)  7.26 us
    pallas_call x1, Pallas kernels, project(): pl.pallas_call(project_kernel, name='project', out_shape=[full, full, ful...  6.72 us
  transfers between devices with their start and end apart: 22, of which 9 were waited for; matrix products, arithmetic and copies ran while one was open for 2% of the time, Pallas kernels for 21%

profile of v5, /device:TPU:0, one launch (start us, length us, event | category | flops | bytes accessed | tf_op | source)
XLA Modules:
  0.0 88.6 jit_solution(13529980160723601109)
XLA Ops:
  0.0 0.5 collective-permute-start.1
  0.5 9.3 %attend.1 = bf16[16,16,512]{2,1,0:T(8,128)(2,1)} custom-call(s32[16]{0:T(128)} %lengths_ref.1, bf16[16,64,128]{2,1,0:T(8,128)(2,1)} %q_ref.1, bf16[16,8,256,128]{3,2,1,0:T(8,128)(2,1)} %k_hbm.1, bf16[16,8,256,128]{3,2,1,0:T(8,128)(2,1)} %v_hbm.1, bf16[16,8,128]{2,1,0:T(8,128)(2,1)} %fk_ref.1, bf16[16,8,128]{2,1,0:T(8,128)(2,1)} %fv_ref.1), custom_call_target="tpu_custom_call" | custom-call | flops 134217728 | bytes 16777216 | tf_op jit(solution)/shard_map/attend/pallas_call | solution.py:147
  9.8 7.3 %all-to-all-start = ((bf16[16,16,512]{2,1,0:T(8,128)(2,1)}), bf16[16,16,512]{2,1,0:T(8,128)(2,1)S(1)}, u32[]{:S(2)}, u32[]{:S(2)}) async-start(bf16[16,16,512]{2,1,0:T(8,128)(2,1)} %attend.1), calls=%async_computation | async-start | bytes 524288 | tf_op jit(solution)/shard_map/all_to_all | solution.py:511
  17.3 1.3 %dynamic-slice_bitcast_fusion.order_ref = s32[16]{0:T(128)} fusion(s32[128,16]{1,0:T(8,128)} %constant.89.clone, s32[]{:T(128)S(6)} %select_n.71), kind=kLoop, calls=%fused_computation.27 | loop fusion | bytes 132 | tf_op jit(solution)/shard_map/squeeze | solution.py:506
  18.6 7.4 %all-to-all-done.f_ref = bf16[16,16,512]{2,1,0:T(8,128)(2,1)S(1)} async-done(((bf16[16,16,512]{2,1,0:T(8,128)(2,1)}), bf16[16,16,512]{2,1,0:T(8,128)(2,1)S(1)}, u32[]{:S(2)}, u32[]{:S(2)}) %all-to-all-start) | async-done | bytes 262176 | tf_op jit(solution)/shard_map/all_to_all | solution.py:511
  26.4 2.0 %collective-permute-start.2 = (bf16[128,512]{1,0:T(8,128)(2,1)S(1)}, bf16[128,512]{1,0:T(8,128)(2,1)S(1)}, u32[]{:S(2)}, u32[]{:S(2)}) collective-permute-start(bf16[128,512]{1,0:T(8,128)(2,1)S(1)} %get-tuple-element.37), channel_id=1, source_target_pairs={{0,32},{1,33},{2,34},{3,35},{4,36},{5,37},{6,38},{7,39},{8,40},{9,... | collective-permute-start | bytes 393224 | tf_op jit(solution)/shard_map/ppermute | solution.py:41
  28.4 3.6 %collective-permute-start.3 = (bf16[128,512]{1,0:T(8,128)(2,1)S(1)}, bf16[128,512]{1,0:T(8,128)(2,1)S(1)}, u32[]{:S(2)}, u32[]{:S(2)}) collective-permute-start(bf16[128,512]{1,0:T(8,128)(2,1)S(1)} %get-tuple-element.38), channel_id=1, source_target_pairs={{0,64},{1,65},{2,66},{3,67},{4,68},{5,69},{6,70},{7,71},{8,72},{9,... | collective-permute-start | bytes 393224 | tf_op jit(solution)/shard_map/ppermute | solution.py:41
  31.9 1.0 %collective-permute-start.4 = (bf16[128,512]{1,0:T(8,128)(2,1)S(1)}, bf16[128,512]{1,0:T(8,128)(2,1)S(1)}, u32[]{:S(2)}, u32[]{:S(2)}) collective-permute-start(bf16[128,512]{1,0:T(8,128)(2,1)S(1)} %get-tuple-element.39), channel_id=1, source_target_pairs={{0,96},{1,97},{2,98},{3,99},{4,100},{5,101},{6,102},{7,103},{8,104... | collective-permute-start | bytes 393224 | tf_op jit(solution)/shard_map/ppermute | solution.py:41
  33.0 6.7 %project.1 = (bf16[64,8192]{1,0:T(8,128)(2,1)}, bf16[64,8192]{1,0:T(8,128)(2,1)}, bf16[64,8192]{1,0:T(8,128)(2,1)}, bf16[64,4096]{1,0:T(8,128)(2,1)}, bf16[64,4096]{1,0:T(8,128)(2,1)}) custom-call(s32[16]{0:T(128)} %dynamic-slice_bitcast_fusion.order_ref, bf16[16,16,512]{2,1,0:T(8,128)(2,1)} %copy-done, bf16[512,8192]{1,0:T(8,128)(2,1)} %w_hbm.1), custom_call_target="tpu_custom_call" | custom-call | flops 2147483648 | bytes 12582912 | tf_op jit(solution)/shard_map/project/pallas_call | solution.py:223
  39.7 0.8 collective-permute-start.6
  40.5 1.3 %collective-permute-start.5 = (bf16[64,8192]{1,0:T(8,128)(2,1)}, bf16[64,8192]{1,0:T(8,128)(2,1)S(1)}, u32[]{:S(2)}, u32[]{:S(2)}) collective-permute-start(bf16[64,8192]{1,0:T(8,128)(2,1)} %get-tuple-element.40), channel_id=1, source_target_pairs={{0,1},{1,2},{2,3},{3,0},{4,5},{5,6},{6,7},{7,4},{8,9},{9,10},{10,1... | collective-permute-start | bytes 3145736 | tf_op jit(solution)/shard_map/ppermute | solution.py:36
  41.9 0.8 shrink.1
  42.6 0.9 %collective-permute-start.9 = (bf16[256,128]{1,0:T(8,128)(2,1)S(1)}, bf16[256,128]{1,0:T(8,128)(2,1)S(1)}, u32[]{:S(2)}, u32[]{:S(2)}) collective-permute-start(bf16[256,128]{1,0:T(8,128)(2,1)S(1)} %shrink.1), channel_id=1, source_target_pairs={{0,12},{1,13},{2,14},{3,15},{4,0},{5,1},{6,2},{7,3},{8,4},{9,5},{1... | collective-permute-start | bytes 196616 | tf_op jit(solution)/shard_map/ppermute | solution.py:36
  43.6 1.3 %collective-permute-start.8 = (bf16[256,128]{1,0:T(8,128)(2,1)S(1)}, bf16[256,128]{1,0:T(8,128)(2,1)S(1)}, u32[]{:S(2)}, u32[]{:S(2)}) collective-permute-start(bf16[256,128]{1,0:T(8,128)(2,1)S(1)} %shrink.1), channel_id=1, source_target_pairs={{0,8},{1,9},{2,10},{3,11},{4,12},{5,13},{6,14},{7,15},{8,0},{9,1},... | collective-permute-start | bytes 196616 | tf_op jit(solution)/shard_map/ppermute | solution.py:36
  45.0 2.8 %collective-permute-done.9 = bf16[256,128]{1,0:T(8,128)(2,1)S(1)} collective-permute-done((bf16[256,128]{1,0:T(8,128)(2,1)S(1)}, bf16[256,128]{1,0:T(8,128)(2,1)S(1)}, u32[]{:S(2)}, u32[]{:S(2)}) %collective-permute-start.9) | collective-permute-done | bytes 65568 | tf_op jit(solution)/shard_map/ppermute | solution.py:36
  47.7 2.4 %collective-permute-done.8 = bf16[256,128]{1,0:T(8,128)(2,1)S(1)} collective-permute-done((bf16[256,128]{1,0:T(8,128)(2,1)S(1)}, bf16[256,128]{1,0:T(8,128)(2,1)S(1)}, u32[]{:S(2)}, u32[]{:S(2)}) %collective-permute-start.8) | collective-permute-done | bytes 65568 | tf_op jit(solution)/shard_map/ppermute | solution.py:36
  50.1 1.2 %collective-permute-done.7 = bf16[256,128]{1,0:T(8,128)(2,1)S(1)} collective-permute-done((bf16[256,128]{1,0:T(8,128)(2,1)S(1)}, bf16[256,128]{1,0:T(8,128)(2,1)S(1)}, u32[]{:S(2)}, u32[]{:S(2)}) %collective-permute-start.7) | collective-permute-done | bytes 65568 | tf_op jit(solution)/shard_map/ppermute | solution.py:36
  51.4 2.4 %collective-permute-start.12 = (bf16[256,128]{1,0:T(8,128)(2,1)S(1)}, bf16[256,128]{1,0:T(8,128)(2,1)S(1)}, u32[]{:S(2)}, u32[]{:S(2)}) collective-permute-start(bf16[256,128]{1,0:T(8,128)(2,1)S(1)} %add_convert_fusion.1), channel_id=1, source_target_pairs={{0,3},{1,0},{2,1},{3,2},{4,7},{5,4},{6,5},{7,6},{8,11},{9,8},{10,9... | collective-permute-start | bytes 196616 | tf_op jit(solution)/shard_map/ppermute | solution.py:36
  53.9 0.8 collective-permute-start.10
  54.7 0.8 collective-permute-done.6.refs_1_.came_back
  55.5 1.0 %copy-done.5 = bf16[64,4096]{1,0:T(8,128)(2,1)S(1)} copy-done((bf16[64,4096]{1,0:T(8,128)(2,1)S(1)}, bf16[64,4096]{1,0:T(8,128)(2,1)}, u32[]{:S(2)}) %copy-start.5) | copy-done | bytes 524312
  56.6 2.1 %collective-permute-start.16 = (bf16[64,4096]{1,0:T(8,128)(2,1)S(1)}, bf16[64,4096]{1,0:T(8,128)(2,1)S(1)}, u32[]{:S(2)}, u32[]{:S(2)}) collective-permute-start(bf16[64,4096]{1,0:T(8,128)(2,1)S(1)} %meet.3), channel_id=1, source_target_pairs={{0,3},{1,0},{2,1},{3,2},{4,7},{5,4},{6,5},{7,6},{8,11},{9,8},{10,9... | collective-permute-start | bytes 1572872 | tf_op jit(solution)/shard_map/ppermute | solution.py:36
  58.7 1.0 %copy-done.4 = bf16[64,4096]{1,0:T(8,128)(2,1)S(1)} copy-done((bf16[64,4096]{1,0:T(8,128)(2,1)S(1)}, bf16[64,4096]{1,0:T(8,128)(2,1)}, u32[]{:S(2)}) %copy-start.4) | copy-done | bytes 524312
  60.9 2.9 %collective-permute-start.15 = (bf16[128,512]{1,0:T(8,128)(2,1)S(1)}, bf16[128,512]{1,0:T(8,128)(2,1)S(1)}, u32[]{:S(2)}, u32[]{:S(2)}) collective-permute-start(bf16[128,512]{1,0:T(8,128)(2,1)S(1)} %get-tuple-element.52), channel_id=1, source_target_pairs={{0,64},{1,65},{2,66},{3,67},{4,68},{5,69},{6,70},{7,71},{8,72},{9,... | collective-permute-start | bytes 393224 | tf_op jit(solution)/shard_map/ppermute | solution.py:41
  63.8 2.1 %collective-permute-done.16.back_last = bf16[64,4096]{1,0:T(8,128)(2,1)S(1)} collective-permute-done((bf16[64,4096]{1,0:T(8,128)(2,1)S(1)}, bf16[64,4096]{1,0:T(8,128)(2,1)S(1)}, u32[]{:S(2)}, u32[]{:S(2)}) %collective-permute-start.16) | collective-permute-done | bytes 524320 | tf_op jit(solution)/shard_map/ppermute | solution.py:36
  65.9 1.6 %collective-permute-done.15.r2 = bf16[128,512]{1,0:T(8,128)(2,1)S(1)} collective-permute-done((bf16[128,512]{1,0:T(8,128)(2,1)S(1)}, bf16[128,512]{1,0:T(8,128)(2,1)S(1)}, u32[]{:S(2)}, u32[]{:S(2)}) %collective-permute-start.15) | collective-permute-done | bytes 131104 | tf_op jit(solution)/shard_map/ppermute | solution.py:41
  67.5 3.0 %collective-permute-done.13.ahead_last = bf16[64,4096]{1,0:T(8,128)(2,1)S(1)} collective-permute-done((bf16[64,4096]{1,0:T(8,128)(2,1)S(1)}, bf16[64,4096]{1,0:T(8,128)(2,1)S(1)}, u32[]{:S(2)}, u32[]{:S(2)}) %collective-permute-start.13) | collective-permute-done | bytes 524320 | tf_op jit(solution)/shard_map/ppermute | solution.py:36
  70.8 0.6 collective-permute-start.17
  71.5 3.6 %collective-permute-start.18 = (bf16[16,8192]{1,0:T(8,128)(2,1)S(1)}, bf16[16,8192]{1,0:T(8,128)(2,1)S(1)}, u32[]{:S(2)}, u32[]{:S(2)}) collective-permute-start(bf16[16,8192]{1,0:T(8,128)(2,1)S(1)} %get-tuple-element.57), channel_id=1, source_target_pairs={{0,8},{1,9},{2,10},{3,11},{4,12},{5,13},{6,14},{7,15},{8,0},{9,1},... | collective-permute-start | bytes 786440 | tf_op jit(solution)/shard_map/ppermute | solution.py:36
  75.1 0.8 collective-permute-start.19
  76.3 11.3 %all_to_all.10.delta_ref = bf16[16,16,512]{2,1,0:T(8,128)(2,1)S(1)} all-to-all(bf16[16,16,512]{2,1,0:T(8,128)(2,1)S(1)} %collect.1), channel_id=1, replica_groups=mesh['rep'=8,'tp'=16] {'tp'}, dimensions={0} | all-to-all | bytes 524288 | tf_op jit(solution)/shard_map/all_to_all | solution.py:537
  87.6 0.9 %finish.1 = bf16[16,8192]{1,0:T(8,128)(2,1)} custom-call(bf16[16,8192]{1,0:T(8,128)(2,1)S(1)} %copy-done.6, bf16[16,8192]{1,0:T(8,128)(2,1)S(1)} %get-tuple-element.55.s_ref, bf16[16,8192]{1,0:T(8,128)(2,1)S(1)} %collective-permute-done.17.a_ref, bf16[16,8192]{1,0:T(8,128)(2,1)S(1)} %collective-permute-done.18.b_ref, ...), custom_call_target="tpu_custom_call" | custom-call | flops 1048576 | bytes 2097152 | tf_op jit(solution)/shard_map/finish/pallas_call | solution.py:446
  (44 shorter events, 3.0 us)
Async XLA Ops:
  0.0 26.0 %collective-permute-start = (bf16[1024,512]{1,0:T(8,128)(2,1)}, bf16[1024,512]{1,0:T(8,128)(2,1)S(1)}, u32[]{:S(2)}, u32[]{:S(2)}) collective-permute-start(bf16[1024,512]{1,0:T(8,128)(2,1)} %bitcast.27), channel_id=1, source_target_pairs={{0,16},{1,17},{2,18},{3,19},{4,20},{5,21},{6,22},{7,23},{8,24},{9,... | collective-permute-start | bytes 3145736 | tf_op jit(solution)/shard_map/ppermute | solution.py:45
  0.0 17.1 %copy-start.7 = (s32[256,1]{0,1:T(1,128)S(1)}, s32[256,1]{0,1:T(1,128)}, u32[]{:S(2)}) copy-start(s32[256,1]{0,1:T(1,128)} %param.18) | copy-start | bytes 3076
  0.0 26.0 %collective-permute-start.1 = (bf16[1024,512]{1,0:T(8,128)(2,1)}, bf16[1024,512]{1,0:T(8,128)(2,1)S(1)}, u32[]{:S(2)}, u32[]{:S(2)}) collective-permute-start(bf16[1024,512]{1,0:T(8,128)(2,1)} %bitcast.25), channel_id=1, source_target_pairs={{0,16},{1,17},{2,18},{3,19},{4,20},{5,21},{6,22},{7,23},{8,24},{9,... | collective-permute-start | bytes 3145736 | tf_op jit(solution)/shard_map/ppermute | solution.py:45
  9.8 32.1 %copy-start.2 = (bf16[16,512,64]{1,2,0:T(8,128)(2,1)S(1)}, bf16[16,512,64]{1,2,0:T(8,128)(2,1)}, u32[]{:S(2)}) copy-start(bf16[16,512,64]{1,2,0:T(8,128)(2,1)} %param.21) | copy-start | bytes 3145732
  9.8 16.2 %all-to-all-start = ((bf16[16,16,512]{2,1,0:T(8,128)(2,1)}), bf16[16,16,512]{2,1,0:T(8,128)(2,1)S(1)}, u32[]{:S(2)}, u32[]{:S(2)}) async-start(bf16[16,16,512]{2,1,0:T(8,128)(2,1)} %attend.1), calls=%async_computation | async-start | bytes 524288 | tf_op jit(solution)/shard_map/all_to_all | solution.py:511
  26.0 6.9 %copy-start = (bf16[16,16,512]{2,1,0:T(8,128)(2,1)}, bf16[16,16,512]{2,1,0:T(8,128)(2,1)S(1)}, u32[]{:S(2)}) copy-start(bf16[16,16,512]{2,1,0:T(8,128)(2,1)S(1)} %all-to-all-done.f_ref) | copy-start | bytes 786436
  26.4 33.8 %copy-start.1 = (bf16[16,64,512]{2,1,0:T(8,128)(2,1)S(1)}, bf16[16,64,512]{2,1,0:T(8,128)(2,1)}, u32[]{:S(2)}) copy-start(bf16[16,64,512]{2,1,0:T(8,128)(2,1)} %param.22) | copy-start | bytes 3145732
  26.4 14.2 %collective-permute-start.2 = (bf16[128,512]{1,0:T(8,128)(2,1)S(1)}, bf16[128,512]{1,0:T(8,128)(2,1)S(1)}, u32[]{:S(2)}, u32[]{:S(2)}) collective-permute-start(bf16[128,512]{1,0:T(8,128)(2,1)S(1)} %get-tuple-element.37), channel_id=1, source_target_pairs={{0,32},{1,33},{2,34},{3,35},{4,36},{5,37},{6,38},{7,39},{8,40},{9,... | collective-permute-start | bytes 393224 | tf_op jit(solution)/shard_map/ppermute | solution.py:41
  28.4 12.2 %collective-permute-start.3 = (bf16[128,512]{1,0:T(8,128)(2,1)S(1)}, bf16[128,512]{1,0:T(8,128)(2,1)S(1)}, u32[]{:S(2)}, u32[]{:S(2)}) collective-permute-start(bf16[128,512]{1,0:T(8,128)(2,1)S(1)} %get-tuple-element.38), channel_id=1, source_target_pairs={{0,64},{1,65},{2,66},{3,67},{4,68},{5,69},{6,70},{7,71},{8,72},{9,... | collective-permute-start | bytes 393224 | tf_op jit(solution)/shard_map/ppermute | solution.py:41
  31.9 8.6 %collective-permute-start.4 = (bf16[128,512]{1,0:T(8,128)(2,1)S(1)}, bf16[128,512]{1,0:T(8,128)(2,1)S(1)}, u32[]{:S(2)}, u32[]{:S(2)}) collective-permute-start(bf16[128,512]{1,0:T(8,128)(2,1)S(1)} %get-tuple-element.39), channel_id=1, source_target_pairs={{0,96},{1,97},{2,98},{3,99},{4,100},{5,101},{6,102},{7,103},{8,104... | collective-permute-start | bytes 393224 | tf_op jit(solution)/shard_map/ppermute | solution.py:41
  39.7 30.8 %copy-start.3 = (bf16[64,8192]{1,0:T(8,128)(2,1)S(1)}, bf16[64,8192]{1,0:T(8,128)(2,1)}, u32[]{:S(2)}) copy-start(bf16[64,8192]{1,0:T(8,128)(2,1)} %get-tuple-element.34.own) | copy-start | bytes 3145732
  39.7 47.9 %copy-start.6 = (bf16[16,8192]{1,0:T(8,128)(2,1)S(1)}, bf16[16,8192]{1,0:T(8,128)(2,1)}, u32[]{:S(2)}) copy-start(bf16[16,8192]{1,0:T(8,128)(2,1)} %skip_ref.1) | copy-start | bytes 786436
  39.7 15.8 %collective-permute-start.6 = (bf16[64,8192]{1,0:T(8,128)(2,1)}, bf16[64,8192]{1,0:T(8,128)(2,1)S(1)}, u32[]{:S(2)}, u32[]{:S(2)}) collective-permute-start(bf16[64,8192]{1,0:T(8,128)(2,1)} %get-tuple-element.41), channel_id=1, source_target_pairs={{0,3},{1,0},{2,1},{3,2},{4,7},{5,4},{6,5},{7,6},{8,11},{9,8},{10,9... | collective-permute-start | bytes 3145736 | tf_op jit(solution)/shard_map/ppermute | solution.py:36
  40.5 18.1 %collective-permute-start.5 = (bf16[64,8192]{1,0:T(8,128)(2,1)}, bf16[64,8192]{1,0:T(8,128)(2,1)S(1)}, u32[]{:S(2)}, u32[]{:S(2)}) collective-permute-start(bf16[64,8192]{1,0:T(8,128)(2,1)} %get-tuple-element.40), channel_id=1, source_target_pairs={{0,1},{1,2},{2,3},{3,0},{4,5},{5,6},{6,7},{7,4},{8,9},{9,10},{10,1... | collective-permute-start | bytes 3145736 | tf_op jit(solution)/shard_map/ppermute | solution.py:36
  42.6 5.1 %collective-permute-start.9 = (bf16[256,128]{1,0:T(8,128)(2,1)S(1)}, bf16[256,128]{1,0:T(8,128)(2,1)S(1)}, u32[]{:S(2)}, u32[]{:S(2)}) collective-permute-start(bf16[256,128]{1,0:T(8,128)(2,1)S(1)} %shrink.1), channel_id=1, source_target_pairs={{0,12},{1,13},{2,14},{3,15},{4,0},{5,1},{6,2},{7,3},{8,4},{9,5},{1... | collective-permute-start | bytes 196616 | tf_op jit(solution)/shard_map/ppermute | solution.py:36
  43.6 6.5 %collective-permute-start.8 = (bf16[256,128]{1,0:T(8,128)(2,1)S(1)}, bf16[256,128]{1,0:T(8,128)(2,1)S(1)}, u32[]{:S(2)}, u32[]{:S(2)}) collective-permute-start(bf16[256,128]{1,0:T(8,128)(2,1)S(1)} %shrink.1), channel_id=1, source_target_pairs={{0,8},{1,9},{2,10},{3,11},{4,12},{5,13},{6,14},{7,15},{8,0},{9,1},... | collective-permute-start | bytes 196616 | tf_op jit(solution)/shard_map/ppermute | solution.py:36
  44.8 6.5 %collective-permute-start.7 = (bf16[256,128]{1,0:T(8,128)(2,1)S(1)}, bf16[256,128]{1,0:T(8,128)(2,1)S(1)}, u32[]{:S(2)}, u32[]{:S(2)}) collective-permute-start(bf16[256,128]{1,0:T(8,128)(2,1)S(1)} %shrink.1), channel_id=1, source_target_pairs={{0,4},{1,5},{2,6},{3,7},{4,8},{5,9},{6,10},{7,11},{8,12},{9,13},{1... | collective-permute-start | bytes 196616 | tf_op jit(solution)/shard_map/ppermute | solution.py:36
  51.4 8.5 %collective-permute-start.12 = (bf16[256,128]{1,0:T(8,128)(2,1)S(1)}, bf16[256,128]{1,0:T(8,128)(2,1)S(1)}, u32[]{:S(2)}, u32[]{:S(2)}) collective-permute-start(bf16[256,128]{1,0:T(8,128)(2,1)S(1)} %add_convert_fusion.1), channel_id=1, source_target_pairs={{0,3},{1,0},{2,1},{3,2},{4,7},{5,4},{6,5},{7,6},{8,11},{9,8},{10,9... | collective-permute-start | bytes 196616 | tf_op jit(solution)/shard_map/ppermute | solution.py:36
  53.7 6.1 %collective-permute-start.11 = (bf16[256,128]{1,0:T(8,128)(2,1)S(1)}, bf16[256,128]{1,0:T(8,128)(2,1)S(1)}, u32[]{:S(2)}, u32[]{:S(2)}) collective-permute-start(bf16[256,128]{1,0:T(8,128)(2,1)S(1)} %add_convert_fusion.1), channel_id=1, source_target_pairs={{0,2},{1,3},{2,0},{3,1},{4,6},{5,7},{6,4},{7,5},{8,10},{9,11},{10,... | collective-permute-start | bytes 196616 | tf_op jit(solution)/shard_map/ppermute | solution.py:36
  53.9 6.2 %collective-permute-start.10 = (bf16[256,128]{1,0:T(8,128)(2,1)S(1)}, bf16[256,128]{1,0:T(8,128)(2,1)S(1)}, u32[]{:S(2)}, u32[]{:S(2)}) collective-permute-start(bf16[256,128]{1,0:T(8,128)(2,1)S(1)} %add_convert_fusion.1), channel_id=1, source_target_pairs={{0,1},{1,2},{2,3},{3,0},{4,5},{5,6},{6,7},{7,4},{8,9},{9,10},{10,1... | collective-permute-start | bytes 196616 | tf_op jit(solution)/shard_map/ppermute | solution.py:36
  55.5 1.0 %copy-start.5 = (bf16[64,4096]{1,0:T(8,128)(2,1)S(1)}, bf16[64,4096]{1,0:T(8,128)(2,1)}, u32[]{:S(2)}) copy-start(bf16[64,4096]{1,0:T(8,128)(2,1)} %get-tuple-element.53.refs_0_) | copy-start | bytes 1572868
  56.6 9.2 %collective-permute-start.16 = (bf16[64,4096]{1,0:T(8,128)(2,1)S(1)}, bf16[64,4096]{1,0:T(8,128)(2,1)S(1)}, u32[]{:S(2)}, u32[]{:S(2)}) collective-permute-start(bf16[64,4096]{1,0:T(8,128)(2,1)S(1)} %meet.3), channel_id=1, source_target_pairs={{0,3},{1,0},{2,1},{3,2},{4,7},{5,4},{6,5},{7,6},{8,11},{9,8},{10,9... | collective-permute-start | bytes 1572872 | tf_op jit(solution)/shard_map/ppermute | solution.py:36
  58.7 1.0 %copy-start.4 = (bf16[64,4096]{1,0:T(8,128)(2,1)S(1)}, bf16[64,4096]{1,0:T(8,128)(2,1)}, u32[]{:S(2)}) copy-start(bf16[64,4096]{1,0:T(8,128)(2,1)} %get-tuple-element.46.refs_0_) | copy-start | bytes 1572868
  60.1 10.4 %collective-permute-start.13 = (bf16[64,4096]{1,0:T(8,128)(2,1)S(1)}, bf16[64,4096]{1,0:T(8,128)(2,1)S(1)}, u32[]{:S(2)}, u32[]{:S(2)}) collective-permute-start(bf16[64,4096]{1,0:T(8,128)(2,1)S(1)} %meet.2), channel_id=1, source_target_pairs={{0,1},{1,2},{2,3},{3,0},{4,5},{5,6},{6,7},{7,4},{8,9},{9,10},{10,1... | collective-permute-start | bytes 1572872 | tf_op jit(solution)/shard_map/ppermute | solution.py:36
  60.6 5.3 %collective-permute-start.14 = (bf16[128,512]{1,0:T(8,128)(2,1)S(1)}, bf16[128,512]{1,0:T(8,128)(2,1)S(1)}, u32[]{:S(2)}, u32[]{:S(2)}) collective-permute-start(bf16[128,512]{1,0:T(8,128)(2,1)S(1)} %get-tuple-element.51), channel_id=1, source_target_pairs={{0,96},{1,97},{2,98},{3,99},{4,100},{5,101},{6,102},{7,103},{8,104... | collective-permute-start | bytes 393224 | tf_op jit(solution)/shard_map/ppermute | solution.py:41
  60.9 6.6 %collective-permute-start.15 = (bf16[128,512]{1,0:T(8,128)(2,1)S(1)}, bf16[128,512]{1,0:T(8,128)(2,1)S(1)}, u32[]{:S(2)}, u32[]{:S(2)}) collective-permute-start(bf16[128,512]{1,0:T(8,128)(2,1)S(1)} %get-tuple-element.52), channel_id=1, source_target_pairs={{0,64},{1,65},{2,66},{3,67},{4,68},{5,69},{6,70},{7,71},{8,72},{9,... | collective-permute-start | bytes 393224 | tf_op jit(solution)/shard_map/ppermute | solution.py:41
  63.8 12.1 %collective-permute-start.20 = (bf16[128,512]{1,0:T(8,128)(2,1)S(1)}, bf16[128,512]{1,0:T(8,128)(2,1)S(1)}, u32[]{:S(2)}, u32[]{:S(2)}) collective-permute-start(bf16[128,512]{1,0:T(8,128)(2,1)S(1)} %get-tuple-element.62), channel_id=1, source_target_pairs={{0,32},{1,33},{2,34},{3,35},{4,36},{5,37},{6,38},{7,39},{8,40},{9,... | collective-permute-start | bytes 393224 | tf_op jit(solution)/shard_map/ppermute | solution.py:41
  70.8 16.8 %collective-permute-start.17 = (bf16[16,8192]{1,0:T(8,128)(2,1)S(1)}, bf16[16,8192]{1,0:T(8,128)(2,1)S(1)}, u32[]{:S(2)}, u32[]{:S(2)}) collective-permute-start(bf16[16,8192]{1,0:T(8,128)(2,1)S(1)} %get-tuple-element.56), channel_id=1, source_target_pairs={{0,4},{1,5},{2,6},{3,7},{4,8},{5,9},{6,10},{7,11},{8,12},{9,13},{1... | collective-permute-start | bytes 786440 | tf_op jit(solution)/shard_map/ppermute | solution.py:36
  71.5 16.1 %collective-permute-start.18 = (bf16[16,8192]{1,0:T(8,128)(2,1)S(1)}, bf16[16,8192]{1,0:T(8,128)(2,1)S(1)}, u32[]{:S(2)}, u32[]{:S(2)}) collective-permute-start(bf16[16,8192]{1,0:T(8,128)(2,1)S(1)} %get-tuple-element.57), channel_id=1, source_target_pairs={{0,8},{1,9},{2,10},{3,11},{4,12},{5,13},{6,14},{7,15},{8,0},{9,1},... | collective-permute-start | bytes 786440 | tf_op jit(solution)/shard_map/ppermute | solution.py:36
  75.1 12.6 %collective-permute-start.19 = (bf16[16,8192]{1,0:T(8,128)(2,1)S(1)}, bf16[16,8192]{1,0:T(8,128)(2,1)S(1)}, u32[]{:S(2)}, u32[]{:S(2)}) collective-permute-start(bf16[16,8192]{1,0:T(8,128)(2,1)S(1)} %get-tuple-element.58), channel_id=1, source_target_pairs={{0,12},{1,13},{2,14},{3,15},{4,0},{5,1},{6,2},{7,3},{8,4},{9,5},{1... | collective-permute-start | bytes 786440 | tf_op jit(solution)/shard_map/ppermute | solution.py:36

commit v6 on v5

--- a/solution.py
+++ b/solution.py
@@ -153,7 +153,7 @@
         scratch_shapes=[
             pltpu.VMEM(keys.shape, BF16),
             pltpu.VMEM(values.shape, BF16),
-            pltpu.VMEM((rows * heads, width), F32),
+            pltpu.VMEM(((rows + 1) * heads, width), F32),
             pltpu.SemaphoreType.DMA((rows // AT_ONCE,)),
             pltpu.SemaphoreType.DMA((rows // AT_ONCE,)),
         ],

time: 89 us -> 89 us (level)
  no operation moved by 1% of the time
where the time goes in v6:
time: 89 us; the launch traced here: 88.6 us
  starting transfers between devices  32.4 us (36%)
  waiting for transfers between devices  21.5 us (24%)
  Pallas kernels  19.6 us (22%)
  blocking collectives  11.3 us (13%)
  local copies, waits for them, and re-layouts  3.39 us (4%)
    ppermute x13, starting transfers between devices, pass_plane(): return lax.ppermute(value, BOTH, pairs)  14.9 us
    ppermute x13, waiting for transfers between devices, pass_plane(): return lax.ppermute(value, BOTH, pairs)  12.4 us
    all_to_all x1, blocking collectives, body(): delta = lax.all_to_all(delta, 'tp', split_axis=0, concat_axis=0, tiled=True)  11.3 us
    ppermute x6, starting transfers between devices, pass_z(): return lax.ppermute(value, BOTH, pairs)  9.73 us
    pallas_call x1, Pallas kernels, attend(): pl.pallas_call(attend_kernel, name='attend', out_shape=jax.ShapeDtypeStru...  9.3 us
    all_to_all x1, waiting for transfers between devices, body(): lax.all_to_all(attended, 'tp', split_axis=0, concat_axis=0, tiled=True)  7.42 us
    all_to_all x1, starting transfers between devices, body(): lax.all_to_all(attended, 'tp', split_axis=0, concat_axis=0, tiled=True)  7.26 us
    pallas_call x1, Pallas kernels, project(): pl.pallas_call(project_kernel, name='project', out_shape=[full, full, ful...  6.72 us
  transfers between devices with their start and end apart: 22, of which 9 were waited for; matrix products, arithmetic and copies ran while one was open for 2% of the time, Pallas kernels for 21%

profile of v6, /device:TPU:0, one launch (start us, length us, event | category | flops | bytes accessed | tf_op | source)
XLA Modules:
  0.0 88.6 jit_solution(1852235657842847489)
XLA Ops:
  0.0 0.5 collective-permute-start.1
  0.5 9.3 %attend.1 = bf16[16,16,512]{2,1,0:T(8,128)(2,1)} custom-call(s32[16]{0:T(128)} %lengths_ref.1, bf16[16,64,128]{2,1,0:T(8,128)(2,1)} %q_ref.1, bf16[16,8,256,128]{3,2,1,0:T(8,128)(2,1)} %k_hbm.1, bf16[16,8,256,128]{3,2,1,0:T(8,128)(2,1)} %v_hbm.1, bf16[16,8,128]{2,1,0:T(8,128)(2,1)} %fk_ref.1, bf16[16,8,128]{2,1,0:T(8,128)(2,1)} %fv_ref.1), custom_call_target="tpu_custom_call" | custom-call | flops 134217728 | bytes 16777216 | tf_op jit(solution)/shard_map/attend/pallas_call | solution.py:147
  9.8 7.3 %all-to-all-start = ((bf16[16,16,512]{2,1,0:T(8,128)(2,1)}), bf16[16,16,512]{2,1,0:T(8,128)(2,1)S(1)}, u32[]{:S(2)}, u32[]{:S(2)}) async-start(bf16[16,16,512]{2,1,0:T(8,128)(2,1)} %attend.1), calls=%async_computation | async-start | bytes 524288 | tf_op jit(solution)/shard_map/all_to_all | solution.py:511
  17.3 1.3 %dynamic-slice_bitcast_fusion.order_ref = s32[16]{0:T(128)} fusion(s32[128,16]{1,0:T(8,128)} %constant.89.clone, s32[]{:T(128)S(6)} %select_n.71), kind=kLoop, calls=%fused_computation.27 | loop fusion | bytes 132 | tf_op jit(solution)/shard_map/squeeze | solution.py:506
  18.6 7.4 %all-to-all-done.f_ref = bf16[16,16,512]{2,1,0:T(8,128)(2,1)S(1)} async-done(((bf16[16,16,512]{2,1,0:T(8,128)(2,1)}), bf16[16,16,512]{2,1,0:T(8,128)(2,1)S(1)}, u32[]{:S(2)}, u32[]{:S(2)}) %all-to-all-start) | async-done | bytes 262176 | tf_op jit(solution)/shard_map/all_to_all | solution.py:511
  26.4 2.0 %collective-permute-start.2 = (bf16[128,512]{1,0:T(8,128)(2,1)S(1)}, bf16[128,512]{1,0:T(8,128)(2,1)S(1)}, u32[]{:S(2)}, u32[]{:S(2)}) collective-permute-start(bf16[128,512]{1,0:T(8,128)(2,1)S(1)} %get-tuple-element.37), channel_id=1, source_target_pairs={{0,32},{1,33},{2,34},{3,35},{4,36},{5,37},{6,38},{7,39},{8,40},{9,... | collective-permute-start | bytes 393224 | tf_op jit(solution)/shard_map/ppermute | solution.py:41
  28.4 3.6 %collective-permute-start.3 = (bf16[128,512]{1,0:T(8,128)(2,1)S(1)}, bf16[128,512]{1,0:T(8,128)(2,1)S(1)}, u32[]{:S(2)}, u32[]{:S(2)}) collective-permute-start(bf16[128,512]{1,0:T(8,128)(2,1)S(1)} %get-tuple-element.38), channel_id=1, source_target_pairs={{0,64},{1,65},{2,66},{3,67},{4,68},{5,69},{6,70},{7,71},{8,72},{9,... | collective-permute-start | bytes 393224 | tf_op jit(solution)/shard_map/ppermute | solution.py:41
  31.9 1.0 %collective-permute-start.4 = (bf16[128,512]{1,0:T(8,128)(2,1)S(1)}, bf16[128,512]{1,0:T(8,128)(2,1)S(1)}, u32[]{:S(2)}, u32[]{:S(2)}) collective-permute-start(bf16[128,512]{1,0:T(8,128)(2,1)S(1)} %get-tuple-element.39), channel_id=1, source_target_pairs={{0,96},{1,97},{2,98},{3,99},{4,100},{5,101},{6,102},{7,103},{8,104... | collective-permute-start | bytes 393224 | tf_op jit(solution)/shard_map/ppermute | solution.py:41
  33.0 6.7 %project.1 = (bf16[64,8192]{1,0:T(8,128)(2,1)}, bf16[64,8192]{1,0:T(8,128)(2,1)}, bf16[64,8192]{1,0:T(8,128)(2,1)}, bf16[64,4096]{1,0:T(8,128)(2,1)}, bf16[64,4096]{1,0:T(8,128)(2,1)}) custom-call(s32[16]{0:T(128)} %dynamic-slice_bitcast_fusion.order_ref, bf16[16,16,512]{2,1,0:T(8,128)(2,1)} %copy-done, bf16[512,8192]{1,0:T(8,128)(2,1)} %w_hbm.1), custom_call_target="tpu_custom_call" | custom-call | flops 2147483648 | bytes 12582912 | tf_op jit(solution)/shard_map/project/pallas_call | solution.py:223
  39.7 0.8 collective-permute-start.6
  40.5 1.3 %collective-permute-start.5 = (bf16[64,8192]{1,0:T(8,128)(2,1)}, bf16[64,8192]{1,0:T(8,128)(2,1)S(1)}, u32[]{:S(2)}, u32[]{:S(2)}) collective-permute-start(bf16[64,8192]{1,0:T(8,128)(2,1)} %get-tuple-element.40), channel_id=1, source_target_pairs={{0,1},{1,2},{2,3},{3,0},{4,5},{5,6},{6,7},{7,4},{8,9},{9,10},{10,1... | collective-permute-start | bytes 3145736 | tf_op jit(solution)/shard_map/ppermute | solution.py:36
  41.9 0.8 shrink.1
  42.6 0.9 %collective-permute-start.9 = (bf16[256,128]{1,0:T(8,128)(2,1)S(1)}, bf16[256,128]{1,0:T(8,128)(2,1)S(1)}, u32[]{:S(2)}, u32[]{:S(2)}) collective-permute-start(bf16[256,128]{1,0:T(8,128)(2,1)S(1)} %shrink.1), channel_id=1, source_target_pairs={{0,12},{1,13},{2,14},{3,15},{4,0},{5,1},{6,2},{7,3},{8,4},{9,5},{1... | collective-permute-start | bytes 196616 | tf_op jit(solution)/shard_map/ppermute | solution.py:36
  43.6 1.3 %collective-permute-start.8 = (bf16[256,128]{1,0:T(8,128)(2,1)S(1)}, bf16[256,128]{1,0:T(8,128)(2,1)S(1)}, u32[]{:S(2)}, u32[]{:S(2)}) collective-permute-start(bf16[256,128]{1,0:T(8,128)(2,1)S(1)} %shrink.1), channel_id=1, source_target_pairs={{0,8},{1,9},{2,10},{3,11},{4,12},{5,13},{6,14},{7,15},{8,0},{9,1},... | collective-permute-start | bytes 196616 | tf_op jit(solution)/shard_map/ppermute | solution.py:36
  45.0 2.8 %collective-permute-done.9 = bf16[256,128]{1,0:T(8,128)(2,1)S(1)} collective-permute-done((bf16[256,128]{1,0:T(8,128)(2,1)S(1)}, bf16[256,128]{1,0:T(8,128)(2,1)S(1)}, u32[]{:S(2)}, u32[]{:S(2)}) %collective-permute-start.9) | collective-permute-done | bytes 65568 | tf_op jit(solution)/shard_map/ppermute | solution.py:36
  47.7 2.4 %collective-permute-done.8 = bf16[256,128]{1,0:T(8,128)(2,1)S(1)} collective-permute-done((bf16[256,128]{1,0:T(8,128)(2,1)S(1)}, bf16[256,128]{1,0:T(8,128)(2,1)S(1)}, u32[]{:S(2)}, u32[]{:S(2)}) %collective-permute-start.8) | collective-permute-done | bytes 65568 | tf_op jit(solution)/shard_map/ppermute | solution.py:36
  50.1 1.2 %collective-permute-done.7 = bf16[256,128]{1,0:T(8,128)(2,1)S(1)} collective-permute-done((bf16[256,128]{1,0:T(8,128)(2,1)S(1)}, bf16[256,128]{1,0:T(8,128)(2,1)S(1)}, u32[]{:S(2)}, u32[]{:S(2)}) %collective-permute-start.7) | collective-permute-done | bytes 65568 | tf_op jit(solution)/shard_map/ppermute | solution.py:36
  51.4 2.4 %collective-permute-start.12 = (bf16[256,128]{1,0:T(8,128)(2,1)S(1)}, bf16[256,128]{1,0:T(8,128)(2,1)S(1)}, u32[]{:S(2)}, u32[]{:S(2)}) collective-permute-start(bf16[256,128]{1,0:T(8,128)(2,1)S(1)} %add_convert_fusion.1), channel_id=1, source_target_pairs={{0,3},{1,0},{2,1},{3,2},{4,7},{5,4},{6,5},{7,6},{8,11},{9,8},{10,9... | collective-permute-start | bytes 196616 | tf_op jit(solution)/shard_map/ppermute | solution.py:36
  53.9 0.8 collective-permute-start.10
  54.7 0.8 collective-permute-done.6.refs_1_.came_back
  55.5 1.0 %copy-done.5 = bf16[64,4096]{1,0:T(8,128)(2,1)S(1)} copy-done((bf16[64,4096]{1,0:T(8,128)(2,1)S(1)}, bf16[64,4096]{1,0:T(8,128)(2,1)}, u32[]{:S(2)}) %copy-start.5) | copy-done | bytes 524312
  56.6 2.1 %collective-permute-start.16 = (bf16[64,4096]{1,0:T(8,128)(2,1)S(1)}, bf16[64,4096]{1,0:T(8,128)(2,1)S(1)}, u32[]{:S(2)}, u32[]{:S(2)}) collective-permute-start(bf16[64,4096]{1,0:T(8,128)(2,1)S(1)} %meet.3), channel_id=1, source_target_pairs={{0,3},{1,0},{2,1},{3,2},{4,7},{5,4},{6,5},{7,6},{8,11},{9,8},{10,9... | collective-permute-start | bytes 1572872 | tf_op jit(solution)/shard_map/ppermute | solution.py:36
  58.7 1.0 %copy-done.4 = bf16[64,4096]{1,0:T(8,128)(2,1)S(1)} copy-done((bf16[64,4096]{1,0:T(8,128)(2,1)S(1)}, bf16[64,4096]{1,0:T(8,128)(2,1)}, u32[]{:S(2)}) %copy-start.4) | copy-done | bytes 524312
  60.9 2.9 %collective-permute-start.15 = (bf16[128,512]{1,0:T(8,128)(2,1)S(1)}, bf16[128,512]{1,0:T(8,128)(2,1)S(1)}, u32[]{:S(2)}, u32[]{:S(2)}) collective-permute-start(bf16[128,512]{1,0:T(8,128)(2,1)S(1)} %get-tuple-element.52), channel_id=1, source_target_pairs={{0,64},{1,65},{2,66},{3,67},{4,68},{5,69},{6,70},{7,71},{8,72},{9,... | collective-permute-start | bytes 393224 | tf_op jit(solution)/shard_map/ppermute | solution.py:41
  63.8 2.1 %collective-permute-done.16.back_last = bf16[64,4096]{1,0:T(8,128)(2,1)S(1)} collective-permute-done((bf16[64,4096]{1,0:T(8,128)(2,1)S(1)}, bf16[64,4096]{1,0:T(8,128)(2,1)S(1)}, u32[]{:S(2)}, u32[]{:S(2)}) %collective-permute-start.16) | collective-permute-done | bytes 524320 | tf_op jit(solution)/shard_map/ppermute | solution.py:36
  65.9 1.6 %collective-permute-done.15.r2 = bf16[128,512]{1,0:T(8,128)(2,1)S(1)} collective-permute-done((bf16[128,512]{1,0:T(8,128)(2,1)S(1)}, bf16[128,512]{1,0:T(8,128)(2,1)S(1)}, u32[]{:S(2)}, u32[]{:S(2)}) %collective-permute-start.15) | collective-permute-done | bytes 131104 | tf_op jit(solution)/shard_map/ppermute | solution.py:41
  67.5 3.0 %collective-permute-done.13.ahead_last = bf16[64,4096]{1,0:T(8,128)(2,1)S(1)} collective-permute-done((bf16[64,4096]{1,0:T(8,128)(2,1)S(1)}, bf16[64,4096]{1,0:T(8,128)(2,1)S(1)}, u32[]{:S(2)}, u32[]{:S(2)}) %collective-permute-start.13) | collective-permute-done | bytes 524320 | tf_op jit(solution)/shard_map/ppermute | solution.py:36
  70.8 0.6 collective-permute-start.17
  71.5 3.6 %collective-permute-start.18 = (bf16[16,8192]{1,0:T(8,128)(2,1)S(1)}, bf16[16,8192]{1,0:T(8,128)(2,1)S(1)}, u32[]{:S(2)}, u32[]{:S(2)}) collective-permute-start(bf16[16,8192]{1,0:T(8,128)(2,1)S(1)} %get-tuple-element.57), channel_id=1, source_target_pairs={{0,8},{1,9},{2,10},{3,11},{4,12},{5,13},{6,14},{7,15},{8,0},{9,1},... | collective-permute-start | bytes 786440 | tf_op jit(solution)/shard_map/ppermute | solution.py:36
  75.1 0.8 collective-permute-start.19
  76.3 11.3 %all_to_all.10.delta_ref = bf16[16,16,512]{2,1,0:T(8,128)(2,1)S(1)} all-to-all(bf16[16,16,512]{2,1,0:T(8,128)(2,1)S(1)} %collect.1), channel_id=1, replica_groups=mesh['rep'=8,'tp'=16] {'tp'}, dimensions={0} | all-to-all | bytes 524288 | tf_op jit(solution)/shard_map/all_to_all | solution.py:537
  87.6 0.9 %finish.1 = bf16[16,8192]{1,0:T(8,128)(2,1)} custom-call(bf16[16,8192]{1,0:T(8,128)(2,1)S(1)} %copy-done.6, bf16[16,8192]{1,0:T(8,128)(2,1)S(1)} %get-tuple-element.55.s_ref, bf16[16,8192]{1,0:T(8,128)(2,1)S(1)} %collective-permute-done.17.a_ref, bf16[16,8192]{1,0:T(8,128)(2,1)S(1)} %collective-permute-done.18.b_ref, ...), custom_call_target="tpu_custom_call" | custom-call | flops 1048576 | bytes 2097152 | tf_op jit(solution)/shard_map/finish/pallas_call | solution.py:446
  (44 shorter events, 3.0 us)
Async XLA Ops:
  0.0 26.0 %collective-permute-start = (bf16[1024,512]{1,0:T(8,128)(2,1)}, bf16[1024,512]{1,0:T(8,128)(2,1)S(1)}, u32[]{:S(2)}, u32[]{:S(2)}) collective-permute-start(bf16[1024,512]{1,0:T(8,128)(2,1)} %bitcast.27), channel_id=1, source_target_pairs={{0,16},{1,17},{2,18},{3,19},{4,20},{5,21},{6,22},{7,23},{8,24},{9,... | collective-permute-start | bytes 3145736 | tf_op jit(solution)/shard_map/ppermute | solution.py:45
  0.0 17.1 %copy-start.7 = (s32[256,1]{0,1:T(1,128)S(1)}, s32[256,1]{0,1:T(1,128)}, u32[]{:S(2)}) copy-start(s32[256,1]{0,1:T(1,128)} %param.18) | copy-start | bytes 3076
  0.0 26.0 %collective-permute-start.1 = (bf16[1024,512]{1,0:T(8,128)(2,1)}, bf16[1024,512]{1,0:T(8,128)(2,1)S(1)}, u32[]{:S(2)}, u32[]{:S(2)}) collective-permute-start(bf16[1024,512]{1,0:T(8,128)(2,1)} %bitcast.25), channel_id=1, source_target_pairs={{0,16},{1,17},{2,18},{3,19},{4,20},{5,21},{6,22},{7,23},{8,24},{9,... | collective-permute-start | bytes 3145736 | tf_op jit(solution)/shard_map/ppermute | solution.py:45
  9.8 32.1 %copy-start.2 = (bf16[16,512,64]{1,2,0:T(8,128)(2,1)S(1)}, bf16[16,512,64]{1,2,0:T(8,128)(2,1)}, u32[]{:S(2)}) copy-start(bf16[16,512,64]{1,2,0:T(8,128)(2,1)} %param.21) | copy-start | bytes 3145732
  9.8 16.2 %all-to-all-start = ((bf16[16,16,512]{2,1,0:T(8,128)(2,1)}), bf16[16,16,512]{2,1,0:T(8,128)(2,1)S(1)}, u32[]{:S(2)}, u32[]{:S(2)}) async-start(bf16[16,16,512]{2,1,0:T(8,128)(2,1)} %attend.1), calls=%async_computation | async-start | bytes 524288 | tf_op jit(solution)/shard_map/all_to_all | solution.py:511
  26.0 6.9 %copy-start = (bf16[16,16,512]{2,1,0:T(8,128)(2,1)}, bf16[16,16,512]{2,1,0:T(8,128)(2,1)S(1)}, u32[]{:S(2)}) copy-start(bf16[16,16,512]{2,1,0:T(8,128)(2,1)S(1)} %all-to-all-done.f_ref) | copy-start | bytes 786436
  26.4 33.8 %copy-start.1 = (bf16[16,64,512]{2,1,0:T(8,128)(2,1)S(1)}, bf16[16,64,512]{2,1,0:T(8,128)(2,1)}, u32[]{:S(2)}) copy-start(bf16[16,64,512]{2,1,0:T(8,128)(2,1)} %param.22) | copy-start | bytes 3145732
  26.4 14.2 %collective-permute-start.2 = (bf16[128,512]{1,0:T(8,128)(2,1)S(1)}, bf16[128,512]{1,0:T(8,128)(2,1)S(1)}, u32[]{:S(2)}, u32[]{:S(2)}) collective-permute-start(bf16[128,512]{1,0:T(8,128)(2,1)S(1)} %get-tuple-element.37), channel_id=1, source_target_pairs={{0,32},{1,33},{2,34},{3,35},{4,36},{5,37},{6,38},{7,39},{8,40},{9,... | collective-permute-start | bytes 393224 | tf_op jit(solution)/shard_map/ppermute | solution.py:41
  28.4 12.2 %collective-permute-start.3 = (bf16[128,512]{1,0:T(8,128)(2,1)S(1)}, bf16[128,512]{1,0:T(8,128)(2,1)S(1)}, u32[]{:S(2)}, u32[]{:S(2)}) collective-permute-start(bf16[128,512]{1,0:T(8,128)(2,1)S(1)} %get-tuple-element.38), channel_id=1, source_target_pairs={{0,64},{1,65},{2,66},{3,67},{4,68},{5,69},{6,70},{7,71},{8,72},{9,... | collective-permute-start | bytes 393224 | tf_op jit(solution)/shard_map/ppermute | solution.py:41
  31.9 8.6 %collective-permute-start.4 = (bf16[128,512]{1,0:T(8,128)(2,1)S(1)}, bf16[128,512]{1,0:T(8,128)(2,1)S(1)}, u32[]{:S(2)}, u32[]{:S(2)}) collective-permute-start(bf16[128,512]{1,0:T(8,128)(2,1)S(1)} %get-tuple-element.39), channel_id=1, source_target_pairs={{0,96},{1,97},{2,98},{3,99},{4,100},{5,101},{6,102},{7,103},{8,104... | collective-permute-start | bytes 393224 | tf_op jit(solution)/shard_map/ppermute | solution.py:41
  39.7 30.8 %copy-start.3 = (bf16[64,8192]{1,0:T(8,128)(2,1)S(1)}, bf16[64,8192]{1,0:T(8,128)(2,1)}, u32[]{:S(2)}) copy-start(bf16[64,8192]{1,0:T(8,128)(2,1)} %get-tuple-element.34.own) | copy-start | bytes 3145732
  39.7 47.9 %copy-start.6 = (bf16[16,8192]{1,0:T(8,128)(2,1)S(1)}, bf16[16,8192]{1,0:T(8,128)(2,1)}, u32[]{:S(2)}) copy-start(bf16[16,8192]{1,0:T(8,128)(2,1)} %skip_ref.1) | copy-start | bytes 786436
  39.7 15.8 %collective-permute-start.6 = (bf16[64,8192]{1,0:T(8,128)(2,1)}, bf16[64,8192]{1,0:T(8,128)(2,1)S(1)}, u32[]{:S(2)}, u32[]{:S(2)}) collective-permute-start(bf16[64,8192]{1,0:T(8,128)(2,1)} %get-tuple-element.41), channel_id=1, source_target_pairs={{0,3},{1,0},{2,1},{3,2},{4,7},{5,4},{6,5},{7,6},{8,11},{9,8},{10,9... | collective-permute-start | bytes 3145736 | tf_op jit(solution)/shard_map/ppermute | solution.py:36
  40.5 18.1 %collective-permute-start.5 = (bf16[64,8192]{1,0:T(8,128)(2,1)}, bf16[64,8192]{1,0:T(8,128)(2,1)S(1)}, u32[]{:S(2)}, u32[]{:S(2)}) collective-permute-start(bf16[64,8192]{1,0:T(8,128)(2,1)} %get-tuple-element.40), channel_id=1, source_target_pairs={{0,1},{1,2},{2,3},{3,0},{4,5},{5,6},{6,7},{7,4},{8,9},{9,10},{10,1... | collective-permute-start | bytes 3145736 | tf_op jit(solution)/shard_map/ppermute | solution.py:36
  42.6 5.1 %collective-permute-start.9 = (bf16[256,128]{1,0:T(8,128)(2,1)S(1)}, bf16[256,128]{1,0:T(8,128)(2,1)S(1)}, u32[]{:S(2)}, u32[]{:S(2)}) collective-permute-start(bf16[256,128]{1,0:T(8,128)(2,1)S(1)} %shrink.1), channel_id=1, source_target_pairs={{0,12},{1,13},{2,14},{3,15},{4,0},{5,1},{6,2},{7,3},{8,4},{9,5},{1... | collective-permute-start | bytes 196616 | tf_op jit(solution)/shard_map/ppermute | solution.py:36
  43.6 6.5 %collective-permute-start.8 = (bf16[256,128]{1,0:T(8,128)(2,1)S(1)}, bf16[256,128]{1,0:T(8,128)(2,1)S(1)}, u32[]{:S(2)}, u32[]{:S(2)}) collective-permute-start(bf16[256,128]{1,0:T(8,128)(2,1)S(1)} %shrink.1), channel_id=1, source_target_pairs={{0,8},{1,9},{2,10},{3,11},{4,12},{5,13},{6,14},{7,15},{8,0},{9,1},... | collective-permute-start | bytes 196616 | tf_op jit(solution)/shard_map/ppermute | solution.py:36
  44.8 6.5 %collective-permute-start.7 = (bf16[256,128]{1,0:T(8,128)(2,1)S(1)}, bf16[256,128]{1,0:T(8,128)(2,1)S(1)}, u32[]{:S(2)}, u32[]{:S(2)}) collective-permute-start(bf16[256,128]{1,0:T(8,128)(2,1)S(1)} %shrink.1), channel_id=1, source_target_pairs={{0,4},{1,5},{2,6},{3,7},{4,8},{5,9},{6,10},{7,11},{8,12},{9,13},{1... | collective-permute-start | bytes 196616 | tf_op jit(solution)/shard_map/ppermute | solution.py:36
  51.4 8.5 %collective-permute-start.12 = (bf16[256,128]{1,0:T(8,128)(2,1)S(1)}, bf16[256,128]{1,0:T(8,128)(2,1)S(1)}, u32[]{:S(2)}, u32[]{:S(2)}) collective-permute-start(bf16[256,128]{1,0:T(8,128)(2,1)S(1)} %add_convert_fusion.1), channel_id=1, source_target_pairs={{0,3},{1,0},{2,1},{3,2},{4,7},{5,4},{6,5},{7,6},{8,11},{9,8},{10,9... | collective-permute-start | bytes 196616 | tf_op jit(solution)/shard_map/ppermute | solution.py:36
  53.7 6.1 %collective-permute-start.11 = (bf16[256,128]{1,0:T(8,128)(2,1)S(1)}, bf16[256,128]{1,0:T(8,128)(2,1)S(1)}, u32[]{:S(2)}, u32[]{:S(2)}) collective-permute-start(bf16[256,128]{1,0:T(8,128)(2,1)S(1)} %add_convert_fusion.1), channel_id=1, source_target_pairs={{0,2},{1,3},{2,0},{3,1},{4,6},{5,7},{6,4},{7,5},{8,10},{9,11},{10,... | collective-permute-start | bytes 196616 | tf_op jit(solution)/shard_map/ppermute | solution.py:36
  53.9 6.2 %collective-permute-start.10 = (bf16[256,128]{1,0:T(8,128)(2,1)S(1)}, bf16[256,128]{1,0:T(8,128)(2,1)S(1)}, u32[]{:S(2)}, u32[]{:S(2)}) collective-permute-start(bf16[256,128]{1,0:T(8,128)(2,1)S(1)} %add_convert_fusion.1), channel_id=1, source_target_pairs={{0,1},{1,2},{2,3},{3,0},{4,5},{5,6},{6,7},{7,4},{8,9},{9,10},{10,1... | collective-permute-start | bytes 196616 | tf_op jit(solution)/shard_map/ppermute | solution.py:36
  55.5 1.0 %copy-start.5 = (bf16[64,4096]{1,0:T(8,128)(2,1)S(1)}, bf16[64,4096]{1,0:T(8,128)(2,1)}, u32[]{:S(2)}) copy-start(bf16[64,4096]{1,0:T(8,128)(2,1)} %get-tuple-element.53.refs_0_) | copy-start | bytes 1572868
  56.6 9.2 %collective-permute-start.16 = (bf16[64,4096]{1,0:T(8,128)(2,1)S(1)}, bf16[64,4096]{1,0:T(8,128)(2,1)S(1)}, u32[]{:S(2)}, u32[]{:S(2)}) collective-permute-start(bf16[64,4096]{1,0:T(8,128)(2,1)S(1)} %meet.3), channel_id=1, source_target_pairs={{0,3},{1,0},{2,1},{3,2},{4,7},{5,4},{6,5},{7,6},{8,11},{9,8},{10,9... | collective-permute-start | bytes 1572872 | tf_op jit(solution)/shard_map/ppermute | solution.py:36
  58.7 1.0 %copy-start.4 = (bf16[64,4096]{1,0:T(8,128)(2,1)S(1)}, bf16[64,4096]{1,0:T(8,128)(2,1)}, u32[]{:S(2)}) copy-start(bf16[64,4096]{1,0:T(8,128)(2,1)} %get-tuple-element.46.refs_0_) | copy-start | bytes 1572868
  60.1 10.4 %collective-permute-start.13 = (bf16[64,4096]{1,0:T(8,128)(2,1)S(1)}, bf16[64,4096]{1,0:T(8,128)(2,1)S(1)}, u32[]{:S(2)}, u32[]{:S(2)}) collective-permute-start(bf16[64,4096]{1,0:T(8,128)(2,1)S(1)} %meet.2), channel_id=1, source_target_pairs={{0,1},{1,2},{2,3},{3,0},{4,5},{5,6},{6,7},{7,4},{8,9},{9,10},{10,1... | collective-permute-start | bytes 1572872 | tf_op jit(solution)/shard_map/ppermute | solution.py:36
  60.6 5.3 %collective-permute-start.14 = (bf16[128,512]{1,0:T(8,128)(2,1)S(1)}, bf16[128,512]{1,0:T(8,128)(2,1)S(1)}, u32[]{:S(2)}, u32[]{:S(2)}) collective-permute-start(bf16[128,512]{1,0:T(8,128)(2,1)S(1)} %get-tuple-element.51), channel_id=1, source_target_pairs={{0,96},{1,97},{2,98},{3,99},{4,100},{5,101},{6,102},{7,103},{8,104... | collective-permute-start | bytes 393224 | tf_op jit(solution)/shard_map/ppermute | solution.py:41
  60.9 6.6 %collective-permute-start.15 = (bf16[128,512]{1,0:T(8,128)(2,1)S(1)}, bf16[128,512]{1,0:T(8,128)(2,1)S(1)}, u32[]{:S(2)}, u32[]{:S(2)}) collective-permute-start(bf16[128,512]{1,0:T(8,128)(2,1)S(1)} %get-tuple-element.52), channel_id=1, source_target_pairs={{0,64},{1,65},{2,66},{3,67},{4,68},{5,69},{6,70},{7,71},{8,72},{9,... | collective-permute-start | bytes 393224 | tf_op jit(solution)/shard_map/ppermute | solution.py:41
  63.8 12.1 %collective-permute-start.20 = (bf16[128,512]{1,0:T(8,128)(2,1)S(1)}, bf16[128,512]{1,0:T(8,128)(2,1)S(1)}, u32[]{:S(2)}, u32[]{:S(2)}) collective-permute-start(bf16[128,512]{1,0:T(8,128)(2,1)S(1)} %get-tuple-element.62), channel_id=1, source_target_pairs={{0,32},{1,33},{2,34},{3,35},{4,36},{5,37},{6,38},{7,39},{8,40},{9,... | collective-permute-start | bytes 393224 | tf_op jit(solution)/shard_map/ppermute | solution.py:41
  70.8 16.8 %collective-permute-start.17 = (bf16[16,8192]{1,0:T(8,128)(2,1)S(1)}, bf16[16,8192]{1,0:T(8,128)(2,1)S(1)}, u32[]{:S(2)}, u32[]{:S(2)}) collective-permute-start(bf16[16,8192]{1,0:T(8,128)(2,1)S(1)} %get-tuple-element.56), channel_id=1, source_target_pairs={{0,4},{1,5},{2,6},{3,7},{4,8},{5,9},{6,10},{7,11},{8,12},{9,13},{1... | collective-permute-start | bytes 786440 | tf_op jit(solution)/shard_map/ppermute | solution.py:36
  71.5 16.1 %collective-permute-start.18 = (bf16[16,8192]{1,0:T(8,128)(2,1)S(1)}, bf16[16,8192]{1,0:T(8,128)(2,1)S(1)}, u32[]{:S(2)}, u32[]{:S(2)}) collective-permute-start(bf16[16,8192]{1,0:T(8,128)(2,1)S(1)} %get-tuple-element.57), channel_id=1, source_target_pairs={{0,8},{1,9},{2,10},{3,11},{4,12},{5,13},{6,14},{7,15},{8,0},{9,1},... | collective-permute-start | bytes 786440 | tf_op jit(solution)/shard_map/ppermute | solution.py:36
  75.1 12.6 %collective-permute-start.19 = (bf16[16,8192]{1,0:T(8,128)(2,1)S(1)}, bf16[16,8192]{1,0:T(8,128)(2,1)S(1)}, u32[]{:S(2)}, u32[]{:S(2)}) collective-permute-start(bf16[16,8192]{1,0:T(8,128)(2,1)S(1)} %get-tuple-element.58), channel_id=1, source_target_pairs={{0,12},{1,13},{2,14},{3,15},{4,0},{5,1},{6,2},{7,3},{8,4},{9,5},{1... | collective-permute-start | bytes 786440 | tf_op jit(solution)/shard_map/ppermute | solution.py:36

commit v7 on v6

--- a/solution.py
+++ b/solution.py
@@ -59,7 +59,7 @@
     return table
 
 
-AT_ONCE = 4
+AT_ONCE = 8
 
 
 def attend_kernel(
@@ -76,17 +76,12 @@
         at = pl.ds(step * AT_ONCE, AT_ONCE)
         return pltpu.make_async_copy(far.at[at], near.at[at], sem.at[step])
 
-    for step in range(steps - 1):
+    for step in range(steps):
         copy(step, k_hbm, k_ref, k_sem).start()
         copy(step, v_hbm, v_ref, v_sem).start()
 
     def one_step(step, carry):
         copy(step, k_hbm, k_ref, k_sem).wait()
-
-        @pl.when(step == 0)
-        def _():
-            copy(steps - 1, k_hbm, k_ref, k_sem).start()
-            copy(steps - 1, v_hbm, v_ref, v_sem).start()
 
         all_scores = []
         for item in range(AT_ONCE):

time: 89 us -> 88.8 us (level)
  no operation moved by 1% of the time
where the time goes in v7:
time: 88.8 us; the launch traced here: 88.4 us
  starting transfers between devices  32.4 us (36%)
  waiting for transfers between devices  21.5 us (24%)
  Pallas kernels  19.4 us (22%)
  blocking collectives  11.3 us (13%)
  local copies, waits for them, and re-layouts  3.39 us (4%)
    ppermute x13, starting transfers between devices, pass_plane(): return lax.ppermute(value, BOTH, pairs)  14.9 us
    ppermute x13, waiting for transfers between devices, pass_plane(): return lax.ppermute(value, BOTH, pairs)  12.4 us
    all_to_all x1, blocking collectives, body(): delta = lax.all_to_all(delta, 'tp', split_axis=0, concat_axis=0, tiled=True)  11.3 us
    ppermute x6, starting transfers between devices, pass_z(): return lax.ppermute(value, BOTH, pairs)  9.73 us
    pallas_call x1, Pallas kernels, attend(): pl.pallas_call(attend_kernel, name='attend', out_shape=jax.ShapeDtypeStru...  9.14 us
    all_to_all x1, waiting for transfers between devices, body(): lax.all_to_all(attended, 'tp', split_axis=0, concat_axis=0, tiled=True)  7.42 us
    all_to_all x1, starting transfers between devices, body(): lax.all_to_all(attended, 'tp', split_axis=0, concat_axis=0, tiled=True)  7.26 us
    pallas_call x1, Pallas kernels, project(): pl.pallas_call(project_kernel, name='project', out_shape=[full, full, ful...  6.72 us
  transfers between devices with their start and end apart: 22, of which 9 were waited for; matrix products, arithmetic and copies ran while one was open for 2% of the time, Pallas kernels for 21%

profile of v7, /device:TPU:0, one launch (start us, length us, event | category | flops | bytes accessed | tf_op | source)
XLA Modules:
  0.0 88.4 jit_solution(254121133409185620)
XLA Ops:
  0.0 0.5 collective-permute-start.1
  0.5 9.1 %attend.1 = bf16[16,16,512]{2,1,0:T(8,128)(2,1)} custom-call(s32[16]{0:T(128)} %lengths_ref.1, bf16[16,64,128]{2,1,0:T(8,128)(2,1)} %q_ref.1, bf16[16,8,256,128]{3,2,1,0:T(8,128)(2,1)} %k_hbm.1, bf16[16,8,256,128]{3,2,1,0:T(8,128)(2,1)} %v_hbm.1, bf16[16,8,128]{2,1,0:T(8,128)(2,1)} %fk_ref.1, bf16[16,8,128]{2,1,0:T(8,128)(2,1)} %fv_ref.1), custom_call_target="tpu_custom_call" | custom-call | flops 134217728 | bytes 16777216 | tf_op jit(solution)/shard_map/attend/pallas_call | solution.py:142
  9.7 7.3 %all-to-all-start = ((bf16[16,16,512]{2,1,0:T(8,128)(2,1)}), bf16[16,16,512]{2,1,0:T(8,128)(2,1)S(1)}, u32[]{:S(2)}, u32[]{:S(2)}) async-start(bf16[16,16,512]{2,1,0:T(8,128)(2,1)} %attend.1), calls=%async_computation | async-start | bytes 524288 | tf_op jit(solution)/shard_map/all_to_all | solution.py:506
  17.1 1.3 %dynamic-slice_bitcast_fusion.order_ref = s32[16]{0:T(128)} fusion(s32[128,16]{1,0:T(8,128)} %constant.89.clone, s32[]{:T(128)S(6)} %select_n.71), kind=kLoop, calls=%fused_computation.27 | loop fusion | bytes 132 | tf_op jit(solution)/shard_map/squeeze | solution.py:501
  18.4 7.4 %all-to-all-done.f_ref = bf16[16,16,512]{2,1,0:T(8,128)(2,1)S(1)} async-done(((bf16[16,16,512]{2,1,0:T(8,128)(2,1)}), bf16[16,16,512]{2,1,0:T(8,128)(2,1)S(1)}, u32[]{:S(2)}, u32[]{:S(2)}) %all-to-all-start) | async-done | bytes 262176 | tf_op jit(solution)/shard_map/all_to_all | solution.py:506
  26.2 2.0 %collective-permute-start.2 = (bf16[128,512]{1,0:T(8,128)(2,1)S(1)}, bf16[128,512]{1,0:T(8,128)(2,1)S(1)}, u32[]{:S(2)}, u32[]{:S(2)}) collective-permute-start(bf16[128,512]{1,0:T(8,128)(2,1)S(1)} %get-tuple-element.37), channel_id=1, source_target_pairs={{0,32},{1,33},{2,34},{3,35},{4,36},{5,37},{6,38},{7,39},{8,40},{9,... | collective-permute-start | bytes 393224 | tf_op jit(solution)/shard_map/ppermute | solution.py:41
  28.2 3.6 %collective-permute-start.3 = (bf16[128,512]{1,0:T(8,128)(2,1)S(1)}, bf16[128,512]{1,0:T(8,128)(2,1)S(1)}, u32[]{:S(2)}, u32[]{:S(2)}) collective-permute-start(bf16[128,512]{1,0:T(8,128)(2,1)S(1)} %get-tuple-element.38), channel_id=1, source_target_pairs={{0,64},{1,65},{2,66},{3,67},{4,68},{5,69},{6,70},{7,71},{8,72},{9,... | collective-permute-start | bytes 393224 | tf_op jit(solution)/shard_map/ppermute | solution.py:41
  31.8 1.0 %collective-permute-start.4 = (bf16[128,512]{1,0:T(8,128)(2,1)S(1)}, bf16[128,512]{1,0:T(8,128)(2,1)S(1)}, u32[]{:S(2)}, u32[]{:S(2)}) collective-permute-start(bf16[128,512]{1,0:T(8,128)(2,1)S(1)} %get-tuple-element.39), channel_id=1, source_target_pairs={{0,96},{1,97},{2,98},{3,99},{4,100},{5,101},{6,102},{7,103},{8,104... | collective-permute-start | bytes 393224 | tf_op jit(solution)/shard_map/ppermute | solution.py:41
  32.8 6.7 %project.1 = (bf16[64,8192]{1,0:T(8,128)(2,1)}, bf16[64,8192]{1,0:T(8,128)(2,1)}, bf16[64,8192]{1,0:T(8,128)(2,1)}, bf16[64,4096]{1,0:T(8,128)(2,1)}, bf16[64,4096]{1,0:T(8,128)(2,1)}) custom-call(s32[16]{0:T(128)} %dynamic-slice_bitcast_fusion.order_ref, bf16[16,16,512]{2,1,0:T(8,128)(2,1)} %copy-done, bf16[512,8192]{1,0:T(8,128)(2,1)} %w_hbm.1), custom_call_target="tpu_custom_call" | custom-call | flops 2147483648 | bytes 12582912 | tf_op jit(solution)/shard_map/project/pallas_call | solution.py:218
  39.5 0.8 collective-permute-start.6
  40.4 1.3 %collective-permute-start.5 = (bf16[64,8192]{1,0:T(8,128)(2,1)}, bf16[64,8192]{1,0:T(8,128)(2,1)S(1)}, u32[]{:S(2)}, u32[]{:S(2)}) collective-permute-start(bf16[64,8192]{1,0:T(8,128)(2,1)} %get-tuple-element.40), channel_id=1, source_target_pairs={{0,1},{1,2},{2,3},{3,0},{4,5},{5,6},{6,7},{7,4},{8,9},{9,10},{10,1... | collective-permute-start | bytes 3145736 | tf_op jit(solution)/shard_map/ppermute | solution.py:36
  41.7 0.8 shrink.1
  42.5 0.9 %collective-permute-start.9 = (bf16[256,128]{1,0:T(8,128)(2,1)S(1)}, bf16[256,128]{1,0:T(8,128)(2,1)S(1)}, u32[]{:S(2)}, u32[]{:S(2)}) collective-permute-start(bf16[256,128]{1,0:T(8,128)(2,1)S(1)} %shrink.1), channel_id=1, source_target_pairs={{0,12},{1,13},{2,14},{3,15},{4,0},{5,1},{6,2},{7,3},{8,4},{9,5},{1... | collective-permute-start | bytes 196616 | tf_op jit(solution)/shard_map/ppermute | solution.py:36
  43.4 1.3 %collective-permute-start.8 = (bf16[256,128]{1,0:T(8,128)(2,1)S(1)}, bf16[256,128]{1,0:T(8,128)(2,1)S(1)}, u32[]{:S(2)}, u32[]{:S(2)}) collective-permute-start(bf16[256,128]{1,0:T(8,128)(2,1)S(1)} %shrink.1), channel_id=1, source_target_pairs={{0,8},{1,9},{2,10},{3,11},{4,12},{5,13},{6,14},{7,15},{8,0},{9,1},... | collective-permute-start | bytes 196616 | tf_op jit(solution)/shard_map/ppermute | solution.py:36
  44.8 2.8 %collective-permute-done.9 = bf16[256,128]{1,0:T(8,128)(2,1)S(1)} collective-permute-done((bf16[256,128]{1,0:T(8,128)(2,1)S(1)}, bf16[256,128]{1,0:T(8,128)(2,1)S(1)}, u32[]{:S(2)}, u32[]{:S(2)}) %collective-permute-start.9) | collective-permute-done | bytes 65568 | tf_op jit(solution)/shard_map/ppermute | solution.py:36
  47.6 2.4 %collective-permute-done.8 = bf16[256,128]{1,0:T(8,128)(2,1)S(1)} collective-permute-done((bf16[256,128]{1,0:T(8,128)(2,1)S(1)}, bf16[256,128]{1,0:T(8,128)(2,1)S(1)}, u32[]{:S(2)}, u32[]{:S(2)}) %collective-permute-start.8) | collective-permute-done | bytes 65568 | tf_op jit(solution)/shard_map/ppermute | solution.py:36
  49.9 1.2 %collective-permute-done.7 = bf16[256,128]{1,0:T(8,128)(2,1)S(1)} collective-permute-done((bf16[256,128]{1,0:T(8,128)(2,1)S(1)}, bf16[256,128]{1,0:T(8,128)(2,1)S(1)}, u32[]{:S(2)}, u32[]{:S(2)}) %collective-permute-start.7) | collective-permute-done | bytes 65568 | tf_op jit(solution)/shard_map/ppermute | solution.py:36
  51.2 2.4 %collective-permute-start.12 = (bf16[256,128]{1,0:T(8,128)(2,1)S(1)}, bf16[256,128]{1,0:T(8,128)(2,1)S(1)}, u32[]{:S(2)}, u32[]{:S(2)}) collective-permute-start(bf16[256,128]{1,0:T(8,128)(2,1)S(1)} %add_convert_fusion.1), channel_id=1, source_target_pairs={{0,3},{1,0},{2,1},{3,2},{4,7},{5,4},{6,5},{7,6},{8,11},{9,8},{10,9... | collective-permute-start | bytes 196616 | tf_op jit(solution)/shard_map/ppermute | solution.py:36
  53.7 0.8 collective-permute-start.10
  54.5 0.8 collective-permute-done.6.refs_1_.came_back
  55.3 1.0 %copy-done.5 = bf16[64,4096]{1,0:T(8,128)(2,1)S(1)} copy-done((bf16[64,4096]{1,0:T(8,128)(2,1)S(1)}, bf16[64,4096]{1,0:T(8,128)(2,1)}, u32[]{:S(2)}) %copy-start.5) | copy-done | bytes 524312
  56.5 2.1 %collective-permute-start.16 = (bf16[64,4096]{1,0:T(8,128)(2,1)S(1)}, bf16[64,4096]{1,0:T(8,128)(2,1)S(1)}, u32[]{:S(2)}, u32[]{:S(2)}) collective-permute-start(bf16[64,4096]{1,0:T(8,128)(2,1)S(1)} %meet.3), channel_id=1, source_target_pairs={{0,3},{1,0},{2,1},{3,2},{4,7},{5,4},{6,5},{7,6},{8,11},{9,8},{10,9... | collective-permute-start | bytes 1572872 | tf_op jit(solution)/shard_map/ppermute | solution.py:36
  58.5 1.0 %copy-done.4 = bf16[64,4096]{1,0:T(8,128)(2,1)S(1)} copy-done((bf16[64,4096]{1,0:T(8,128)(2,1)S(1)}, bf16[64,4096]{1,0:T(8,128)(2,1)}, u32[]{:S(2)}) %copy-start.4) | copy-done | bytes 524312
  60.7 2.9 %collective-permute-start.15 = (bf16[128,512]{1,0:T(8,128)(2,1)S(1)}, bf16[128,512]{1,0:T(8,128)(2,1)S(1)}, u32[]{:S(2)}, u32[]{:S(2)}) collective-permute-start(bf16[128,512]{1,0:T(8,128)(2,1)S(1)} %get-tuple-element.52), channel_id=1, source_target_pairs={{0,64},{1,65},{2,66},{3,67},{4,68},{5,69},{6,70},{7,71},{8,72},{9,... | collective-permute-start | bytes 393224 | tf_op jit(solution)/shard_map/ppermute | solution.py:41
  63.6 2.1 %collective-permute-done.16.back_last = bf16[64,4096]{1,0:T(8,128)(2,1)S(1)} collective-permute-done((bf16[64,4096]{1,0:T(8,128)(2,1)S(1)}, bf16[64,4096]{1,0:T(8,128)(2,1)S(1)}, u32[]{:S(2)}, u32[]{:S(2)}) %collective-permute-start.16) | collective-permute-done | bytes 524320 | tf_op jit(solution)/shard_map/ppermute | solution.py:36
  65.7 1.6 %collective-permute-done.15.r2 = bf16[128,512]{1,0:T(8,128)(2,1)S(1)} collective-permute-done((bf16[128,512]{1,0:T(8,128)(2,1)S(1)}, bf16[128,512]{1,0:T(8,128)(2,1)S(1)}, u32[]{:S(2)}, u32[]{:S(2)}) %collective-permute-start.15) | collective-permute-done | bytes 131104 | tf_op jit(solution)/shard_map/ppermute | solution.py:41
  67.3 3.0 %collective-permute-done.13.ahead_last = bf16[64,4096]{1,0:T(8,128)(2,1)S(1)} collective-permute-done((bf16[64,4096]{1,0:T(8,128)(2,1)S(1)}, bf16[64,4096]{1,0:T(8,128)(2,1)S(1)}, u32[]{:S(2)}, u32[]{:S(2)}) %collective-permute-start.13) | collective-permute-done | bytes 524320 | tf_op jit(solution)/shard_map/ppermute | solution.py:36
  70.7 0.6 collective-permute-start.17
  71.3 3.6 %collective-permute-start.18 = (bf16[16,8192]{1,0:T(8,128)(2,1)S(1)}, bf16[16,8192]{1,0:T(8,128)(2,1)S(1)}, u32[]{:S(2)}, u32[]{:S(2)}) collective-permute-start(bf16[16,8192]{1,0:T(8,128)(2,1)S(1)} %get-tuple-element.57), channel_id=1, source_target_pairs={{0,8},{1,9},{2,10},{3,11},{4,12},{5,13},{6,14},{7,15},{8,0},{9,1},... | collective-permute-start | bytes 786440 | tf_op jit(solution)/shard_map/ppermute | solution.py:36
  74.9 0.8 collective-permute-start.19
  76.2 11.3 %all_to_all.10.delta_ref = bf16[16,16,512]{2,1,0:T(8,128)(2,1)S(1)} all-to-all(bf16[16,16,512]{2,1,0:T(8,128)(2,1)S(1)} %collect.1), channel_id=1, replica_groups=mesh['rep'=8,'tp'=16] {'tp'}, dimensions={0} | all-to-all | bytes 524288 | tf_op jit(solution)/shard_map/all_to_all | solution.py:532
  87.5 0.9 %finish.1 = bf16[16,8192]{1,0:T(8,128)(2,1)} custom-call(bf16[16,8192]{1,0:T(8,128)(2,1)S(1)} %copy-done.6, bf16[16,8192]{1,0:T(8,128)(2,1)S(1)} %get-tuple-element.55.s_ref, bf16[16,8192]{1,0:T(8,128)(2,1)S(1)} %collective-permute-done.17.a_ref, bf16[16,8192]{1,0:T(8,128)(2,1)S(1)} %collective-permute-done.18.b_ref, ...), custom_call_target="tpu_custom_call" | custom-call | flops 1048576 | bytes 2097152 | tf_op jit(solution)/shard_map/finish/pallas_call | solution.py:441
  (44 shorter events, 3.0 us)
Async XLA Ops:
  0.0 25.9 %collective-permute-start = (bf16[1024,512]{1,0:T(8,128)(2,1)}, bf16[1024,512]{1,0:T(8,128)(2,1)S(1)}, u32[]{:S(2)}, u32[]{:S(2)}) collective-permute-start(bf16[1024,512]{1,0:T(8,128)(2,1)} %bitcast.27), channel_id=1, source_target_pairs={{0,16},{1,17},{2,18},{3,19},{4,20},{5,21},{6,22},{7,23},{8,24},{9,... | collective-permute-start | bytes 3145736 | tf_op jit(solution)/shard_map/ppermute | solution.py:45
  0.0 16.9 %copy-start.7 = (s32[256,1]{0,1:T(1,128)S(1)}, s32[256,1]{0,1:T(1,128)}, u32[]{:S(2)}) copy-start(s32[256,1]{0,1:T(1,128)} %param.18) | copy-start | bytes 3076
  0.0 25.9 %collective-permute-start.1 = (bf16[1024,512]{1,0:T(8,128)(2,1)}, bf16[1024,512]{1,0:T(8,128)(2,1)S(1)}, u32[]{:S(2)}, u32[]{:S(2)}) collective-permute-start(bf16[1024,512]{1,0:T(8,128)(2,1)} %bitcast.25), channel_id=1, source_target_pairs={{0,16},{1,17},{2,18},{3,19},{4,20},{5,21},{6,22},{7,23},{8,24},{9,... | collective-permute-start | bytes 3145736 | tf_op jit(solution)/shard_map/ppermute | solution.py:45
  9.7 32.1 %copy-start.2 = (bf16[16,512,64]{1,2,0:T(8,128)(2,1)S(1)}, bf16[16,512,64]{1,2,0:T(8,128)(2,1)}, u32[]{:S(2)}) copy-start(bf16[16,512,64]{1,2,0:T(8,128)(2,1)} %param.21) | copy-start | bytes 3145732
  9.7 16.2 %all-to-all-start = ((bf16[16,16,512]{2,1,0:T(8,128)(2,1)}), bf16[16,16,512]{2,1,0:T(8,128)(2,1)S(1)}, u32[]{:S(2)}, u32[]{:S(2)}) async-start(bf16[16,16,512]{2,1,0:T(8,128)(2,1)} %attend.1), calls=%async_computation | async-start | bytes 524288 | tf_op jit(solution)/shard_map/all_to_all | solution.py:506
  25.9 6.9 %copy-start = (bf16[16,16,512]{2,1,0:T(8,128)(2,1)}, bf16[16,16,512]{2,1,0:T(8,128)(2,1)S(1)}, u32[]{:S(2)}) copy-start(bf16[16,16,512]{2,1,0:T(8,128)(2,1)S(1)} %all-to-all-done.f_ref) | copy-start | bytes 786436
  26.2 33.8 %copy-start.1 = (bf16[16,64,512]{2,1,0:T(8,128)(2,1)S(1)}, bf16[16,64,512]{2,1,0:T(8,128)(2,1)}, u32[]{:S(2)}) copy-start(bf16[16,64,512]{2,1,0:T(8,128)(2,1)} %param.22) | copy-start | bytes 3145732
  26.2 14.2 %collective-permute-start.2 = (bf16[128,512]{1,0:T(8,128)(2,1)S(1)}, bf16[128,512]{1,0:T(8,128)(2,1)S(1)}, u32[]{:S(2)}, u32[]{:S(2)}) collective-permute-start(bf16[128,512]{1,0:T(8,128)(2,1)S(1)} %get-tuple-element.37), channel_id=1, source_target_pairs={{0,32},{1,33},{2,34},{3,35},{4,36},{5,37},{6,38},{7,39},{8,40},{9,... | collective-permute-start | bytes 393224 | tf_op jit(solution)/shard_map/ppermute | solution.py:41
  28.2 12.2 %collective-permute-start.3 = (bf16[128,512]{1,0:T(8,128)(2,1)S(1)}, bf16[128,512]{1,0:T(8,128)(2,1)S(1)}, u32[]{:S(2)}, u32[]{:S(2)}) collective-permute-start(bf16[128,512]{1,0:T(8,128)(2,1)S(1)} %get-tuple-element.38), channel_id=1, source_target_pairs={{0,64},{1,65},{2,66},{3,67},{4,68},{5,69},{6,70},{7,71},{8,72},{9,... | collective-permute-start | bytes 393224 | tf_op jit(solution)/shard_map/ppermute | solution.py:41
  31.8 8.6 %collective-permute-start.4 = (bf16[128,512]{1,0:T(8,128)(2,1)S(1)}, bf16[128,512]{1,0:T(8,128)(2,1)S(1)}, u32[]{:S(2)}, u32[]{:S(2)}) collective-permute-start(bf16[128,512]{1,0:T(8,128)(2,1)S(1)} %get-tuple-element.39), channel_id=1, source_target_pairs={{0,96},{1,97},{2,98},{3,99},{4,100},{5,101},{6,102},{7,103},{8,104... | collective-permute-start | bytes 393224 | tf_op jit(solution)/shard_map/ppermute | solution.py:41
  39.5 30.8 %copy-start.3 = (bf16[64,8192]{1,0:T(8,128)(2,1)S(1)}, bf16[64,8192]{1,0:T(8,128)(2,1)}, u32[]{:S(2)}) copy-start(bf16[64,8192]{1,0:T(8,128)(2,1)} %get-tuple-element.34.own) | copy-start | bytes 3145732
  39.5 47.9 %copy-start.6 = (bf16[16,8192]{1,0:T(8,128)(2,1)S(1)}, bf16[16,8192]{1,0:T(8,128)(2,1)}, u32[]{:S(2)}) copy-start(bf16[16,8192]{1,0:T(8,128)(2,1)} %skip_ref.1) | copy-start | bytes 786436
  39.5 15.8 %collective-permute-start.6 = (bf16[64,8192]{1,0:T(8,128)(2,1)}, bf16[64,8192]{1,0:T(8,128)(2,1)S(1)}, u32[]{:S(2)}, u32[]{:S(2)}) collective-permute-start(bf16[64,8192]{1,0:T(8,128)(2,1)} %get-tuple-element.41), channel_id=1, source_target_pairs={{0,3},{1,0},{2,1},{3,2},{4,7},{5,4},{6,5},{7,6},{8,11},{9,8},{10,9... | collective-permute-start | bytes 3145736 | tf_op jit(solution)/shard_map/ppermute | solution.py:36
  40.4 18.1 %collective-permute-start.5 = (bf16[64,8192]{1,0:T(8,128)(2,1)}, bf16[64,8192]{1,0:T(8,128)(2,1)S(1)}, u32[]{:S(2)}, u32[]{:S(2)}) collective-permute-start(bf16[64,8192]{1,0:T(8,128)(2,1)} %get-tuple-element.40), channel_id=1, source_target_pairs={{0,1},{1,2},{2,3},{3,0},{4,5},{5,6},{6,7},{7,4},{8,9},{9,10},{10,1... | collective-permute-start | bytes 3145736 | tf_op jit(solution)/shard_map/ppermute | solution.py:36
  42.5 5.1 %collective-permute-start.9 = (bf16[256,128]{1,0:T(8,128)(2,1)S(1)}, bf16[256,128]{1,0:T(8,128)(2,1)S(1)}, u32[]{:S(2)}, u32[]{:S(2)}) collective-permute-start(bf16[256,128]{1,0:T(8,128)(2,1)S(1)} %shrink.1), channel_id=1, source_target_pairs={{0,12},{1,13},{2,14},{3,15},{4,0},{5,1},{6,2},{7,3},{8,4},{9,5},{1... | collective-permute-start | bytes 196616 | tf_op jit(solution)/shard_map/ppermute | solution.py:36
  43.4 6.5 %collective-permute-start.8 = (bf16[256,128]{1,0:T(8,128)(2,1)S(1)}, bf16[256,128]{1,0:T(8,128)(2,1)S(1)}, u32[]{:S(2)}, u32[]{:S(2)}) collective-permute-start(bf16[256,128]{1,0:T(8,128)(2,1)S(1)} %shrink.1), channel_id=1, source_target_pairs={{0,8},{1,9},{2,10},{3,11},{4,12},{5,13},{6,14},{7,15},{8,0},{9,1},... | collective-permute-start | bytes 196616 | tf_op jit(solution)/shard_map/ppermute | solution.py:36
  44.7 6.5 %collective-permute-start.7 = (bf16[256,128]{1,0:T(8,128)(2,1)S(1)}, bf16[256,128]{1,0:T(8,128)(2,1)S(1)}, u32[]{:S(2)}, u32[]{:S(2)}) collective-permute-start(bf16[256,128]{1,0:T(8,128)(2,1)S(1)} %shrink.1), channel_id=1, source_target_pairs={{0,4},{1,5},{2,6},{3,7},{4,8},{5,9},{6,10},{7,11},{8,12},{9,13},{1... | collective-permute-start | bytes 196616 | tf_op jit(solution)/shard_map/ppermute | solution.py:36
  51.2 8.5 %collective-permute-start.12 = (bf16[256,128]{1,0:T(8,128)(2,1)S(1)}, bf16[256,128]{1,0:T(8,128)(2,1)S(1)}, u32[]{:S(2)}, u32[]{:S(2)}) collective-permute-start(bf16[256,128]{1,0:T(8,128)(2,1)S(1)} %add_convert_fusion.1), channel_id=1, source_target_pairs={{0,3},{1,0},{2,1},{3,2},{4,7},{5,4},{6,5},{7,6},{8,11},{9,8},{10,9... | collective-permute-start | bytes 196616 | tf_op jit(solution)/shard_map/ppermute | solution.py:36
  53.6 6.1 %collective-permute-start.11 = (bf16[256,128]{1,0:T(8,128)(2,1)S(1)}, bf16[256,128]{1,0:T(8,128)(2,1)S(1)}, u32[]{:S(2)}, u32[]{:S(2)}) collective-permute-start(bf16[256,128]{1,0:T(8,128)(2,1)S(1)} %add_convert_fusion.1), channel_id=1, source_target_pairs={{0,2},{1,3},{2,0},{3,1},{4,6},{5,7},{6,4},{7,5},{8,10},{9,11},{10,... | collective-permute-start | bytes 196616 | tf_op jit(solution)/shard_map/ppermute | solution.py:36
  53.7 6.2 %collective-permute-start.10 = (bf16[256,128]{1,0:T(8,128)(2,1)S(1)}, bf16[256,128]{1,0:T(8,128)(2,1)S(1)}, u32[]{:S(2)}, u32[]{:S(2)}) collective-permute-start(bf16[256,128]{1,0:T(8,128)(2,1)S(1)} %add_convert_fusion.1), channel_id=1, source_target_pairs={{0,1},{1,2},{2,3},{3,0},{4,5},{5,6},{6,7},{7,4},{8,9},{9,10},{10,1... | collective-permute-start | bytes 196616 | tf_op jit(solution)/shard_map/ppermute | solution.py:36
  55.3 1.0 %copy-start.5 = (bf16[64,4096]{1,0:T(8,128)(2,1)S(1)}, bf16[64,4096]{1,0:T(8,128)(2,1)}, u32[]{:S(2)}) copy-start(bf16[64,4096]{1,0:T(8,128)(2,1)} %get-tuple-element.53.refs_0_) | copy-start | bytes 1572868
  56.5 9.2 %collective-permute-start.16 = (bf16[64,4096]{1,0:T(8,128)(2,1)S(1)}, bf16[64,4096]{1,0:T(8,128)(2,1)S(1)}, u32[]{:S(2)}, u32[]{:S(2)}) collective-permute-start(bf16[64,4096]{1,0:T(8,128)(2,1)S(1)} %meet.3), channel_id=1, source_target_pairs={{0,3},{1,0},{2,1},{3,2},{4,7},{5,4},{6,5},{7,6},{8,11},{9,8},{10,9... | collective-permute-start | bytes 1572872 | tf_op jit(solution)/shard_map/ppermute | solution.py:36
  58.5 1.0 %copy-start.4 = (bf16[64,4096]{1,0:T(8,128)(2,1)S(1)}, bf16[64,4096]{1,0:T(8,128)(2,1)}, u32[]{:S(2)}) copy-start(bf16[64,4096]{1,0:T(8,128)(2,1)} %get-tuple-element.46.refs_0_) | copy-start | bytes 1572868
  59.9 10.4 %collective-permute-start.13 = (bf16[64,4096]{1,0:T(8,128)(2,1)S(1)}, bf16[64,4096]{1,0:T(8,128)(2,1)S(1)}, u32[]{:S(2)}, u32[]{:S(2)}) collective-permute-start(bf16[64,4096]{1,0:T(8,128)(2,1)S(1)} %meet.2), channel_id=1, source_target_pairs={{0,1},{1,2},{2,3},{3,0},{4,5},{5,6},{6,7},{7,4},{8,9},{9,10},{10,1... | collective-permute-start | bytes 1572872 | tf_op jit(solution)/shard_map/ppermute | solution.py:36
  60.4 5.3 %collective-permute-start.14 = (bf16[128,512]{1,0:T(8,128)(2,1)S(1)}, bf16[128,512]{1,0:T(8,128)(2,1)S(1)}, u32[]{:S(2)}, u32[]{:S(2)}) collective-permute-start(bf16[128,512]{1,0:T(8,128)(2,1)S(1)} %get-tuple-element.51), channel_id=1, source_target_pairs={{0,96},{1,97},{2,98},{3,99},{4,100},{5,101},{6,102},{7,103},{8,104... | collective-permute-start | bytes 393224 | tf_op jit(solution)/shard_map/ppermute | solution.py:41
  60.7 6.6 %collective-permute-start.15 = (bf16[128,512]{1,0:T(8,128)(2,1)S(1)}, bf16[128,512]{1,0:T(8,128)(2,1)S(1)}, u32[]{:S(2)}, u32[]{:S(2)}) collective-permute-start(bf16[128,512]{1,0:T(8,128)(2,1)S(1)} %get-tuple-element.52), channel_id=1, source_target_pairs={{0,64},{1,65},{2,66},{3,67},{4,68},{5,69},{6,70},{7,71},{8,72},{9,... | collective-permute-start | bytes 393224 | tf_op jit(solution)/shard_map/ppermute | solution.py:41
  63.6 12.1 %collective-permute-start.20 = (bf16[128,512]{1,0:T(8,128)(2,1)S(1)}, bf16[128,512]{1,0:T(8,128)(2,1)S(1)}, u32[]{:S(2)}, u32[]{:S(2)}) collective-permute-start(bf16[128,512]{1,0:T(8,128)(2,1)S(1)} %get-tuple-element.62), channel_id=1, source_target_pairs={{0,32},{1,33},{2,34},{3,35},{4,36},{5,37},{6,38},{7,39},{8,40},{9,... | collective-permute-start | bytes 393224 | tf_op jit(solution)/shard_map/ppermute | solution.py:41
  70.7 16.8 %collective-permute-start.17 = (bf16[16,8192]{1,0:T(8,128)(2,1)S(1)}, bf16[16,8192]{1,0:T(8,128)(2,1)S(1)}, u32[]{:S(2)}, u32[]{:S(2)}) collective-permute-start(bf16[16,8192]{1,0:T(8,128)(2,1)S(1)} %get-tuple-element.56), channel_id=1, source_target_pairs={{0,4},{1,5},{2,6},{3,7},{4,8},{5,9},{6,10},{7,11},{8,12},{9,13},{1... | collective-permute-start | bytes 786440 | tf_op jit(solution)/shard_map/ppermute | solution.py:36
  71.3 16.1 %collective-permute-start.18 = (bf16[16,8192]{1,0:T(8,128)(2,1)S(1)}, bf16[16,8192]{1,0:T(8,128)(2,1)S(1)}, u32[]{:S(2)}, u32[]{:S(2)}) collective-permute-start(bf16[16,8192]{1,0:T(8,128)(2,1)S(1)} %get-tuple-element.57), channel_id=1, source_target_pairs={{0,8},{1,9},{2,10},{3,11},{4,12},{5,13},{6,14},{7,15},{8,0},{9,1},... | collective-permute-start | bytes 786440 | tf_op jit(solution)/shard_map/ppermute | solution.py:36
  74.9 12.5 %collective-permute-start.19 = (bf16[16,8192]{1,0:T(8,128)(2,1)S(1)}, bf16[16,8192]{1,0:T(8,128)(2,1)S(1)}, u32[]{:S(2)}, u32[]{:S(2)}) collective-permute-start(bf16[16,8192]{1,0:T(8,128)(2,1)S(1)} %get-tuple-element.58), channel_id=1, source_target_pairs={{0,12},{1,13},{2,14},{3,15},{4,0},{5,1},{6,2},{7,3},{8,4},{9,5},{1... | collective-permute-start | bytes 786440 | tf_op jit(solution)/shard_map/ppermute | solution.py:36
